TPU v7x, 512 devices: a whole 4x8x8 slice. The times are simulated.
512 devices in a mesh: dp: 64 (over x, y, core), tensor: 8 (over z).
Axes of the slice: x: 4, y: 8, z: 8, core: 2. Of those that a mesh axis runs over, the one named last changes fastest.
Arguments:
- grad: bfloat16 [64, 1024, 6144], P('dp', 'tensor'), may hold values from -40 to 40
- error: bfloat16 [64, 1024, 6144], P('dp', 'tensor'), may hold values from -4 to 4
- q_in: bfloat16 [6144, 64], P('tensor'), may hold values from -6 to 6
Outputs:
- new_error: bfloat16 [64, 1024, 6144], P('dp', 'tensor')
- p_factor: float32 [1024, 64], P('tensor')
- q_next: bfloat16 [6144, 64], P('tensor')
All inputs are finite; a program needn't handle non-finite values.
Results may differ from a plain program's by a relative error of at most 0.0045.
The roundings to bfloat16 on the way count: a program that leaves them out, or rounds other values in their place, can miss the bound.
Values may be sent and summed in bfloat16 or wider, within the bound.
No kernel may reach another device: no remote copies, remote signals or barrier semaphores. Data moves between devices by JAX's collectives and lax.ppermute only.
A program may use at most 64 MiB of HBM per device.

v0:
```python
import jax
import jax.numpy as jnp
from jax import lax
from jax.sharding import PartitionSpec as P


def local(grad, error, q_in):
    summed = grad[0].astype(jnp.float32) + error[0].astype(jnp.float32)
    merged = summed.astype(jnp.bfloat16)
    tensor_index = lax.axis_index("tensor")
    replica_count = lax.axis_size("dp")
    left_local = jnp.dot(
        merged,
        lax.all_gather(q_in, "tensor", axis=0, tiled=True),
        preferred_element_type=jnp.float32,
    )
    left_sum = lax.psum(left_local, "dp")
    partial_gram = jnp.dot(left_sum.T, left_sum, precision=lax.Precision.HIGHEST)
    gram = lax.psum(partial_gram, "tensor")
    cholesky_lower = jnp.linalg.cholesky(gram)
    p_factor = lax.linalg.triangular_solve(
        cholesky_lower, left_sum, left_side=False, lower=True, transpose_a=True
    )
    p_round = p_factor.astype(jnp.bfloat16)
    shard_cols = q_in.shape[0]
    right_term = lax.dot_general(
        merged, p_round, (((0,), (0,)), ((), ())), preferred_element_type=jnp.float32
    )
    right_sum = lax.psum(right_term, ("dp", "tensor"))
    right_full = (right_sum / replica_count).astype(jnp.bfloat16)
    q_next = lax.dynamic_slice_in_dim(right_full, tensor_index * shard_cols, shard_cols, 0)
    decoded = lax.dot_general(
        p_round, right_full, (((1,), (1,)), ((), ())), preferred_element_type=jnp.float32
    )
    new_error = (summed - decoded).astype(jnp.bfloat16)[None]
    return (new_error, p_factor, q_next)


def solution(mesh):
    placed = (P("dp", "tensor", None), P("dp", "tensor", None), P("tensor", None))
    return jax.shard_map(
        local,
        mesh=mesh,
        in_specs=placed,
        out_specs=(P("dp", "tensor", None), P("tensor", None), P("tensor", None)),
        check_vma=False,
    )
```

profile of v0, /device:TPU:1, one launch (start us, length us, event | category | flops | bytes accessed | tf_op | source)
XLA Modules:
  0.0 611.7 jit_solution(8173062687477292283)
XLA Ops:
  7.2 0.0 all-reduce.2.cloned.1.call-start
  7.2 28.3 %all_gather.3 = bf16[6144,64]{0,1:T(8,128)(2,1)S(1)} all-gather(bf16[768,64]{0,1:T(8,128)(2,1)} %param.5), channel_id=1, replica_groups=mesh['dp'=64,'tensor'=8] {'tensor'}, dimensions={0}, use_global_device_ids=true | all-gather | bytes 884736 | tf_op jit(solution)/shard_map/all_gather | solution.py:14
  35.5 0.0 copy-start
  35.5 0.0 copy-start.1
  35.5 2.7 fusion.3
  38.2 247.1 %psum.21 = f32[128,64]{0,1:T(8,128)S(1)} all-reduce(f32[128,64]{0,1:T(8,128)S(1)} %fusion.3), channel_id=1, replica_groups=mesh['dp'=64,'tensor'=8] {'dp'}, use_global_device_ids=true, to_apply=%region_0.0 | all-reduce | flops 8192 | bytes 65536 | tf_op jit(solution)/shard_map/psum | solution.py:17
  285.3 0.2 fusion.10
  285.5 22.5 %psum.22 = f32[64,64]{0,1:T(8,128)S(1)} all-reduce(f32[64,64]{0,1:T(8,128)S(1)} %fusion.10), channel_id=1, replica_groups=mesh['dp'=64,'tensor'=8] {'tensor'}, use_global_device_ids=true, to_apply=%region_1.0 | all-reduce | flops 4096 | bytes 32768 | tf_op jit(solution)/shard_map/psum | solution.py:19
  308.0 0.1 copy.7
  308.1 5.8 cholesky.16
  314.0 0.6 compare_reduce_fusion
  314.6 0.7 fusion.4
  315.3 4.9 custom-call.6
  320.2 0.3 fusion.5
  320.4 0.0 copy-done
  320.5 0.0 copy-done.1
  320.5 0.0 copy-start.2
  320.5 1.8 fusion.2
  322.2 0.0 all-reduce.2.cloned.1.call-update
  322.3 278.6 %all-reduce.2.cloned.1.call-done = f32[6144,64]{0,1:T(8,128)} async-done(((f32[6144,64]{0,1:T(8,128)}), f32[6144,64]{0,1:T(8,128)}) %all-reduce.2.cloned.1.call-update) | async-done | bytes 1572880 | tf_op jit(solution)/shard_map/psum | solution.py:29
  600.9 1.5 multiply_convert_fusion
  602.4 0.0 copy-done.2
  602.4 1.8 fusion.1
  604.2 0.6 constant_dynamic-slice_fusion
  (2 shorter events, 0.0 us)
Async XLA Ops:
  7.2 593.7 %all-reduce.2.cloned.1.call-start = ((), (), s32[]{:S(2)}) async-start(), calls=%async_computation | async-start | bytes 3145728 | tf_op jit(solution)/shard_map/psum | solution.py:29
  35.5 284.9 %copy-start = (bf16[1,128,6144]{2,1,0:T(8,128)(2,1)S(1)}, bf16[1,128,6144]{2,1,0:T(8,128)(2,1)}, u32[]{:S(2)}) copy-start(bf16[1,128,6144]{2,1,0:T(8,128)(2,1)} %param.4) | copy-start | bytes 4718596
  35.5 284.9 %copy-start.1 = (bf16[1,128,6144]{2,1,0:T(8,128)(2,1)S(1)}, bf16[1,128,6144]{2,1,0:T(8,128)(2,1)}, u32[]{:S(2)}) copy-start(bf16[1,128,6144]{2,1,0:T(8,128)(2,1)} %param.3) | copy-start | bytes 4718596
  320.5 281.9 %copy-start.2 = (f32[128,64]{0,1:T(8,128)}, f32[128,64]{0,1:T(8,128)S(1)}, u32[]{:S(2)}) copy-start(f32[128,64]{0,1:T(8,128)S(1)} %fusion.5) | copy-start | bytes 98308
Sparse Core Ops, SparseCore 0:
  322.4 278.4 all-reduce.1
where the time goes:
time: 612 us
  blocking collectives  298 us (49%)
  waiting for transfers between devices  279 us (46%)
  between operations  14.1 us (2%)
  other arithmetic  13.6 us (2%)
  matrix products  6.71 us (1%)
    psum x1, waiting for transfers between devices, local(): right_sum = lax.psum(right_term, ('dp', 'tensor'))  279 us
    psum x1, blocking collectives, local(): left_sum = lax.psum(left_local, 'dp')  247 us
    all_gather x1, blocking collectives, local(): lax.all_gather(q_in, 'tensor', axis=0, tiled=True)  28.3 us
    psum x1, blocking collectives, local(): gram = lax.psum(partial_gram, 'tensor')  22.5 us
  transfers between devices with their start and end apart: 1, of which 1 were waited for; matrix products, arithmetic and copies ran while one was open for 0% of the time, Pallas kernels for 0%

commit v1 on v0

v1 whole, which is shorter than its diff:
```python
import functools

import jax
import jax.numpy as jnp
from jax import lax
from jax.experimental import pallas as pl
from jax.experimental.pallas import tpu as pltpu
from jax.sharding import Mesh, PartitionSpec as P

F32, BF16 = jnp.float32, jnp.bfloat16
SMEM = pl.BlockSpec(memory_space=pltpu.SMEM)
VMEM = pl.BlockSpec(memory_space=pltpu.VMEM)
PLANE = ("x", "y")
REPLICA = ("x", "y", "core")


def merge_kernel(core_ref, grad_ref, error_ref, keep_ref, give_ref):
    half = keep_ref.shape[-1]
    merged = (grad_ref[...].astype(F32) + error_ref[...].astype(F32)).astype(BF16)
    low, high = merged[:, :half], merged[:, half:]

    @pl.when(core_ref[0] == 0)
    def _():
        keep_ref[0], give_ref[0] = low, high

    @pl.when(core_ref[0] != 0)
    def _():
        keep_ref[0], give_ref[0] = high, low


def left_kernel(factor_ref, keep_ref, took_ref, out_ref):
    @pl.when(pl.program_id(0) == 0)
    def _():
        out_ref[...] = jnp.zeros_like(out_ref)

    lanes = (((1,), (1,)), ((), ()))
    out_ref[...] += lax.dot_general(
        factor_ref[0], keep_ref[0], lanes, preferred_element_type=F32
    ) + lax.dot_general(
        factor_ref[0], took_ref[0], lanes, preferred_element_type=F32
    )


def gram_kernel(left_ref, out_ref):
    left = left_ref[...]
    out_ref[...] = lax.dot_general(
        left, left, (((1,), (1,)), ((), ())),
        precision=lax.Precision.HIGHEST, preferred_element_type=F32,
    )


def factor_kernel(grams_ref, left_ref, factor_ref, round_ref):
    gram = grams_ref[0]
    for part in range(1, grams_ref.shape[0]):
        gram = gram + grams_ref[part]
    rank = gram.shape[0]
    blocks = rank // 8
    rows = [
        (gram[8 * b : 8 * b + 8], left_ref[8 * b : 8 * b + 8, :]) for b in range(blocks)
    ]
    sub = lax.broadcasted_iota(jnp.int32, (8, 1), 0)
    for k in range(rank):
        own, at = k // 8, k % 8
        gram_row = rows[own][0][at : at + 1, :]
        left_row = rows[own][1][at : at + 1, :]
        inverse = 1.0 / gram_row[:, k : k + 1]
        gram_row, left_row = gram_row * inverse, left_row * inverse
        for b in range(own, blocks):
            column = rows[b][0][:, k : k + 1]
            if b == own:
                column = jnp.where(sub > at, column, 0.0)
            rows[b] = (rows[b][0] - column * gram_row, rows[b][1] - column * left_row)
    lane = lax.broadcasted_iota(jnp.int32, (8, rank), 1)
    for b in range(blocks):
        row = lax.broadcasted_iota(jnp.int32, (8, rank), 0) + 8 * b
        pivot = jnp.sum(jnp.where(lane == row, rows[b][0], 0.0), axis=1, keepdims=True)
        factor_ref[8 * b : 8 * b + 8, :] = rows[b][1] / jnp.sqrt(pivot)
    round_ref[...] = factor_ref[...].astype(BF16)


def right_kernel(round_ref, keep_ref, took_ref, out_ref):
    out_ref[0] = jnp.dot(
        round_ref[...], keep_ref[0], preferred_element_type=F32
    ) + jnp.dot(round_ref[...], took_ref[0], preferred_element_type=F32)


def decode_kernel(core_ref, round_ref, own_ref, other_ref, grad_ref, error_ref, out_ref):
    half = own_ref.shape[-1]
    first = core_ref[0] == 0
    own, other = own_ref[0], other_ref[0]
    for part in range(2):
        factor = jnp.where(first if part == 0 else jnp.logical_not(first), own, other)
        decoded = lax.dot_general(
            round_ref[...], factor, (((0,), (0,)), ((), ())), preferred_element_type=F32
        )
        at = pl.ds(part * half, half)
        out_ref[:, at] = (
            grad_ref[:, at].astype(F32) + error_ref[:, at].astype(F32) - decoded
        ).astype(BF16)


def spread(block, axes, count):
    return lax.all_to_all(jnp.broadcast_to(block[None], (count, *block.shape)), axes, 0, 0)


def local(sizes, grad, error, q_in):
    planes, shards, cores = sizes["x"] * sizes["y"], sizes["z"], sizes["core"]
    replicas = planes * cores
    grad, error = grad[0], error[0]
    height, width = grad.shape
    cols, rank = q_in.shape
    half = cols // cores
    core = lax.axis_index("core")
    core_id = core.reshape(1)
    swap = [(0, 1), (1, 0)]

    whole = pl.BlockSpec((height, cols), lambda i: (0, i))
    piece = pl.BlockSpec((1, height, half), lambda i: (i, 0, 0))
    factors = pl.BlockSpec((1, rank, half), lambda i: (i, 0, 0))
    small = pl.BlockSpec((rank, height), lambda i: (0, 0))

    keep, give = pl.pallas_call(
        merge_kernel,
        grid=(shards,),
        in_specs=[SMEM, whole, whole],
        out_specs=[piece, piece],
        out_shape=[jax.ShapeDtypeStruct((shards, height, half), BF16)] * 2,
        name="merge",
    )(core_id, grad, error)
    took = lax.ppermute(give, "core", swap)

    q_mine = lax.dynamic_slice_in_dim(q_in.T, core * half, half, 1)
    q_all = spread(q_mine, "z", shards)
    left = pl.pallas_call(
        left_kernel,
        grid=(shards,),
        in_specs=[factors, piece, piece],
        out_specs=small,
        out_shape=jax.ShapeDtypeStruct((rank, height), F32),
        name="left",
    )(q_all, keep, took)
    left_row = lax.all_to_all(left.reshape(replicas, -1, height), REPLICA, 0, 0).sum(0)
    left_sum = spread(left_row, REPLICA, replicas).reshape(rank, height)

    gram = pl.pallas_call(
        gram_kernel,
        in_specs=[VMEM],
        out_specs=VMEM,
        out_shape=jax.ShapeDtypeStruct((rank, rank), F32),
        name="gram",
    )(left_sum)
    grams = spread(gram, "z", shards)
    p_factor, p_round = pl.pallas_call(
        factor_kernel,
        in_specs=[VMEM, VMEM],
        out_specs=[VMEM, VMEM],
        out_shape=[
            jax.ShapeDtypeStruct((rank, height), F32),
            jax.ShapeDtypeStruct((rank, height), BF16),
        ],
        name="factor",
    )(grams, left_sum)

    right = pl.pallas_call(
        right_kernel,
        grid=(shards,),
        in_specs=[small, piece, piece],
        out_specs=factors,
        out_shape=jax.ShapeDtypeStruct((shards, rank, half), F32),
        name="right",
    )(p_round, keep, took)
    right = lax.all_to_all(right, "z", 0, 0).sum(0)
    right = lax.all_to_all(right.reshape(planes, -1, half), PLANE, 0, 0).sum(0)
    q_rows = (right / replicas).astype(BF16)
    q_block = spread(q_rows, PLANE, planes).reshape(rank, half)
    q_own = spread(q_block, "z", shards)
    q_other = lax.ppermute(q_own, "core", swap)

    new_error = pl.pallas_call(
        decode_kernel,
        grid=(shards,),
        in_specs=[SMEM, small, factors, factors, whole, whole],
        out_specs=whole,
        out_shape=jax.ShapeDtypeStruct((height, cols * shards), BF16),
        name="decode",
    )(core_id, p_round, q_own, q_other, grad, error)

    z = lax.axis_index("z")
    q_pair = [
        lax.dynamic_index_in_dim(q, z, 0, keepdims=False) for q in (q_own, q_other)
    ]
    first = core == 0
    q_next = jnp.concatenate(
        [
            jnp.where(first, q_pair[0], q_pair[1]),
            jnp.where(first, q_pair[1], q_pair[0]),
        ],
        axis=1,
    )
    return new_error[None], p_factor.T, q_next.T


def solution(mesh):
    sizes = {"x": 4, "y": 8, "core": 2, "z": 8}
    fine = Mesh(mesh.devices.reshape(tuple(sizes.values())), tuple(sizes))
    placed = (P(REPLICA, "z", None), P(REPLICA, "z", None), P("z", None))
    return jax.shard_map(
        functools.partial(local, sizes),
        mesh=fine,
        in_specs=placed,
        out_specs=(P(REPLICA, "z", None), P("z", None), P("z", None)),
        check_vma=False,
    )
```

time: 612 us -> 185 us (0.30)
  waiting for transfers between devices: 279 us -> 1.32 us
  blocking collectives: 298 us -> 126 us
  Pallas kernels: 0 us -> 33 us
  starting transfers between devices: 0.04 us -> 16.8 us
  between operations: 14.1 us -> 0.76 us
  other arithmetic: 13.6 us -> 1.87 us
  matrix products: 6.71 us -> 0 us
    psum x1 -> x0, waiting for transfers between devices: 279 us -> none  [local(): right_sum = lax.psum(right_term, ('dp', 'tensor'))]
    psum x2 -> x0, blocking collectives: 270 us -> none  [the longest x1 247 us: local(): left_sum = lax.psum(left_local, 'dp')]
    all_to_all x0 -> x8, blocking collectives: none -> 126 us  [the longest x5 70.7 us: spread(): lax.all_to_all(jnp.broadcast_to(block[None], (count, *block.shape)), axes...]
    pallas_call x0 -> x6, Pallas kernels: none -> 33 us  [the longest x1 6.98 us: local(): pl.pallas_call(factor_kernel, in_specs=[VMEM, VMEM], out_specs=[VMEM, VME...]
    all_gather x1 -> x0, blocking collectives: 28.3 us -> none  [local(): lax.all_gather(q_in, 'tensor', axis=0, tiled=True)]
    ppermute x0 -> x2, starting transfers between devices: none -> 16.8 us  [the longest x1 8.78 us: local(): took = lax.ppermute(give, 'core', swap)]
    another operation x5 -> x0, other arithmetic: 12.1 us -> none  [the longest x3 6.52 us: local(): cholesky_lower = jnp.linalg.cholesky(gram)]
    dot_general x4 -> x0, matrix products: 6.46 us -> none  [the longest x1 2.68 us: local(): jnp.dot(merged, lax.all_gather(q_in, 'tensor', axis=0, tiled=True), prefe...]
  transfers between devices with their start and end apart: 1 -> 2, of which waited for: 1 -> 1; matrix products, arithmetic and copies ran while one was open for 0% -> 0% of each run, Pallas kernels for 0% -> 0%
where the time goes in v1:
time: 185 us; the launch traced here: 183 us
  blocking collectives  126 us (68%)
  Pallas kernels  33 us (18%)
  starting transfers between devices  16.8 us (9%)
  local copies, waits for them, and re-layouts  3.44 us (2%)
  other arithmetic  1.87 us (1%)
    all_to_all x5, blocking collectives, spread(): lax.all_to_all(jnp.broadcast_to(block[None], (count, *block.shape)), axes...  70.7 us
    all_to_all x1, blocking collectives, local(): right = lax.all_to_all(right, 'z', 0, 0).sum(0)  23.7 us
    all_to_all x1, blocking collectives, local(): lax.all_to_all(left.reshape(replicas, -1, height), REPLICA, 0, 0).sum(0)  19.8 us
    all_to_all x1, blocking collectives, local(): right = lax.all_to_all(right.reshape(planes, -1, half), PLANE, 0, 0).sum(0)  12 us
    ppermute x1, starting transfers between devices, local(): took = lax.ppermute(give, 'core', swap)  8.78 us
    ppermute x1, starting transfers between devices, local(): q_other = lax.ppermute(q_own, 'core', swap)  8.04 us
    pallas_call x1, Pallas kernels, local(): pl.pallas_call(factor_kernel, in_specs=[VMEM, VMEM], out_specs=[VMEM, VME...  6.98 us
    pallas_call x1, Pallas kernels, local(): pl.pallas_call(decode_kernel, grid=(shards,), in_specs=[SMEM, small, fact...  6.85 us
  transfers between devices with their start and end apart: 2, of which 1 were waited for; matrix products, arithmetic and copies ran while one was open for 0% of the time, Pallas kernels for 0%

profile of v1, /device:TPU:1, one launch (start us, length us, event | category | flops | bytes accessed | tf_op | source)
XLA Modules:
  0.0 183.5 jit_solution(16654215954381061287)
XLA Ops:
  0.6 0.0 copy-start
  0.7 6.1 %merge.1 = (bf16[8,128,384]{2,1,0:T(8,128)(2,1)}, bf16[8,128,384]{2,1,0:T(8,128)(2,1)}) custom-call(s32[1]{0:T(128)} %bitcast.core_ref, bf16[128,6144]{1,0:T(8,128)(2,1)} %bitcast.17, bf16[128,6144]{1,0:T(8,128)(2,1)} %bitcast.19), custom_call_target="tpu_custom_call" | custom-call | tf_op jit(solution)/shard_map/merge/pallas_call | solution.py:122
  6.8 8.8 %collective-permute-start = (bf16[8,128,384]{2,1,0:T(8,128)(2,1)}, bf16[8,128,384]{2,1,0:T(8,128)(2,1)S(1)}, u32[]{:S(2)}, u32[]{:S(2)}) collective-permute-start(bf16[8,128,384]{2,1,0:T(8,128)(2,1)} %get-tuple-element.8), channel_id=1, source_target_pairs={{0,8},{8,0},{1,9},{9,1},{2,10},{10,2},{3,11},{11,3},{4,12},{12,4},... | collective-permute-start | bytes 2359304 | tf_op jit(solution)/shard_map/ppermute | solution.py:130
  15.6 0.0 copy-done
  15.6 19.7 %all_to_all.40.factor_ref = bf16[8,64,384]{2,1,0:T(8,128)(2,1)} all-to-all(bf16[8,64,384]{2,1,0:T(8,128)(2,1)S(1)} %broadcast_in_dim.14), channel_id=1, replica_groups=mesh['x'=4,'y'=8,'core'=2,'z'=8] {'z'}, dimensions={0} | all-to-all | bytes 786432 | tf_op jit(solution)/shard_map/all_to_all | solution.py:103
  35.4 0.0 collective-permute-done.took_ref
  35.4 0.0 copy-start.1
  35.4 0.9 copy-done.1
  36.3 5.6 %left.1 = f32[64,128]{1,0:T(8,128)} custom-call(bf16[8,64,384]{2,1,0:T(8,128)(2,1)} %all_to_all.40.factor_ref, bf16[8,128,384]{2,1,0:T(8,128)(2,1)} %get-tuple-element.7.keep_ref, bf16[8,128,384]{2,1,0:T(8,128)(2,1)} %copy-done.1), custom_call_target="tpu_custom_call" | custom-call | tf_op jit(solution)/shard_map/left/pallas_call | solution.py:134
  41.9 19.8 %all_to_all.41 = f32[64,1,128]{2,1,0:T(1,128)S(1)} all-to-all(f32[64,1,128]{2,1,0:T(1,128)} %bitcast.24), channel_id=1, replica_groups=mesh['x'=4,'y'=8,'core'=2,'z'=8] {'x','y','core'}, dimensions={0} | all-to-all | bytes 65536 | tf_op jit(solution)/shard_map/all_to_all | solution.py:142
  61.7 0.1 reduce_sum.27
  61.8 14.0 %all_to_all.42 = f32[64,1,128]{2,1,0:T(1,128)} all-to-all(f32[64,1,128]{2,1,0:T(1,128)S(1)} %broadcast_in_dim.15), channel_id=1, replica_groups=mesh['x'=4,'y'=8,'core'=2,'z'=8] {'x','y','core'}, dimensions={0} | all-to-all | bytes 65536 | tf_op jit(solution)/shard_map/all_to_all | solution.py:103
  75.8 1.6 gram.1
  77.4 0.8 broadcast_in_dim.16
  78.1 0.2 reshape.38
  78.3 10.5 %all_to_all.43 = f32[8,1,4096]{2,1,0:T(1,128)S(1)} all-to-all(f32[8,1,4096]{2,1,0:T(1,128)S(1)} %reshape.38), channel_id=1, replica_groups=mesh['x'=4,'y'=8,'core'=2,'z'=8] {'z'}, dimensions={0} | all-to-all | bytes 262144 | tf_op jit(solution)/shard_map/all_to_all | solution.py:103
  88.9 0.5 broadcast.12
  89.4 1.0 reduce.1
  90.3 0.8 reshape.39.grams_ref
  91.2 7.0 %factor.1 = (f32[64,128]{1,0:T(8,128)}, bf16[64,128]{1,0:T(8,128)(2,1)}) custom-call(f32[8,64,64]{2,1,0:T(8,128)} %reshape.39.grams_ref, f32[64,128]{1,0:T(8,128)} %bitcast.23), custom_call_target="tpu_custom_call" | custom-call | tf_op jit(solution)/shard_map/factor/pallas_call | solution.py:153
  98.1 5.9 %right.1 = f32[8,64,384]{2,1,0:T(8,128)} custom-call(bf16[64,128]{1,0:T(8,128)(2,1)} %get-tuple-element.9.round_ref, bf16[8,128,384]{2,1,0:T(8,128)(2,1)} %get-tuple-element.7.keep_ref, bf16[8,128,384]{2,1,0:T(8,128)(2,1)} %copy-done.1), custom_call_target="tpu_custom_call" | custom-call | tf_op jit(solution)/shard_map/right/pallas_call | solution.py:164
  104.0 23.7 %all_to_all.44 = f32[8,64,384]{2,1,0:T(8,128)S(1)} all-to-all(f32[8,64,384]{2,1,0:T(8,128)} %right.1), channel_id=1, replica_groups=mesh['x'=4,'y'=8,'core'=2,'z'=8] {'z'}, dimensions={0} | all-to-all | bytes 1572864 | tf_op jit(solution)/shard_map/all_to_all | solution.py:172
  127.8 0.1 reshape.37
  127.9 12.0 %all_to_all.45 = f32[32,2,384]{2,1,0:T(2,128)S(1)} all-to-all(f32[32,2,384]{2,1,0:T(2,128)S(1)} %reshape.37), channel_id=1, replica_groups=mesh['x'=4,'y'=8,'core'=2,'z'=8] {'x','y'}, dimensions={0} | all-to-all | bytes 196608 | tf_op jit(solution)/shard_map/all_to_all | solution.py:173
  139.9 0.1 reduce_sum.29
  140.0 12.1 %all_to_all.46 = bf16[32,2,384]{2,1,0:T(2,128)(2,1)S(1)} all-to-all(bf16[32,2,384]{2,1,0:T(2,128)(2,1)S(1)} %broadcast_in_dim.17), channel_id=1, replica_groups=mesh['x'=4,'y'=8,'core'=2,'z'=8] {'x','y'}, dimensions={0} | all-to-all | bytes 98304 | tf_op jit(solution)/shard_map/all_to_all | solution.py:103
  152.1 14.4 %all_to_all.47.own_ref = bf16[8,64,384]{2,1,0:T(8,128)(2,1)S(1)} all-to-all(bf16[8,64,384]{2,1,0:T(8,128)(2,1)S(1)} %broadcast_in_dim.19), channel_id=1, replica_groups=mesh['x'=4,'y'=8,'core'=2,'z'=8] {'z'}, dimensions={0} | all-to-all | bytes 786432 | tf_op jit(solution)/shard_map/all_to_all | solution.py:103
  166.5 0.0 copy-start.2
  166.5 8.0 %collective-permute-start.1 = (bf16[8,64,384]{2,1,0:T(8,128)(2,1)S(1)}, bf16[8,64,384]{2,1,0:T(8,128)(2,1)S(1)}, u32[]{:S(2)}, u32[]{:S(2)}) collective-permute-start(bf16[8,64,384]{2,1,0:T(8,128)(2,1)S(1)} %all_to_all.47.own_ref), channel_id=1, source_target_pairs={{0,8},{8,0},{1,9},{9,1},{2,10},{10,2},{3,11},{11,3},{4,12},{12,4},... | collective-permute-start | bytes 1179656 | tf_op jit(solution)/shard_map/ppermute | solution.py:177
  174.5 1.3 collective-permute-done.1.other_ref
  175.8 0.0 copy-start.3
  175.9 0.7 maximum_bitcast_fusion
  176.6 0.0 copy-done.2
  176.6 0.0 copy-done.3
  176.6 6.8 %decode.1 = bf16[128,6144]{1,0:T(8,128)(2,1)} custom-call(s32[1]{0:T(128)} %bitcast.core_ref, bf16[64,128]{1,0:T(8,128)(2,1)} %get-tuple-element.9.round_ref, bf16[8,64,384]{2,1,0:T(8,128)(2,1)} %copy-done.2, bf16[8,64,384]{2,1,0:T(8,128)(2,1)} %copy-done.3, bf16[128,6144]{1,0:T(8,128)(2,1)} %bitcast.18, bf16[128,6144]{1,0:T(8,128)(2,1)} %bitcast.20), custom_call_target="tpu_custom_call" | custom-call | tf_op jit(solution)/shard_map/decode/pallas_call | solution.py:179
  (9 shorter events, 0.2 us)
Async XLA Ops:
  0.6 14.9 %copy-start = (bf16[768,64]{0,1:T(8,128)(2,1)S(1)}, bf16[768,64]{0,1:T(8,128)(2,1)}, u32[]{:S(2)}) copy-start(bf16[768,64]{0,1:T(8,128)(2,1)} %param.5) | copy-start | bytes 294916
  6.8 28.6 %collective-permute-start = (bf16[8,128,384]{2,1,0:T(8,128)(2,1)}, bf16[8,128,384]{2,1,0:T(8,128)(2,1)S(1)}, u32[]{:S(2)}, u32[]{:S(2)}) collective-permute-start(bf16[8,128,384]{2,1,0:T(8,128)(2,1)} %get-tuple-element.8), channel_id=1, source_target_pairs={{0,8},{8,0},{1,9},{9,1},{2,10},{10,2},{3,11},{11,3},{4,12},{12,4},... | collective-permute-start | bytes 2359304 | tf_op jit(solution)/shard_map/ppermute | solution.py:130
  35.4 0.9 copy-start.1
  166.5 10.1 %copy-start.2 = (bf16[8,64,384]{2,1,0:T(8,128)(2,1)}, bf16[8,64,384]{2,1,0:T(8,128)(2,1)S(1)}, u32[]{:S(2)}) copy-start(bf16[8,64,384]{2,1,0:T(8,128)(2,1)S(1)} %all_to_all.47.own_ref) | copy-start | bytes 1179652
  166.5 9.4 %collective-permute-start.1 = (bf16[8,64,384]{2,1,0:T(8,128)(2,1)S(1)}, bf16[8,64,384]{2,1,0:T(8,128)(2,1)S(1)}, u32[]{:S(2)}, u32[]{:S(2)}) collective-permute-start(bf16[8,64,384]{2,1,0:T(8,128)(2,1)S(1)} %all_to_all.47.own_ref), channel_id=1, source_target_pairs={{0,8},{8,0},{1,9},{9,1},{2,10},{10,2},{3,11},{11,3},{4,12},{12,4},... | collective-permute-start | bytes 1179656 | tf_op jit(solution)/shard_map/ppermute | solution.py:177
  175.8 0.8 copy-start.3

commit v2 on v1

v2 whole, which is shorter than its diff:
```python
import functools

import jax
import jax.numpy as jnp
from jax import lax
from jax.experimental import pallas as pl
from jax.experimental.pallas import tpu as pltpu
from jax.sharding import Mesh, PartitionSpec as P

F32, BF16 = jnp.float32, jnp.bfloat16
SMEM = pl.BlockSpec(memory_space=pltpu.SMEM)
VMEM = pl.BlockSpec(memory_space=pltpu.VMEM)
ANY = pl.BlockSpec(memory_space=pl.ANY)
PLANE = ("x", "y")
REPLICA = ("x", "y", "core")
LIMIT = 32 * 2**20


def merge_kernel(core_ref, grad_hbm, error_hbm, keep_ref, give_ref, grad, error, sems):
    parts, _, half = keep_ref.shape
    cols = 2 * half
    copies = []
    for i in range(parts):
        at = pl.ds(i * cols, cols)
        copies.append(
            [
                pltpu.make_async_copy(src.at[:, at], dst.at[:, at], sems.at[j, i])
                for j, (src, dst) in enumerate(((grad_hbm, grad), (error_hbm, error)))
            ]
        )
        for copy in copies[-1]:
            copy.start()
    core = core_ref[0]
    for i in range(parts):
        for copy in copies[i]:
            copy.wait()
        for out, which in ((give_ref, 1 - core), (keep_ref, core)):
            at = pl.ds(pl.multiple_of(i * cols + which * half, half), half)
            out[i] = (grad[:, at].astype(F32) + error[:, at].astype(F32)).astype(BF16)


def left_kernel(factor_ref, keep_ref, took_ref, out_ref):
    height = keep_ref.shape[1]
    total = None
    for i in range(keep_ref.shape[0]):
        both = jnp.concatenate([keep_ref[i], took_ref[i]], axis=0)
        term = lax.dot_general(
            factor_ref[i], both, (((1,), (1,)), ((), ())), preferred_element_type=F32
        )
        total = term if total is None else total + term
    out_ref[...] = total[:, :height] + total[:, height:]


def gram_kernel(left_ref, out_ref):
    left = left_ref[...]
    gram = lax.dot_general(
        left, left, (((1,), (1,)), ((), ())),
        precision=lax.Precision.HIGHEST, preferred_element_type=F32,
    )
    packed = jnp.concatenate(jnp.split(gram, 2, axis=0), axis=1)
    for i in range(out_ref.shape[0]):
        out_ref[i] = packed


def factor_kernel(grams_ref, left_ref, factor_ref, round_ref):
    packed = grams_ref[0]
    for part in range(1, grams_ref.shape[0]):
        packed = packed + grams_ref[part]
    rank = packed.shape[1] // 2
    gram = jnp.concatenate([packed[:, :rank], packed[:, rank:]], axis=0)
    blocks = rank // 8
    rows = [
        (gram[8 * b : 8 * b + 8], left_ref[8 * b : 8 * b + 8, :]) for b in range(blocks)
    ]
    sub = lax.broadcasted_iota(jnp.int32, (8, 1), 0)
    for k in range(0, rank, 2):
        own, at = k // 8, k % 8
        g0, g1 = (rows[own][0][at + j : at + j + 1, :] for j in range(2))
        p0, p1 = (rows[own][1][at + j : at + j + 1, :] for j in range(2))
        a, b, d = g0[:, k : k + 1], g0[:, k + 1 : k + 2], g1[:, k + 1 : k + 2]
        det = a * d - b * b
        inverse = 1.0 / det
        factor_ref[k : k + 1, :] = p0 / jnp.sqrt(a)
        factor_ref[k + 1 : k + 2, :] = (p1 - (b / a) * p0) / jnp.sqrt(det / a)
        ai, bi, di = a * inverse, b * inverse, d * inverse
        u0, u1 = di * g0 - bi * g1, ai * g1 - bi * g0
        v0, v1 = di * p0 - bi * p1, ai * p1 - bi * p0
        for n in range(own, blocks):
            c0, c1 = rows[n][0][:, k : k + 1], rows[n][0][:, k + 1 : k + 2]
            if n == own:
                c0, c1 = (jnp.where(sub > at + 1, c, 0.0) for c in (c0, c1))
            rows[n] = (
                rows[n][0] - c0 * u0 - c1 * u1,
                rows[n][1] - c0 * v0 - c1 * v1,
            )
    round_ref[...] = factor_ref[...].astype(BF16)


def right_kernel(round_ref, keep_ref, took_ref, out_ref):
    twice = jnp.concatenate([round_ref[...], round_ref[...]], axis=1)
    for i in range(keep_ref.shape[0]):
        both = jnp.concatenate([keep_ref[i], took_ref[i]], axis=0)
        out_ref[i] = jnp.dot(twice, both, preferred_element_type=F32)


def decode_kernel(core_ref, round_ref, own_ref, other_ref, grad_hbm, error_hbm, out_hbm, grad, error, out, sems):
    parts, _, half = own_ref.shape
    cols = 2 * half
    copies = []
    for i in range(parts):
        at = pl.ds(i * cols, cols)
        copies.append(
            [
                pltpu.make_async_copy(src.at[:, at], dst.at[:, at], sems.at[j, i])
                for j, (src, dst) in enumerate(((grad_hbm, grad), (error_hbm, error)))
            ]
        )
        for copy in copies[-1]:
            copy.start()
    core = core_ref[0]
    rounded = round_ref[...]
    sent = []
    for i in range(parts):
        for copy in copies[i]:
            copy.wait()
        for factor_ref, which in ((own_ref, core), (other_ref, 1 - core)):
            decoded = lax.dot_general(
                rounded, factor_ref[i], (((0,), (0,)), ((), ())),
                preferred_element_type=F32,
            )
            at = pl.ds(pl.multiple_of(i * cols + which * half, half), half)
            out[:, at] = (
                grad[:, at].astype(F32) + error[:, at].astype(F32) - decoded
            ).astype(BF16)
        at = pl.ds(i * cols, cols)
        sent.append(pltpu.make_async_copy(out.at[:, at], out_hbm.at[:, at], sems.at[2, i]))
        sent[-1].start()
    for copy in sent:
        copy.wait()


def spread(block, axes, count):
    return lax.all_to_all(jnp.broadcast_to(block[None], (count, *block.shape)), axes, 0, 0)


def local(sizes, grad, error, q_in):
    planes, shards, cores = sizes["x"] * sizes["y"], sizes["z"], sizes["core"]
    replicas = planes * cores
    grad, error = grad[0], error[0]
    height, width = grad.shape
    cols, rank = q_in.shape
    half = cols // cores
    core = lax.axis_index("core")
    core_id = core.reshape(1)
    swap = [(0, 1), (1, 0)]

    pieces = jax.ShapeDtypeStruct((shards, height, half), BF16)
    staged = pltpu.VMEM((height, width), BF16)

    keep, give = pl.pallas_call(
        merge_kernel,
        in_specs=[SMEM, ANY, ANY],
        out_specs=[VMEM, VMEM],
        out_shape=[pieces, pieces],
        scratch_shapes=[staged, staged, pltpu.SemaphoreType.DMA((2, shards))],
        compiler_params=pltpu.CompilerParams(vmem_limit_bytes=LIMIT),
        name="merge",
    )(core_id, grad, error)
    took = lax.ppermute(give, "core", swap)

    q_mine = lax.dynamic_slice_in_dim(q_in.T, core * half, half, 1)
    q_all = spread(q_mine, "z", shards)
    left = pl.pallas_call(
        left_kernel,
        in_specs=[VMEM, VMEM, VMEM],
        out_specs=VMEM,
        out_shape=jax.ShapeDtypeStruct((rank, height), F32),
        compiler_params=pltpu.CompilerParams(vmem_limit_bytes=LIMIT),
        name="left",
    )(q_all, keep, took)
    left_row = lax.all_to_all(left.reshape(replicas, -1, height), REPLICA, 0, 0).sum(0)
    left_sum = spread(left_row, REPLICA, replicas).reshape(rank, height)

    gram = pl.pallas_call(
        gram_kernel,
        in_specs=[VMEM],
        out_specs=VMEM,
        out_shape=jax.ShapeDtypeStruct((shards, rank // 2, 2 * rank), F32),
        name="gram",
    )(left_sum)
    grams = lax.all_to_all(gram, "z", 0, 0)
    p_factor, p_round = pl.pallas_call(
        factor_kernel,
        in_specs=[VMEM, VMEM],
        out_specs=[VMEM, VMEM],
        out_shape=[
            jax.ShapeDtypeStruct((rank, height), F32),
            jax.ShapeDtypeStruct((rank, height), BF16),
        ],
        name="factor",
    )(grams, left_sum)

    right = pl.pallas_call(
        right_kernel,
        in_specs=[VMEM, VMEM, VMEM],
        out_specs=VMEM,
        out_shape=jax.ShapeDtypeStruct((shards, rank, half), F32),
        compiler_params=pltpu.CompilerParams(vmem_limit_bytes=LIMIT),
        name="right",
    )(p_round, keep, took)
    right = lax.all_to_all(right, "z", 0, 0).sum(0)
    right = lax.all_to_all(right.reshape(planes, -1, half), PLANE, 0, 0).sum(0)
    q_rows = (right / replicas).astype(BF16)
    q_block = spread(q_rows, PLANE, planes).reshape(rank, half)
    q_own = spread(q_block, "z", shards)
    q_other = lax.ppermute(q_own, "core", swap)

    new_error = pl.pallas_call(
        decode_kernel,
        in_specs=[SMEM, VMEM, VMEM, VMEM, ANY, ANY],
        out_specs=ANY,
        out_shape=jax.ShapeDtypeStruct((height, width), BF16),
        scratch_shapes=[staged] * 3 + [pltpu.SemaphoreType.DMA((3, shards))],
        compiler_params=pltpu.CompilerParams(vmem_limit_bytes=LIMIT),
        name="decode",
    )(core_id, p_round, q_own, q_other, grad, error)

    z = lax.axis_index("z")
    q_pair = [
        lax.dynamic_index_in_dim(q, z, 0, keepdims=False) for q in (q_own, q_other)
    ]
    first = core == 0
    q_next = jnp.concatenate(
        [
            jnp.where(first, q_pair[0], q_pair[1]),
            jnp.where(first, q_pair[1], q_pair[0]),
        ],
        axis=1,
    )
    return new_error[None], p_factor.T, q_next.T


def solution(mesh):
    sizes = {"x": 4, "y": 8, "core": 2, "z": 8}
    fine = Mesh(mesh.devices.reshape(tuple(sizes.values())), tuple(sizes))
    placed = (P(REPLICA, "z", None), P(REPLICA, "z", None), P("z", None))
    return jax.shard_map(
        functools.partial(local, sizes),
        mesh=fine,
        in_specs=placed,
        out_specs=(P(REPLICA, "z", None), P("z", None), P("z", None)),
        check_vma=False,
    )
```

time: 185 us -> 172 us (0.930)
  Pallas kernels: 33 us -> 17.5 us
    pallas_call x4, Pallas kernels: 24.5 us -> 6.13 us  [the longest x1 4.04 us: local(): pl.pallas_call(decode_kernel, in_specs=[SMEM, VMEM, VMEM, VMEM, ANY, ANY]...]
    all_to_all x0 -> x1, blocking collectives: none -> 12.1 us  [local(): grams = lax.all_to_all(gram, 'z', 0, 0)]
    all_to_all x5 -> x4, blocking collectives: 70.7 us -> 60.1 us  [spread(): lax.all_to_all(jnp.broadcast_to(block[None], (count, *block.shape)), axes...]
    pallas_call x1, Pallas kernels: 6.98 us -> 9.75 us  [local(): pl.pallas_call(factor_kernel, in_specs=[VMEM, VMEM], out_specs=[VMEM, VME...]
where the time goes in v2:
time: 172 us; the launch traced here: 171 us
  blocking collectives  127 us (74%)
  Pallas kernels  17.5 us (10%)
  starting transfers between devices  17.5 us (10%)
  local copies, waits for them, and re-layouts  3.8 us (2%)
  other arithmetic  2.96 us (2%)
    all_to_all x4, blocking collectives, spread(): lax.all_to_all(jnp.broadcast_to(block[None], (count, *block.shape)), axes...  60.1 us
    all_to_all x1, blocking collectives, local(): right = lax.all_to_all(right, 'z', 0, 0).sum(0)  23.3 us
    all_to_all x1, blocking collectives, local(): lax.all_to_all(left.reshape(replicas, -1, height), REPLICA, 0, 0).sum(0)  19.7 us
    all_to_all x1, blocking collectives, local(): grams = lax.all_to_all(gram, 'z', 0, 0)  12.1 us
    all_to_all x1, blocking collectives, local(): right = lax.all_to_all(right.reshape(planes, -1, half), PLANE, 0, 0).sum(0)  12 us
    pallas_call x1, Pallas kernels, local(): pl.pallas_call(factor_kernel, in_specs=[VMEM, VMEM], out_specs=[VMEM, VME...  9.75 us
    ppermute x1, starting transfers between devices, local(): took = lax.ppermute(give, 'core', swap)  8.79 us
    ppermute x1, starting transfers between devices, local(): q_other = lax.ppermute(q_own, 'core', swap)  8.73 us
  transfers between devices with their start and end apart: 2, of which 1 were waited for; matrix products, arithmetic and copies ran while one was open for 0% of the time, Pallas kernels for 0%

profile of v2, /device:TPU:1, one launch (start us, length us, event | category | flops | bytes accessed | tf_op | source)
XLA Modules:
  0.0 171.5 jit_solution(15677844725763211227)
XLA Ops:
  0.6 0.0 copy-start
  0.7 0.0 copy-start.1
  0.7 1.4 copy-done.1
  2.1 0.0 copy-start.3
  2.1 1.4 copy-done.3
  3.5 1.2 merge.1
  4.7 8.8 %collective-permute-start = (bf16[8,128,384]{2,1,0:T(8,128)(2,1)S(1)}, bf16[8,128,384]{2,1,0:T(8,128)(2,1)S(1)}, u32[]{:S(2)}, u32[]{:S(2)}) collective-permute-start(bf16[8,128,384]{2,1,0:T(8,128)(2,1)S(1)} %get-tuple-element.8), channel_id=1, source_target_pairs={{0,8},{8,0},{1,9},{9,1},{2,10},{10,2},{3,11},{11,3},{4,12},{12,4},... | collective-permute-start | bytes 2359304 | tf_op jit(solution)/shard_map/ppermute | solution.py:169
  13.5 0.0 copy-done
  13.5 19.6 %all_to_all.40.factor_ref = bf16[8,64,384]{2,1,0:T(8,128)(2,1)S(1)} all-to-all(bf16[8,64,384]{2,1,0:T(8,128)(2,1)S(1)} %broadcast_in_dim.12), channel_id=1, replica_groups=mesh['x'=4,'y'=8,'core'=2,'z'=8] {'z'}, dimensions={0} | all-to-all | bytes 786432 | tf_op jit(solution)/shard_map/all_to_all | solution.py:143
  33.2 0.0 collective-permute-done.took_ref
  33.2 0.6 left.1
  33.8 19.7 %all_to_all.41 = f32[64,1,128]{2,1,0:T(1,128)S(1)} all-to-all(f32[64,1,128]{2,1,0:T(1,128)S(1)} %bitcast.21), channel_id=1, replica_groups=mesh['x'=4,'y'=8,'core'=2,'z'=8] {'x','y','core'}, dimensions={0} | all-to-all | bytes 65536 | tf_op jit(solution)/shard_map/all_to_all | solution.py:181
  53.4 0.1 reduce_sum.27
  53.6 14.0 %all_to_all.42 = f32[64,1,128]{2,1,0:T(1,128)} all-to-all(f32[64,1,128]{2,1,0:T(1,128)S(1)} %broadcast_in_dim.13), channel_id=1, replica_groups=mesh['x'=4,'y'=8,'core'=2,'z'=8] {'x','y','core'}, dimensions={0} | all-to-all | bytes 65536 | tf_op jit(solution)/shard_map/all_to_all | solution.py:143
  67.5 1.7 gram.1
  69.2 12.1 %all_to_all.43.grams_ref = f32[8,32,128]{2,1,0:T(8,128)} all-to-all(f32[8,32,128]{2,1,0:T(8,128)} %gram.1), channel_id=1, replica_groups=mesh['x'=4,'y'=8,'core'=2,'z'=8] {'z'}, dimensions={0} | all-to-all | bytes 262144 | tf_op jit(solution)/shard_map/all_to_all | solution.py:191
  81.3 9.7 %factor.1 = (f32[64,128]{1,0:T(8,128)}, bf16[64,128]{1,0:T(8,128)(2,1)}) custom-call(f32[8,32,128]{2,1,0:T(8,128)} %all_to_all.43.grams_ref, f32[64,128]{1,0:T(8,128)} %bitcast.24), custom_call_target="tpu_custom_call" | custom-call | tf_op jit(solution)/shard_map/factor/pallas_call | solution.py:192
  91.1 0.0 copy-start.5
  91.1 0.7 copy-done.5
  91.8 0.3 right.1
  92.1 23.3 %all_to_all.44 = f32[8,64,384]{2,1,0:T(8,128)} all-to-all(f32[8,64,384]{2,1,0:T(8,128)S(1)} %right.1), channel_id=1, replica_groups=mesh['x'=4,'y'=8,'core'=2,'z'=8] {'z'}, dimensions={0} | all-to-all | bytes 1572864 | tf_op jit(solution)/shard_map/all_to_all | solution.py:211
  115.5 0.0 copy-start.2
  115.5 0.0 copy-start.4
  115.5 0.0 copy-start.6
  115.5 1.3 reduce_sum.28
  116.8 0.1 reshape.36
  116.9 12.0 %all_to_all.45 = f32[32,2,384]{2,1,0:T(2,128)S(1)} all-to-all(f32[32,2,384]{2,1,0:T(2,128)S(1)} %reshape.36), channel_id=1, replica_groups=mesh['x'=4,'y'=8,'core'=2,'z'=8] {'x','y'}, dimensions={0} | all-to-all | bytes 196608 | tf_op jit(solution)/shard_map/all_to_all | solution.py:212
  128.9 0.1 reduce_sum.29
  129.0 12.1 %all_to_all.46 = bf16[32,2,384]{2,1,0:T(2,128)(2,1)S(1)} all-to-all(bf16[32,2,384]{2,1,0:T(2,128)(2,1)S(1)} %broadcast_in_dim.14), channel_id=1, replica_groups=mesh['x'=4,'y'=8,'core'=2,'z'=8] {'x','y'}, dimensions={0} | all-to-all | bytes 98304 | tf_op jit(solution)/shard_map/all_to_all | solution.py:143
  141.1 14.4 %all_to_all.47.own_ref = bf16[8,64,384]{2,1,0:T(8,128)(2,1)} all-to-all(bf16[8,64,384]{2,1,0:T(8,128)(2,1)S(1)} %broadcast_in_dim.32), channel_id=1, replica_groups=mesh['x'=4,'y'=8,'core'=2,'z'=8] {'z'}, dimensions={0} | all-to-all | bytes 786432 | tf_op jit(solution)/shard_map/all_to_all | solution.py:143
  155.5 8.7 %collective-permute-start.1 = (bf16[8,64,384]{2,1,0:T(8,128)(2,1)}, bf16[8,64,384]{2,1,0:T(8,128)(2,1)}, u32[]{:S(2)}, u32[]{:S(2)}) collective-permute-start(bf16[8,64,384]{2,1,0:T(8,128)(2,1)} %all_to_all.47.own_ref), channel_id=1, source_target_pairs={{0,8},{8,0},{1,9},{9,1},{2,10},{10,2},{3,11},{11,3},{4,12},{12,4},... | collective-permute-start | bytes 1179656 | tf_op jit(solution)/shard_map/ppermute | solution.py:216
  164.3 1.7 collective-permute-done.1.other_ref
  165.9 0.8 select_bitcast_fusion.1
  166.8 0.7 maximum_bitcast_fusion
  167.4 0.0 copy-done.2
  167.4 0.0 copy-done.4
  167.4 0.0 copy-done.6
  167.4 4.0 %decode.1 = bf16[128,6144]{1,0:T(8,128)(2,1)} custom-call(s32[1]{0:T(128)} %bitcast.core_ref, bf16[64,128]{1,0:T(8,128)(2,1)S(1)} %copy-done.6, bf16[8,64,384]{2,1,0:T(8,128)(2,1)} %all_to_all.47.own_ref, bf16[8,64,384]{2,1,0:T(8,128)(2,1)} %collective-permute-done.1.other_ref, bf16[128,6144]{1,0:T(8,128)(2,1)S(1)} %bitcast.18, bf16[128,6144]{1,0:T(8,128)(2,1)S(1)} %bitcast.20), custom_call_target="tpu_custom_call" | custom-call | tf_op jit(solution)/shard_map/decode/pallas_call | solution.py:218
  (7 shorter events, 0.2 us)
Async XLA Ops:
  0.6 12.8 %copy-start = (bf16[768,64]{0,1:T(8,128)(2,1)S(1)}, bf16[768,64]{0,1:T(8,128)(2,1)}, u32[]{:S(2)}) copy-start(bf16[768,64]{0,1:T(8,128)(2,1)} %param.5) | copy-start | bytes 294916
  0.7 1.4 copy-start.1
  2.1 1.4 copy-start.3
  4.7 28.5 %collective-permute-start = (bf16[8,128,384]{2,1,0:T(8,128)(2,1)S(1)}, bf16[8,128,384]{2,1,0:T(8,128)(2,1)S(1)}, u32[]{:S(2)}, u32[]{:S(2)}) collective-permute-start(bf16[8,128,384]{2,1,0:T(8,128)(2,1)S(1)} %get-tuple-element.8), channel_id=1, source_target_pairs={{0,8},{8,0},{1,9},{9,1},{2,10},{10,2},{3,11},{11,3},{4,12},{12,4},... | collective-permute-start | bytes 2359304 | tf_op jit(solution)/shard_map/ppermute | solution.py:169
  91.1 0.7 copy-start.5
  115.5 51.9 %copy-start.2 = (bf16[1,128,6144]{2,1,0:T(8,128)(2,1)S(1)}, bf16[1,128,6144]{2,1,0:T(8,128)(2,1)}, u32[]{:S(2)}) copy-start(bf16[1,128,6144]{2,1,0:T(8,128)(2,1)} %param.3) | copy-start | bytes 4718596
  115.5 51.9 %copy-start.4 = (bf16[1,128,6144]{2,1,0:T(8,128)(2,1)S(1)}, bf16[1,128,6144]{2,1,0:T(8,128)(2,1)}, u32[]{:S(2)}) copy-start(bf16[1,128,6144]{2,1,0:T(8,128)(2,1)} %param.4) | copy-start | bytes 4718596
  115.5 51.9 %copy-start.6 = (bf16[64,128]{1,0:T(8,128)(2,1)S(1)}, bf16[64,128]{1,0:T(8,128)(2,1)}, u32[]{:S(2)}) copy-start(bf16[64,128]{1,0:T(8,128)(2,1)} %get-tuple-element.9.round_ref) | copy-start | bytes 49156
  155.5 10.4 %collective-permute-start.1 = (bf16[8,64,384]{2,1,0:T(8,128)(2,1)}, bf16[8,64,384]{2,1,0:T(8,128)(2,1)}, u32[]{:S(2)}, u32[]{:S(2)}) collective-permute-start(bf16[8,64,384]{2,1,0:T(8,128)(2,1)} %all_to_all.47.own_ref), channel_id=1, source_target_pairs={{0,8},{8,0},{1,9},{9,1},{2,10},{10,2},{3,11},{11,3},{4,12},{12,4},... | collective-permute-start | bytes 1179656 | tf_op jit(solution)/shard_map/ppermute | solution.py:216

commit v3 on v2

v3 whole, which is shorter than its diff:
```python
import functools

import jax
import jax.numpy as jnp
from jax import lax
from jax.experimental import pallas as pl
from jax.experimental.pallas import tpu as pltpu
from jax.sharding import Mesh, PartitionSpec as P

F32, BF16 = jnp.float32, jnp.bfloat16
SMEM = pl.BlockSpec(memory_space=pltpu.SMEM)
VMEM = pl.BlockSpec(memory_space=pltpu.VMEM)
HBM = pl.BlockSpec(memory_space=pltpu.HBM)
PLANE = ("x", "y")
REPLICA = ("x", "y", "core")
LIMIT = 16 * 2**20


def merge_kernel(core_ref, grad_hbm, error_hbm, keep_ref, give_ref, grad, error, sems):
    parts, _, half = keep_ref.shape
    cols = 2 * half
    copies = []
    for i in range(parts):
        at = pl.ds(i * cols, cols)
        copies.append(
            [
                pltpu.make_async_copy(src.at[:, at], dst.at[:, at], sems.at[j, i])
                for j, (src, dst) in enumerate(((grad_hbm, grad), (error_hbm, error)))
            ]
        )
        for copy in copies[-1]:
            copy.start()
    core = core_ref[0]
    for i in range(parts):
        for copy in copies[i]:
            copy.wait()
        for out, which in ((give_ref, 1 - core), (keep_ref, core)):
            at = pl.ds(pl.multiple_of(i * cols + which * half, half), half)
            out[i] = (grad[:, at].astype(F32) + error[:, at].astype(F32)).astype(BF16)


def pair_kernel(keep_ref, took_ref, out_ref):
    for i in range(out_ref.shape[0]):
        out_ref[i] = keep_ref[i].astype(F32) + took_ref[i].astype(F32)


def left_kernel(factor_ref, keep_ref, took_ref, out_ref):
    height = keep_ref.shape[1]
    total = None
    for i in range(keep_ref.shape[0]):
        both = jnp.concatenate([keep_ref[i], took_ref[i]], axis=0)
        term = lax.dot_general(
            factor_ref[i], both, (((1,), (1,)), ((), ())), preferred_element_type=F32
        )
        total = term if total is None else total + term
    out_ref[...] = total[:, :height] + total[:, height:]


def gram_kernel(left_ref, out_ref):
    left = left_ref[...]
    gram = lax.dot_general(
        left, left, (((1,), (1,)), ((), ())),
        precision=lax.Precision.HIGHEST, preferred_element_type=F32,
    )
    packed = jnp.concatenate(jnp.split(gram, 2, axis=0), axis=1)
    for i in range(out_ref.shape[0]):
        out_ref[i] = packed


def factor_kernel(grams_ref, left_ref, factor_ref, round_ref):
    packed = grams_ref[0]
    for part in range(1, grams_ref.shape[0]):
        packed = packed + grams_ref[part]
    rank = packed.shape[1] // 2
    gram = jnp.concatenate([packed[:, :rank], packed[:, rank:]], axis=0)
    gram = jnp.concatenate([gram, gram], axis=1)
    blocks = rank // 8
    g = [gram[8 * n : 8 * n + 8] for n in range(blocks)]
    p = [left_ref[8 * n : 8 * n + 8, :] for n in range(blocks)]
    full = (8, 2 * rank)
    sub = lax.broadcasted_iota(jnp.int32, full, 0)

    def lane(v, k):
        return jnp.broadcast_to(v[:, k : k + 1], full)

    def row(v, k):
        return jnp.broadcast_to(v[k : k + 1, :], full)

    hold = None
    for k in range(0, rank, 4):
        own, at = k // 8, k % 8
        gs = [row(g[own], at + j) for j in range(4)]
        ps = [row(p[own], at + j) for j in range(4)]
        e = {(i, j): lane(gs[i], k + j) for i in range(4) for j in range(i, 4)}
        a, b, d = e[0, 0], e[0, 1], e[1, 1]
        det = a * d - b * b
        inverse = 1.0 / det
        ai, bi, di = a * inverse, b * inverse, d * inverse
        t00, t01 = di * e[0, 2] - bi * e[1, 2], di * e[0, 3] - bi * e[1, 3]
        t10, t11 = ai * e[1, 2] - bi * e[0, 2], ai * e[1, 3] - bi * e[0, 3]
        a2 = e[2, 2] - e[0, 2] * t00 - e[1, 2] * t10
        b2 = e[2, 3] - e[0, 2] * t01 - e[1, 2] * t11
        d2 = e[3, 3] - e[0, 3] * t01 - e[1, 3] * t11
        det2 = a2 * d2 - b2 * b2
        inverse2 = 1.0 / det2
        ai2, bi2, di2 = a2 * inverse2, b2 * inverse2, d2 * inverse2

        def solve(r):
            s2 = r[2] - t00 * r[0] - t10 * r[1]
            s3 = r[3] - t01 * r[0] - t11 * r[1]
            w2, w3 = di2 * s2 - bi2 * s3, ai2 * s3 - bi2 * s2
            q0, q1 = di * r[0] - bi * r[1], ai * r[1] - bi * r[0]
            w0, w1 = q0 - t00 * w2 - t01 * w3, q1 - t10 * w2 - t11 * w3
            return (w0, w1, w2, w3), s2, s3

        u, _, _ = solve(gs)
        v, s2, s3 = solve(ps)
        done = (
            ps[0] / jnp.sqrt(a),
            (ps[1] - (b / a) * ps[0]) / jnp.sqrt(det / a),
            s2 / jnp.sqrt(a2),
            (s3 - (b2 / a2) * s2) / jnp.sqrt(det2 / a2),
        )
        out = done[0]
        for j in range(1, 4):
            out = jnp.where(sub == at + j, done[j], out)
        if at == 0:
            hold = out
        else:
            factor_ref[8 * own : 8 * own + 8, :] = jnp.where(sub < 4, hold, out)
        for n in range(own if at == 0 else own + 1, blocks):
            c = [lane(g[n], k + j) for j in range(4)]
            if n == own:
                c = [jnp.where(sub > at + 3, x, 0.0) for x in c]
            g[n] = g[n] - (c[0] * u[0] + c[1] * u[1]) - (c[2] * u[2] + c[3] * u[3])
            p[n] = p[n] - (c[0] * v[0] + c[1] * v[1]) - (c[2] * v[2] + c[3] * v[3])
    round_ref[...] = factor_ref[...].T.astype(BF16)


def right_kernel(slab_ref, round_ref, out_ref):
    slab = slab_ref[0]
    for i in range(1, slab_ref.shape[0]):
        slab = slab + slab_ref[i]
    term = jnp.dot(
        slab, round_ref[...].astype(F32),
        precision=lax.Precision.HIGHEST, preferred_element_type=F32,
    )
    packed = jnp.concatenate(jnp.split(term, 2, axis=0), axis=1)
    for i in range(out_ref.shape[0]):
        out_ref[i] = packed


def decode_kernel(place_ref, round_ref, own_ref, other_ref, grad, error, out_hbm, next_ref, out, sems):
    planes, fold, lanes = own_ref.shape
    rank = lanes // 2
    parts = grad.shape[1] // next_ref.shape[1]
    inner = planes // parts
    half = 2 * fold * inner
    cols = 2 * half
    core, z = place_ref[0], place_ref[1]
    rounded = round_ref[...]

    def factor(ref, part):
        pieces = []
        for x in range(inner):
            piece = ref[x * parts + part]
            pieces += [piece[:, :rank], piece[:, rank:]]
        return jnp.concatenate(pieces, axis=0)

    sent = []
    for i in range(parts):
        for ref, which in ((own_ref, core), (other_ref, 1 - core)):
            decoded = lax.dot_general(
                rounded, factor(ref, i), (((1,), (1,)), ((), ())),
                preferred_element_type=F32,
            )
            at = pl.ds(pl.multiple_of(i * cols + which * half, half), half)
            out[:, at] = (
                grad[:, at].astype(F32) + error[:, at].astype(F32) - decoded
            ).astype(BF16)
        at = pl.ds(i * cols, cols)
        sent.append(pltpu.make_async_copy(out.at[:, at], out_hbm.at[:, at], sems.at[i]))
        sent[-1].start()
    for ref, which in ((own_ref, core), (other_ref, 1 - core)):
        at = pl.ds(pl.multiple_of(which * half, half), half)
        next_ref[:, at] = factor(ref, z).astype(F32).T.astype(BF16)
    for copy in sent:
        copy.wait()


def call(kernel, name, out_shape, in_specs, out_specs=VMEM, scratch_shapes=()):
    return pl.pallas_call(
        kernel,
        in_specs=in_specs,
        out_specs=out_specs,
        out_shape=out_shape,
        scratch_shapes=scratch_shapes,
        compiler_params=pltpu.CompilerParams(vmem_limit_bytes=LIMIT),
        name=name,
    )


def spread(block, axes, count):
    return lax.all_to_all(jnp.broadcast_to(block[None], (count, *block.shape)), axes, 0, 0)


def local(sizes, grad, error, q_in):
    across, along, shards, cores = sizes["x"], sizes["y"], sizes["z"], sizes["core"]
    planes = across * along
    replicas = planes * cores
    grad, error = grad[0], error[0]
    height, width = grad.shape
    cols, rank = q_in.shape
    half = cols // cores
    core, z = lax.axis_index("core"), lax.axis_index("z")
    swap = [(0, 1), (1, 0)]
    array = jax.ShapeDtypeStruct

    pieces = array((along, height, half), BF16)
    staged = pltpu.VMEM((height, width), BF16)
    keep, give = call(
        merge_kernel, "merge", [pieces, pieces], [SMEM, HBM, HBM], [VMEM, VMEM],
        [staged, staged, pltpu.SemaphoreType.DMA((2, along))],
    )(core.reshape(1), grad, error)
    took = lax.ppermute(give, "core", swap)
    pair = call(pair_kernel, "pair", array(pieces.shape, F32), [VMEM, VMEM])(keep, took)
    q_in, pair = lax.optimization_barrier((q_in, pair))
    slab = lax.psum_scatter(pair, "y", scatter_dimension=0, tiled=True)[0]

    q_mine = lax.dynamic_slice_in_dim(q_in.T, core * half, half, 1)
    q_all = spread(q_mine, "z", shards)
    left = call(left_kernel, "left", array((rank, height), F32), [VMEM] * 3)(
        q_all, keep, took
    )
    left_row = lax.all_to_all(left.reshape(replicas, -1, height), REPLICA, 0, 0).sum(0)
    left_sum = spread(left_row, REPLICA, replicas).reshape(rank, height)

    gram = call(gram_kernel, "gram", array((shards, rank // 2, 2 * rank), F32), [VMEM])(
        left_sum
    )
    grams = lax.all_to_all(gram, "z", 0, 0)
    p_factor, p_round = call(
        factor_kernel, "factor",
        [array((rank, height), F32), array((height, rank), BF16)],
        [VMEM, VMEM], [VMEM, VMEM],
    )(grams, left_sum)

    fold = half // across
    slab = lax.all_to_all(slab.T.reshape(across, fold, height), "x", 0, 0)
    term = call(
        right_kernel, "right", array((shards, fold // 2, 2 * rank), F32), [VMEM, VMEM]
    )(slab, p_round)
    q_mine = (lax.all_to_all(term, "z", 0, 0).sum(0) / replicas).astype(BF16)
    q_own = spread(q_mine, PLANE, planes)
    q_other = lax.ppermute(q_own, "core", swap)

    new_error, q_next = call(
        decode_kernel, "decode",
        [array((height, width), BF16), array((rank, cols), BF16)],
        [SMEM] + [VMEM] * 5, [HBM, VMEM],
        [staged, pltpu.SemaphoreType.DMA((along,))],
    )(jnp.stack([core, z]), p_round, q_own, q_other, grad, error)
    return new_error[None], p_factor.T, q_next.T


def solution(mesh):
    sizes = {"x": 4, "y": 8, "core": 2, "z": 8}
    fine = Mesh(mesh.devices.reshape(tuple(sizes.values())), tuple(sizes))
    placed = (P(REPLICA, "z", None), P(REPLICA, "z", None), P("z", None))
    return jax.shard_map(
        functools.partial(local, sizes),
        mesh=fine,
        in_specs=placed,
        out_specs=(P(REPLICA, "z", None), P("z", None), P("z", None)),
        check_vma=False,
    )
```

time: 172 us -> 144 us (0.84)
  blocking collectives: 127 us -> 77.9 us
  between operations: 0.77 us -> 14.2 us
  waiting for transfers between devices: 1.66 us -> 10.1 us
  Pallas kernels: 17.5 us -> 11.1 us
  starting transfers between devices: 17.5 us -> 23.9 us
  other arithmetic: 2.96 us -> 0.18 us
  local copies, waits for them, and re-layouts: 3.8 us -> 6.38 us
    all_to_all x3 -> x1, blocking collectives: 47.5 us -> 11.1 us  [local(): q_mine = (lax.all_to_all(term, 'z', 0, 0).sum(0) / replicas).astype(BF16)]
    all_to_all x4 -> x3, blocking collectives: 60.1 us -> 45.9 us  [spread(): lax.all_to_all(jnp.broadcast_to(block[None], (count, *block.shape)), axes...]
    all_to_all x0 -> x2, starting transfers between devices: none -> 6.74 us  [the longest x1 3.37 us: local(): grams = lax.all_to_all(gram, 'z', 0, 0)]
    all_to_all x0 -> x2, waiting for transfers between devices: none -> 6.56 us  [the longest x1 5.81 us: local(): grams = lax.all_to_all(gram, 'z', 0, 0)]
    pallas_call x6 -> x7, Pallas kernels: 17.5 us -> 11.1 us  [the longest x1 3.48 us: local(): call(factor_kernel, 'factor', [array((rank, height), F32), array((height,...]
    ppermute x1, waiting for transfers between devices: 0.01 us -> 1.89 us  [local(): took = lax.ppermute(give, 'core', swap)]
    transpose x0 -> x1, local copies, waits for them, and re-layouts: none -> 1.89 us  [local(): slab = lax.all_to_all(slab.T.reshape(across, fold, height), 'x', 0, 0)]
  transfers between devices with their start and end apart: 2 -> 5, of which waited for: 1 -> 4; matrix products, arithmetic and copies ran while one was open for 0% -> 1% of each run, Pallas kernels for 0% -> 3%
where the time goes in v3:
time: 144 us
  blocking collectives  77.9 us (54%)
  starting transfers between devices  23.9 us (17%)
  between operations  14.2 us (10%)
  Pallas kernels  11.1 us (8%)
  waiting for transfers between devices  10.1 us (7%)
  local copies, waits for them, and re-layouts  6.38 us (4%)
    all_to_all x3, blocking collectives, spread(): lax.all_to_all(jnp.broadcast_to(block[None], (count, *block.shape)), axes...  45.9 us
    all_to_all x1, blocking collectives, local(): lax.all_to_all(left.reshape(replicas, -1, height), REPLICA, 0, 0).sum(0)  21 us
    all_to_all x1, blocking collectives, local(): q_mine = (lax.all_to_all(term, 'z', 0, 0).sum(0) / replicas).astype(BF16)  11.1 us
    ppermute x1, starting transfers between devices, local(): took = lax.ppermute(give, 'core', swap)  8.79 us
    ppermute x1, starting transfers between devices, local(): q_other = lax.ppermute(q_own, 'core', swap)  8.37 us
    all_to_all x1, waiting for transfers between devices, local(): grams = lax.all_to_all(gram, 'z', 0, 0)  5.81 us
    unnamed x14, local copies, waits for them, and re-layouts  4.37 us
    pallas_call x1, Pallas kernels, local(): call(factor_kernel, 'factor', [array((rank, height), F32), array((height,...  3.48 us
  transfers between devices with their start and end apart: 5, of which 4 were waited for; matrix products, arithmetic and copies ran while one was open for 1% of the time, Pallas kernels for 3%

profile of v3, /device:TPU:1, one launch (start us, length us, event | category | flops | bytes accessed | tf_op | source)
XLA Modules:
  0.0 143.8 jit_solution(1885936004226549628)
XLA Ops:
  7.2 0.0 copy-start
  7.2 0.0 reduce-scatter.2.cloned.1.call-start
  7.2 0.0 copy-start.1
  7.2 1.4 copy-done.1
  8.6 0.0 copy-start.3
  8.6 1.4 copy-done.3
  10.1 1.2 merge.1
  11.2 8.8 %collective-permute-start = (bf16[8,128,384]{2,1,0:T(8,128)(2,1)S(1)}, bf16[8,128,384]{2,1,0:T(8,128)(2,1)S(1)}, u32[]{:S(2)}, u32[]{:S(2)}) collective-permute-start(bf16[8,128,384]{2,1,0:T(8,128)(2,1)S(1)} %get-tuple-element.12), channel_id=1, source_target_pairs={{0,8},{8,0},{1,9},{9,1},{2,10},{10,2},{3,11},{11,3},{4,12},{12,4},... | collective-permute-start | bytes 2359304 | tf_op jit(solution)/shard_map/ppermute | solution.py:225
  20.0 1.9 %collective-permute-done.took_ref = bf16[8,128,384]{2,1,0:T(8,128)(2,1)S(1)} collective-permute-done((bf16[8,128,384]{2,1,0:T(8,128)(2,1)S(1)}, bf16[8,128,384]{2,1,0:T(8,128)(2,1)S(1)}, u32[]{:S(2)}, u32[]{:S(2)}) %collective-permute-start) | collective-permute-done | bytes 786464 | tf_op jit(solution)/shard_map/ppermute | solution.py:225
  21.9 1.3 pair.1
  23.2 0.0 reduce-scatter.2.cloned.1.call-update
  23.2 0.0 copy-done
  23.3 18.3 %all_to_all.35.factor_ref = bf16[8,64,384]{2,1,0:T(8,128)(2,1)S(1)} all-to-all(bf16[8,64,384]{2,1,0:T(8,128)(2,1)S(1)} %broadcast_in_dim.8), channel_id=1, replica_groups=mesh['x'=4,'y'=8,'core'=2,'z'=8] {'z'}, dimensions={0} | all-to-all | bytes 786432 | tf_op jit(solution)/shard_map/all_to_all | solution.py:204
  41.6 0.6 left.1
  42.2 21.0 %all_to_all.36 = f32[64,1,128]{2,1,0:T(1,128)S(1)} all-to-all(f32[64,1,128]{2,1,0:T(1,128)S(1)} %bitcast.23), channel_id=1, replica_groups=mesh['x'=4,'y'=8,'core'=2,'z'=8] {'x','y','core'}, dimensions={0} | all-to-all | bytes 65536 | tf_op jit(solution)/shard_map/all_to_all | solution.py:235
  63.2 0.1 reduce_sum.18
  63.3 13.3 %all_to_all.37 = f32[64,1,128]{2,1,0:T(1,128)S(1)} all-to-all(f32[64,1,128]{2,1,0:T(1,128)S(1)} %broadcast_in_dim.9), channel_id=1, replica_groups=mesh['x'=4,'y'=8,'core'=2,'z'=8] {'x','y','core'}, dimensions={0} | all-to-all | bytes 65536 | tf_op jit(solution)/shard_map/all_to_all | solution.py:204
  76.6 0.9 gram.1
  77.5 3.4 %all-to-all-start.3 = ((f32[8,32,128]{2,1,0:T(8,128)}), f32[8,32,128]{2,1,0:T(8,128)S(1)}, u32[]{:S(2)}, u32[]{:S(2)}) async-start(f32[8,32,128]{2,1,0:T(8,128)} %gram.1), calls=%async_computation.3 | async-start | bytes 262144 | tf_op jit(solution)/shard_map/all_to_all | solution.py:241
  80.9 0.0 reduce-scatter.2.cloned.1.call-done
  80.9 0.0 copy-start.2
  80.9 0.0 copy-start.4
  80.9 1.9 %copy.8 = f32[384,128]{1,0:T(8,128)} copy(f32[384,128]{0,1:T(8,128)} %bitcast.25) | data formatting | bytes 393216 | tf_op jit(solution)/shard_map/transpose | solution.py:249
  82.8 5.8 %all-to-all-done.3.grams_ref = f32[8,32,128]{2,1,0:T(8,128)S(1)} async-done(((f32[8,32,128]{2,1,0:T(8,128)}), f32[8,32,128]{2,1,0:T(8,128)S(1)}, u32[]{:S(2)}, u32[]{:S(2)}) %all-to-all-start.3) | async-done | bytes 131104 | tf_op jit(solution)/shard_map/all_to_all | solution.py:241
  88.6 0.0 copy-start.5
  88.6 0.6 copy-done.5
  89.3 3.4 %all-to-all-start.4 = ((f32[4,96,128]{2,1,0:T(8,128)}), f32[4,96,128]{2,1,0:T(8,128)S(1)}, u32[]{:S(2)}, u32[]{:S(2)}) async-start(f32[4,96,128]{2,1,0:T(8,128)} %bitcast.24), calls=%async_computation.5 | async-start | bytes 393216 | tf_op jit(solution)/shard_map/all_to_all | solution.py:249
  92.6 0.0 copy-start.6
  92.7 0.9 copy-done.6
  93.6 3.5 %factor.1 = (f32[64,128]{1,0:T(8,128)}, bf16[128,64]{1,0:T(8,128)(2,1)S(1)}) custom-call(f32[8,32,128]{2,1,0:T(8,128)S(1)} %copy-done.6, f32[64,128]{1,0:T(8,128)S(1)} %bitcast.22), custom_call_target="tpu_custom_call" | custom-call | tf_op jit(solution)/shard_map/factor/pallas_call | solution.py:242
  97.0 0.8 all-to-all-done.4.slab_ref
  97.8 0.3 right.1
  98.1 11.1 %all_to_all.38 = f32[8,48,128]{2,1,0:T(8,128)S(1)} all-to-all(f32[8,48,128]{2,1,0:T(8,128)S(1)} %right.1), channel_id=1, replica_groups=mesh['x'=4,'y'=8,'core'=2,'z'=8] {'z'}, dimensions={0} | all-to-all | bytes 393216 | tf_op jit(solution)/shard_map/all_to_all | solution.py:253
  109.2 0.1 broadcast_in_dim.10
  109.2 14.3 %all_to_all.39.own_ref = bf16[32,48,128]{2,1,0:T(8,128)(2,1)} all-to-all(bf16[32,48,128]{2,1,0:T(8,128)(2,1)S(1)} %broadcast_in_dim.10), channel_id=1, replica_groups=mesh['x'=4,'y'=8,'core'=2,'z'=8] {'x','y'}, dimensions={0} | all-to-all | bytes 786432 | tf_op jit(solution)/shard_map/all_to_all | solution.py:204
  123.5 8.4 %collective-permute-start.1 = (bf16[32,48,128]{2,1,0:T(8,128)(2,1)}, bf16[32,48,128]{2,1,0:T(8,128)(2,1)}, u32[]{:S(2)}, u32[]{:S(2)}) collective-permute-start(bf16[32,48,128]{2,1,0:T(8,128)(2,1)} %all_to_all.39.own_ref), channel_id=1, source_target_pairs={{0,8},{8,0},{1,9},{9,1},{2,10},{10,2},{3,11},{11,3},{4,12},{12,4},... | collective-permute-start | bytes 1179656 | tf_op jit(solution)/shard_map/ppermute | solution.py:255
  131.9 0.1 pad_add_fusion.place_ref
  131.9 1.6 %collective-permute-done.1.other_ref = bf16[32,48,128]{2,1,0:T(8,128)(2,1)} collective-permute-done((bf16[32,48,128]{2,1,0:T(8,128)(2,1)}, bf16[32,48,128]{2,1,0:T(8,128)(2,1)}, u32[]{:S(2)}, u32[]{:S(2)}) %collective-permute-start.1) | collective-permute-done | bytes 393248 | tf_op jit(solution)/shard_map/ppermute | solution.py:255
  133.5 0.0 copy-done.2
  133.5 0.0 copy-done.4
  133.5 3.4 %decode.1 = (bf16[128,6144]{1,0:T(8,128)(2,1)}, bf16[64,768]{1,0:T(8,128)(2,1)}) custom-call(s32[2]{0:T(128)S(1)} %pad_add_fusion.place_ref, bf16[128,64]{1,0:T(8,128)(2,1)S(1)} %get-tuple-element.14.round_ref, bf16[32,48,128]{2,1,0:T(8,128)(2,1)} %all_to_all.39.own_ref, bf16[32,48,128]{2,1,0:T(8,128)(2,1)} %collective-permute-done.1.other_ref, ...), custom_call_target="tpu_custom_call" | custom-call | tf_op jit(solution)/shard_map/decode/pallas_call | solution.py:257
  (5 shorter events, 0.1 us)
Async XLA Ops:
  7.2 16.1 %copy-start = (bf16[768,64]{0,1:T(8,128)(2,1)S(1)}, bf16[768,64]{0,1:T(8,128)(2,1)}, u32[]{:S(2)}) copy-start(bf16[768,64]{0,1:T(8,128)(2,1)} %param.5) | copy-start | bytes 294916
  7.2 73.7 %reduce-scatter.2.cloned.1.call-start = ((), (), s32[]{:S(2)}) async-start(), calls=%async_computation.8 | async-start | bytes 1769472 | tf_op jit(solution)/shard_map/reduce_scatter | solution.py:228
  7.2 1.4 copy-start.1
  8.6 1.4 copy-start.3
  11.2 10.7 %collective-permute-start = (bf16[8,128,384]{2,1,0:T(8,128)(2,1)S(1)}, bf16[8,128,384]{2,1,0:T(8,128)(2,1)S(1)}, u32[]{:S(2)}, u32[]{:S(2)}) collective-permute-start(bf16[8,128,384]{2,1,0:T(8,128)(2,1)S(1)} %get-tuple-element.12), channel_id=1, source_target_pairs={{0,8},{8,0},{1,9},{9,1},{2,10},{10,2},{3,11},{11,3},{4,12},{12,4},... | collective-permute-start | bytes 2359304 | tf_op jit(solution)/shard_map/ppermute | solution.py:225
  77.5 11.1 %all-to-all-start.3 = ((f32[8,32,128]{2,1,0:T(8,128)}), f32[8,32,128]{2,1,0:T(8,128)S(1)}, u32[]{:S(2)}, u32[]{:S(2)}) async-start(f32[8,32,128]{2,1,0:T(8,128)} %gram.1), calls=%async_computation.3 | async-start | bytes 262144 | tf_op jit(solution)/shard_map/all_to_all | solution.py:241
  80.9 52.6 %copy-start.2 = (bf16[1,128,6144]{2,1,0:T(8,128)(2,1)S(1)}, bf16[1,128,6144]{2,1,0:T(8,128)(2,1)}, u32[]{:S(2)}) copy-start(bf16[1,128,6144]{2,1,0:T(8,128)(2,1)} %param.3) | copy-start | bytes 4718596
  80.9 52.6 %copy-start.4 = (bf16[1,128,6144]{2,1,0:T(8,128)(2,1)S(1)}, bf16[1,128,6144]{2,1,0:T(8,128)(2,1)}, u32[]{:S(2)}) copy-start(bf16[1,128,6144]{2,1,0:T(8,128)(2,1)} %param.4) | copy-start | bytes 4718596
  88.6 0.6 copy-start.5
  89.3 8.5 %all-to-all-start.4 = ((f32[4,96,128]{2,1,0:T(8,128)}), f32[4,96,128]{2,1,0:T(8,128)S(1)}, u32[]{:S(2)}, u32[]{:S(2)}) async-start(f32[4,96,128]{2,1,0:T(8,128)} %bitcast.24), calls=%async_computation.5 | async-start | bytes 393216 | tf_op jit(solution)/shard_map/all_to_all | solution.py:249
  92.6 0.9 copy-start.6
  123.5 10.0 %collective-permute-start.1 = (bf16[32,48,128]{2,1,0:T(8,128)(2,1)}, bf16[32,48,128]{2,1,0:T(8,128)(2,1)}, u32[]{:S(2)}, u32[]{:S(2)}) collective-permute-start(bf16[32,48,128]{2,1,0:T(8,128)(2,1)} %all_to_all.39.own_ref), channel_id=1, source_target_pairs={{0,8},{8,0},{1,9},{9,1},{2,10},{10,2},{3,11},{11,3},{4,12},{12,4},... | collective-permute-start | bytes 1179656 | tf_op jit(solution)/shard_map/ppermute | solution.py:255
Sparse Core Ops, SparseCore 0:
  23.3 37.7 reduce-scatter.1

commit v4 on v3

--- a/solution.py
+++ b/solution.py
@@ -13,30 +13,33 @@
 HBM = pl.BlockSpec(memory_space=pltpu.HBM)
 PLANE = ("x", "y")
 REPLICA = ("x", "y", "core")
-LIMIT = 16 * 2**20
-
-
-def merge_kernel(core_ref, grad_hbm, error_hbm, keep_ref, give_ref, grad, error, sems):
-    parts, _, half = keep_ref.shape
-    cols = 2 * half
+LIGHT = pl.CostEstimate(flops=0, bytes_accessed=0, transcendentals=0)
+FULL = 60
+WEIGHT = pl.CostEstimate(flops=10**11, bytes_accessed=2**21, transcendentals=0)
+
+
+def merge_kernel(core_ref, grad_hbm, error_hbm, out_hbm, grad, error, merged, sems):
+    parts, _, half = out_hbm.shape
     copies = []
     for i in range(parts):
-        at = pl.ds(i * cols, cols)
+        at = pl.ds(pl.multiple_of((2 * i + core_ref[0]) * half, half), half)
         copies.append(
             [
-                pltpu.make_async_copy(src.at[:, at], dst.at[:, at], sems.at[j, i])
+                pltpu.make_async_copy(src.at[:, at], dst.at[i], sems.at[j, i])
                 for j, (src, dst) in enumerate(((grad_hbm, grad), (error_hbm, error)))
             ]
         )
         for copy in copies[-1]:
             copy.start()
-    core = core_ref[0]
+    sent = []
     for i in range(parts):
         for copy in copies[i]:
             copy.wait()
-        for out, which in ((give_ref, 1 - core), (keep_ref, core)):
-            at = pl.ds(pl.multiple_of(i * cols + which * half, half), half)
-            out[i] = (grad[:, at].astype(F32) + error[:, at].astype(F32)).astype(BF16)
+        merged[i] = (grad[i].astype(F32) + error[i].astype(F32)).astype(BF16)
+        sent.append(pltpu.make_async_copy(merged.at[i], out_hbm.at[i], sems.at[2, i]))
+        sent[-1].start()
+    for copy in sent:
+        copy.wait()
 
 
 def pair_kernel(keep_ref, took_ref, out_ref):
@@ -137,10 +140,21 @@
     round_ref[...] = factor_ref[...].T.astype(BF16)
 
 
-def right_kernel(slab_ref, round_ref, out_ref):
-    slab = slab_ref[0]
-    for i in range(1, slab_ref.shape[0]):
-        slab = slab + slab_ref[i]
+def fan_kernel(place_ref, slab_ref, *out_refs):
+    turned = slab_ref[...].T
+    fold = turned.shape[0] // len(out_refs)
+    for i in range(len(out_refs)):
+        for j, out_ref in enumerate(out_refs):
+            @pl.when(i == place_ref[0] ^ j)
+            def _():
+                out_ref[...] = turned[fold * i : fold * (i + 1)]
+
+
+def right_kernel(round_ref, own_ref, *rest):
+    *others, out_ref = rest
+    slab = own_ref[...]
+    for other in others:
+        slab = slab + other[...]
     term = jnp.dot(
         slab, round_ref[...].astype(F32),
         precision=lax.Precision.HIGHEST, preferred_element_type=F32,
@@ -150,52 +164,53 @@
         out_ref[i] = packed
 
 
-def decode_kernel(place_ref, round_ref, own_ref, other_ref, grad, error, out_hbm, next_ref, out, sems):
-    planes, fold, lanes = own_ref.shape
-    rank = lanes // 2
-    parts = grad.shape[1] // next_ref.shape[1]
-    inner = planes // parts
-    half = 2 * fold * inner
-    cols = 2 * half
-    core, z = place_ref[0], place_ref[1]
+def decode_kernel(place_ref, round_ref, factor_ref, grad, error, *rest):
+    *before, out_hbm, next_ref, out, sems = rest
+    planes, fold, lanes = factor_ref.shape
+    rank, half = lanes // 2, out.shape[-1]
+    inner = half // (2 * fold)
+    parts = planes // inner
+    which = place_ref[0]
     rounded = round_ref[...]
 
-    def factor(ref, part):
+    def factor(part):
         pieces = []
         for x in range(inner):
-            piece = ref[x * parts + part]
+            piece = factor_ref[x * parts + part]
             pieces += [piece[:, :rank], piece[:, rank:]]
         return jnp.concatenate(pieces, axis=0)
 
     sent = []
     for i in range(parts):
-        for ref, which in ((own_ref, core), (other_ref, 1 - core)):
-            decoded = lax.dot_general(
-                rounded, factor(ref, i), (((1,), (1,)), ((), ())),
-                preferred_element_type=F32,
-            )
-            at = pl.ds(pl.multiple_of(i * cols + which * half, half), half)
-            out[:, at] = (
-                grad[:, at].astype(F32) + error[:, at].astype(F32) - decoded
-            ).astype(BF16)
-        at = pl.ds(i * cols, cols)
-        sent.append(pltpu.make_async_copy(out.at[:, at], out_hbm.at[:, at], sems.at[i]))
+        decoded = lax.dot_general(
+            rounded, factor(i), (((1,), (1,)), ((), ())), preferred_element_type=F32
+        )
+        at = pl.ds(pl.multiple_of((2 * i + which) * half, half), half)
+        out[i] = (
+            grad[:, at].astype(F32) + error[:, at].astype(F32) - decoded
+        ).astype(BF16)
+        sent.append(pltpu.make_async_copy(out.at[i], out_hbm.at[:, at], sems.at[i]))
         sent[-1].start()
-    for ref, which in ((own_ref, core), (other_ref, 1 - core)):
-        at = pl.ds(pl.multiple_of(which * half, half), half)
-        next_ref[:, at] = factor(ref, z).astype(F32).T.astype(BF16)
+    turned = factor(place_ref[1]).astype(F32).T.astype(BF16)
+    if before:
+        for at, part in ((which, turned), (1 - which, before[1][...])):
+            next_ref[:, pl.ds(pl.multiple_of(at * half, half), half)] = part
+    else:
+        next_ref[...] = turned
     for copy in sent:
         copy.wait()
 
 
-def call(kernel, name, out_shape, in_specs, out_specs=VMEM, scratch_shapes=()):
+def call(kernel, name, out_shape, in_specs, out_specs=VMEM, scratch_shapes=(), limit=4, cost=None, aliases=None):
     return pl.pallas_call(
         kernel,
         in_specs=in_specs,
         out_specs=out_specs,
         out_shape=out_shape,
         scratch_shapes=scratch_shapes,
-        compiler_params=pltpu.CompilerParams(vmem_limit_bytes=LIMIT),
+        cost_estimate=cost,
+        input_output_aliases=aliases or {},
+        compiler_params=pltpu.CompilerParams(vmem_limit_bytes=limit * 2**20),
         name=name,
     )
 
@@ -218,18 +233,22 @@
 
     pieces = array((along, height, half), BF16)
     staged = pltpu.VMEM((height, width), BF16)
-    keep, give = call(
-        merge_kernel, "merge", [pieces, pieces], [SMEM, HBM, HBM], [VMEM, VMEM],
-        [staged, staged, pltpu.SemaphoreType.DMA((2, along))],
-    )(core.reshape(1), grad, error)
+
+    def merge(which, name, cost):
+        return call(
+            merge_kernel, name, pieces, [SMEM, HBM, HBM], HBM,
+            [pltpu.VMEM(pieces.shape, BF16)] * 3 + [pltpu.SemaphoreType.DMA((3, along))],
+            limit=FULL, cost=cost,
+        )(which.reshape(1), grad, error)
+
+    give, keep = merge(1 - core, "give", LIGHT), merge(core, "keep", WEIGHT)
     took = lax.ppermute(give, "core", swap)
-    pair = call(pair_kernel, "pair", array(pieces.shape, F32), [VMEM, VMEM])(keep, took)
-    q_in, pair = lax.optimization_barrier((q_in, pair))
+    pair = call(pair_kernel, "pair", array(pieces.shape, F32), [VMEM, VMEM], limit=8, cost=LIGHT)(keep, took)
     slab = lax.psum_scatter(pair, "y", scatter_dimension=0, tiled=True)[0]
 
     q_mine = lax.dynamic_slice_in_dim(q_in.T, core * half, half, 1)
     q_all = spread(q_mine, "z", shards)
-    left = call(left_kernel, "left", array((rank, height), F32), [VMEM] * 3)(
+    left = call(left_kernel, "left", array((rank, height), F32), [VMEM] * 3, limit=8, cost=WEIGHT)(
         q_all, keep, took
     )
     left_row = lax.all_to_all(left.reshape(replicas, -1, height), REPLICA, 0, 0).sum(0)
@@ -246,20 +265,31 @@
     )(grams, left_sum)
 
     fold = half // across
-    slab = lax.all_to_all(slab.T.reshape(across, fold, height), "x", 0, 0)
+    own, *give = call(
+        fan_kernel, "fan", [array((fold, height), F32)] * across, [SMEM, VMEM], [VMEM] * across
+    )(lax.axis_index("x").reshape(1), slab)
+    others = [
+        lax.ppermute(part, "x", [(i, i ^ j) for i in range(across)])
+        for j, part in enumerate(give, 1)
+    ]
     term = call(
-        right_kernel, "right", array((shards, fold // 2, 2 * rank), F32), [VMEM, VMEM]
-    )(slab, p_round)
+        right_kernel, "right", array((shards, fold // 2, 2 * rank), F32), [VMEM] * (1 + across)
+    )(p_round, own, *others)
     q_mine = (lax.all_to_all(term, "z", 0, 0).sum(0) / replicas).astype(BF16)
     q_own = spread(q_mine, PLANE, planes)
     q_other = lax.ppermute(q_own, "core", swap)
 
-    new_error, q_next = call(
-        decode_kernel, "decode",
-        [array((height, width), BF16), array((rank, cols), BF16)],
-        [SMEM] + [VMEM] * 5, [HBM, VMEM],
-        [staged, pltpu.SemaphoreType.DMA((along,))],
-    )(jnp.stack([core, z]), p_round, q_own, q_other, grad, error)
+
+    def decode(which, name, factor, *before):
+        return call(
+            decode_kernel, name,
+            [array((height, width), BF16), array((rank, cols if before else half), BF16)],
+            [SMEM] + [VMEM] * 4 + ([HBM, VMEM] if before else []), [HBM, VMEM],
+            [pltpu.VMEM(pieces.shape, BF16), pltpu.SemaphoreType.DMA((along,))],
+            limit=12, aliases={5: 0} if before else None,
+        )(jnp.stack([which, z]), p_round, factor, grad, error, *before)
+
+    new_error, q_next = decode(1 - core, "other", q_other, *decode(core, "own", q_own))
     return new_error[None], p_factor.T, q_next.T
 
 

time: 144 us -> 142 us (0.986)
  blocking collectives: 77.9 us -> 64.2 us
  starting transfers between devices: 23.9 us -> 36.4 us
  Pallas kernels: 11.1 us -> 18.1 us
  waiting for transfers between devices: 10.1 us -> 4.15 us
  local copies, waits for them, and re-layouts: 6.38 us -> 3.81 us
    all_to_all x3 -> x2, blocking collectives: 45.9 us -> 28.5 us  [spread(): lax.all_to_all(jnp.broadcast_to(block[None], (count, *block.shape)), axes...]
    ppermute x0 -> x3, starting transfers between devices: none -> 9.57 us  [local(): lax.ppermute(part, 'x', [(i, i ^ j) for i in range(across)])]
    all_to_all x1, starting transfers between devices: 3.37 us -> 10.9 us  [spread(): lax.all_to_all(jnp.broadcast_to(block[None], (count, *block.shape)), axes...]
    pallas_call x4 -> x7, Pallas kernels: 6.43 us -> 12.6 us  [the longest x2 5.14 us: decode(): call(decode_kernel, name, [array((height, width), BF16), array((rank, col...]
    ppermute x1, starting transfers between devices: 8.79 us -> 2.86 us  [local(): took = lax.ppermute(give, 'core', swap)]
    all_to_all x1, waiting for transfers between devices: 5.81 us -> 0.01 us  [local(): grams = lax.all_to_all(gram, 'z', 0, 0)]
    all_to_all x1, blocking collectives: 11.1 us -> 15 us  [local(): q_mine = (lax.all_to_all(term, 'z', 0, 0).sum(0) / replicas).astype(BF16)]
    all_to_all x1, waiting for transfers between devices: 0.75 us -> 4.1 us  [spread(): lax.all_to_all(jnp.broadcast_to(block[None], (count, *block.shape)), axes...]
  transfers between devices with their start and end apart: 5 -> 8, of which waited for: 4 -> 1; matrix products, arithmetic and copies ran while one was open for 1% -> 0% of each run, Pallas kernels for 3% -> 10%
where the time goes in v4:
time: 142 us; the launch traced here: 141 us
  blocking collectives  64.2 us (45%)
  starting transfers between devices  36.4 us (26%)
  Pallas kernels  18.1 us (13%)
  between operations  14.3 us (10%)
  waiting for transfers between devices  4.15 us (3%)
  local copies, waits for them, and re-layouts  3.81 us (3%)
    all_to_all x2, blocking collectives, spread(): lax.all_to_all(jnp.broadcast_to(block[None], (count, *block.shape)), axes...  28.5 us
    all_to_all x1, blocking collectives, local(): lax.all_to_all(left.reshape(replicas, -1, height), REPLICA, 0, 0).sum(0)  20.7 us
    all_to_all x1, blocking collectives, local(): q_mine = (lax.all_to_all(term, 'z', 0, 0).sum(0) / replicas).astype(BF16)  15 us
    all_to_all x1, starting transfers between devices, spread(): lax.all_to_all(jnp.broadcast_to(block[None], (count, *block.shape)), axes...  10.9 us
    ppermute x1, starting transfers between devices, local(): q_other = lax.ppermute(q_own, 'core', swap)  9.7 us
    ppermute x3, starting transfers between devices, local(): lax.ppermute(part, 'x', [(i, i ^ j) for i in range(across)])  9.57 us
    pallas_call x2, Pallas kernels, decode(): call(decode_kernel, name, [array((height, width), BF16), array((rank, col...  5.14 us
    pallas_call x2, Pallas kernels, merge(): call(merge_kernel, name, pieces, [SMEM, HBM, HBM], HBM, [pltpu.VMEM(piece...  4.7 us
  transfers between devices with their start and end apart: 8, of which 1 were waited for; matrix products, arithmetic and copies ran while one was open for 0% of the time, Pallas kernels for 10%

profile of v4, /device:TPU:1, one launch (start us, length us, event | category | flops | bytes accessed | tf_op | source)
XLA Modules:
  0.0 141.1 jit_solution(18125596998429099194)
XLA Ops:
  7.2 0.0 copy-start
  7.2 0.9 copy-done
  8.1 0.8 broadcast_in_dim.8
  8.9 10.9 %all-to-all-start = ((bf16[8,64,384]{2,1,0:T(8,128)(2,1)}), bf16[8,64,384]{2,1,0:T(8,128)(2,1)S(1)}, u32[]{:S(2)}, u32[]{:S(2)}) async-start(bf16[8,64,384]{2,1,0:T(8,128)(2,1)} %broadcast_in_dim.8), calls=%async_computation | async-start | bytes 786432 | tf_op jit(solution)/shard_map/all_to_all | solution.py:219
  19.7 0.0 reduce-scatter.2.cloned.1.call-start
  19.8 2.3 %give.1 = bf16[8,128,384]{2,1,0:T(8,128)(2,1)} custom-call(s32[1]{0:T(128)} %bitcast.core_ref, bf16[128,6144]{1,0:T(8,128)(2,1)} %bitcast.16, bf16[128,6144]{1,0:T(8,128)(2,1)} %bitcast.20), custom_call_target="tpu_custom_call" | custom-call | tf_op jit(solution)/shard_map/give/pallas_call | solution.py:238
  22.1 2.9 %collective-permute-start = (bf16[8,128,384]{2,1,0:T(8,128)(2,1)}, bf16[8,128,384]{2,1,0:T(8,128)(2,1)S(1)}, u32[]{:S(2)}, u32[]{:S(2)}) collective-permute-start(bf16[8,128,384]{2,1,0:T(8,128)(2,1)} %give.1), channel_id=1, source_target_pairs={{0,8},{8,0},{1,9},{9,1},{2,10},{10,2},{3,11},{11,3},{4,12},{12,4},... | collective-permute-start | bytes 2359304 | tf_op jit(solution)/shard_map/ppermute | solution.py:245
  25.0 2.4 %keep.1.keep_ref = bf16[8,128,384]{2,1,0:T(8,128)(2,1)} custom-call(s32[1]{0:T(128)} %bitcast.3.core_ref, bf16[128,6144]{1,0:T(8,128)(2,1)} %bitcast.17, bf16[128,6144]{1,0:T(8,128)(2,1)} %bitcast.21), custom_call_target="tpu_custom_call" | custom-call | flops 99999997952 | bytes 2097152 | tf_op jit(solution)/shard_map/keep/pallas_call | solution.py:238
  27.4 0.0 collective-permute-done.took_ref
  27.4 0.0 copy-start.3
  27.4 1.1 copy-done.3
  28.5 1.3 pair.1
  29.8 0.0 copy-start.4
  29.8 0.0 reduce-scatter.2.cloned.1.call-update
  29.8 4.1 %all-to-all-done.factor_ref = bf16[8,64,384]{2,1,0:T(8,128)(2,1)S(1)} async-done(((bf16[8,64,384]{2,1,0:T(8,128)(2,1)}), bf16[8,64,384]{2,1,0:T(8,128)(2,1)S(1)}, u32[]{:S(2)}, u32[]{:S(2)}) %all-to-all-start) | async-done | bytes 393248 | tf_op jit(solution)/shard_map/all_to_all | solution.py:219
  33.9 0.0 copy-done.4
  33.9 0.6 left.1
  34.5 20.7 %all_to_all.30 = f32[64,1,128]{2,1,0:T(1,128)S(1)} all-to-all(f32[64,1,128]{2,1,0:T(1,128)S(1)} %bitcast.27), channel_id=1, replica_groups=mesh['x'=4,'y'=8,'core'=2,'z'=8] {'x','y','core'}, dimensions={0} | all-to-all | bytes 65536 | tf_op jit(solution)/shard_map/all_to_all | solution.py:254
  55.3 0.1 reduce_sum.18
  55.4 0.0 copy-start.1
  55.4 0.0 copy-start.2
  55.4 13.6 %all_to_all.31 = f32[64,1,128]{2,1,0:T(1,128)S(1)} all-to-all(f32[64,1,128]{2,1,0:T(1,128)S(1)} %broadcast_in_dim.9), channel_id=1, replica_groups=mesh['x'=4,'y'=8,'core'=2,'z'=8] {'x','y','core'}, dimensions={0} | all-to-all | bytes 65536 | tf_op jit(solution)/shard_map/all_to_all | solution.py:219
  69.0 0.9 gram.1
  69.9 3.4 %all-to-all-start.3 = ((f32[8,32,128]{2,1,0:T(8,128)}), f32[8,32,128]{2,1,0:T(8,128)S(1)}, u32[]{:S(2)}, u32[]{:S(2)}) async-start(f32[8,32,128]{2,1,0:T(8,128)} %gram.1), calls=%async_computation.3 | async-start | bytes 262144 | tf_op jit(solution)/shard_map/all_to_all | solution.py:260
  73.3 0.0 reduce-scatter.2.cloned.1.call-done
  73.3 0.0 copy-start.5
  73.3 0.9 copy-done.5
  74.2 0.9 fan.1
  75.1 2.3 %collective-permute-start.1 = (f32[96,128]{1,0:T(8,128)}, f32[96,128]{1,0:T(8,128)S(1)}, u32[]{:S(2)}, u32[]{:S(2)}) collective-permute-start(f32[96,128]{1,0:T(8,128)} %get-tuple-element.15), channel_id=1, source_target_pairs={{0,128},{128,0},{256,384},{384,256},{1,129},{129,1},{257,385},{385... | collective-permute-start | bytes 147464 | tf_op jit(solution)/shard_map/ppermute | solution.py:272
  77.4 3.5 %collective-permute-start.2 = (f32[96,128]{1,0:T(8,128)}, f32[96,128]{1,0:T(8,128)}, u32[]{:S(2)}, u32[]{:S(2)}) collective-permute-start(f32[96,128]{1,0:T(8,128)} %get-tuple-element.16), channel_id=1, source_target_pairs={{0,256},{128,384},{256,0},{384,128},{1,257},{129,385},{257,1},{385... | collective-permute-start | bytes 147464 | tf_op jit(solution)/shard_map/ppermute | solution.py:272
  80.9 3.8 %collective-permute-start.3 = (f32[96,128]{1,0:T(8,128)}, f32[96,128]{1,0:T(8,128)}, u32[]{:S(2)}, u32[]{:S(2)}) collective-permute-start(f32[96,128]{1,0:T(8,128)} %get-tuple-element.17), channel_id=1, source_target_pairs={{0,384},{128,256},{256,128},{384,0},{1,385},{129,257},{257,129},{3... | collective-permute-start | bytes 147464 | tf_op jit(solution)/shard_map/ppermute | solution.py:272
  84.7 0.0 all-to-all-done.3.grams_ref
  84.7 3.5 %factor.1 = (f32[64,128]{1,0:T(8,128)}, bf16[128,64]{1,0:T(8,128)(2,1)S(1)}) custom-call(f32[8,32,128]{2,1,0:T(8,128)S(1)} %all-to-all-done.3.grams_ref, f32[64,128]{1,0:T(8,128)S(1)} %bitcast.25), custom_call_target="tpu_custom_call" | custom-call | tf_op jit(solution)/shard_map/factor/pallas_call | solution.py:261
  88.2 0.0 collective-permute-done.1.rest_0_
  88.2 0.0 collective-permute-done.2.rest_1_
  88.2 0.0 collective-permute-done.3.rest_2_
  88.2 1.1 right.1
  89.3 15.0 %all_to_all.32 = f32[8,48,128]{2,1,0:T(8,128)S(1)} all-to-all(f32[8,48,128]{2,1,0:T(8,128)S(1)} %right.1), channel_id=1, replica_groups=mesh['x'=4,'y'=8,'core'=2,'z'=8] {'z'}, dimensions={0} | all-to-all | bytes 393216 | tf_op jit(solution)/shard_map/all_to_all | solution.py:278
  104.3 0.1 broadcast_in_dim.10
  104.4 14.9 %all_to_all.33.factor_ref = bf16[32,48,128]{2,1,0:T(8,128)(2,1)} all-to-all(bf16[32,48,128]{2,1,0:T(8,128)(2,1)S(1)} %broadcast_in_dim.10), channel_id=1, replica_groups=mesh['x'=4,'y'=8,'core'=2,'z'=8] {'x','y'}, dimensions={0} | all-to-all | bytes 786432 | tf_op jit(solution)/shard_map/all_to_all | solution.py:219
  119.2 9.7 %collective-permute-start.4 = (bf16[32,48,128]{2,1,0:T(8,128)(2,1)}, bf16[32,48,128]{2,1,0:T(8,128)(2,1)}, u32[]{:S(2)}, u32[]{:S(2)}) collective-permute-start(bf16[32,48,128]{2,1,0:T(8,128)(2,1)} %all_to_all.33.factor_ref), channel_id=1, source_target_pairs={{0,8},{8,0},{1,9},{9,1},{2,10},{10,2},{3,11},{11,3},{4,12},{12,4},... | collective-permute-start | bytes 1179656 | tf_op jit(solution)/shard_map/ppermute | solution.py:280
  128.9 0.1 pad_add_fusion.place_ref
  129.0 0.1 pad_add_fusion.1.place_ref
  129.1 0.0 copy-done.1
  129.1 0.0 copy-done.2
  129.1 2.2 %own.1 = (bf16[128,6144]{1,0:T(8,128)(2,1)}, bf16[64,384]{1,0:T(8,128)(2,1)S(1)}) custom-call(s32[2]{0:T(128)S(1)} %pad_add_fusion.1.place_ref, bf16[128,64]{1,0:T(8,128)(2,1)S(1)} %get-tuple-element.13.round_ref, bf16[32,48,128]{2,1,0:T(8,128)(2,1)} %all_to_all.33.factor_ref, bf16[128,6144]{1,0:T(8,128)(2,1)S(1)} %bitcast.18, bf16[128,6144]{1,0:T(8,128)(2,1)S(1)} %bitcast.22), custom_call_target="tpu_custom_call" | custom-call | tf_op jit(solution)/shard_map/own/pallas_call | solution.py:284
  131.4 0.0 collective-permute-done.4.factor_ref
  131.4 2.9 %other.1 = (bf16[128,6144]{1,0:T(8,128)(2,1)}, bf16[64,768]{1,0:T(8,128)(2,1)}) custom-call(s32[2]{0:T(128)S(1)} %pad_add_fusion.place_ref, bf16[128,64]{1,0:T(8,128)(2,1)S(1)} %get-tuple-element.13.round_ref, bf16[32,48,128]{2,1,0:T(8,128)(2,1)} %collective-permute-done.4.factor_ref, ...), custom_call_target="tpu_custom_call", output_to_operand_aliasing={{0}: (5, {})} | custom-call | tf_op jit(solution)/shard_map/other/pallas_call | solution.py:284
  (4 shorter events, 0.0 us)
Async XLA Ops:
  7.2 0.9 copy-start
  8.9 25.1 %all-to-all-start = ((bf16[8,64,384]{2,1,0:T(8,128)(2,1)}), bf16[8,64,384]{2,1,0:T(8,128)(2,1)S(1)}, u32[]{:S(2)}, u32[]{:S(2)}) async-start(bf16[8,64,384]{2,1,0:T(8,128)(2,1)} %broadcast_in_dim.8), calls=%async_computation | async-start | bytes 786432 | tf_op jit(solution)/shard_map/all_to_all | solution.py:219
  19.7 53.6 %reduce-scatter.2.cloned.1.call-start = ((), (), s32[]{:S(2)}) async-start(), calls=%async_computation.7 | async-start | bytes 1769472 | tf_op jit(solution)/shard_map/reduce_scatter | solution.py:247
  22.1 5.2 %collective-permute-start = (bf16[8,128,384]{2,1,0:T(8,128)(2,1)}, bf16[8,128,384]{2,1,0:T(8,128)(2,1)S(1)}, u32[]{:S(2)}, u32[]{:S(2)}) collective-permute-start(bf16[8,128,384]{2,1,0:T(8,128)(2,1)} %give.1), channel_id=1, source_target_pairs={{0,8},{8,0},{1,9},{9,1},{2,10},{10,2},{3,11},{11,3},{4,12},{12,4},... | collective-permute-start | bytes 2359304 | tf_op jit(solution)/shard_map/ppermute | solution.py:245
  27.4 1.1 copy-start.3
  29.8 4.1 %copy-start.4 = (bf16[8,128,384]{2,1,0:T(8,128)(2,1)S(1)}, bf16[8,128,384]{2,1,0:T(8,128)(2,1)}, u32[]{:S(2)}) copy-start(bf16[8,128,384]{2,1,0:T(8,128)(2,1)} %keep.1.keep_ref) | copy-start | bytes 2359300
  55.4 73.7 %copy-start.1 = (bf16[1,128,6144]{2,1,0:T(8,128)(2,1)S(1)}, bf16[1,128,6144]{2,1,0:T(8,128)(2,1)}, u32[]{:S(2)}) copy-start(bf16[1,128,6144]{2,1,0:T(8,128)(2,1)} %param.3) | copy-start | bytes 4718596
  55.4 73.7 %copy-start.2 = (bf16[1,128,6144]{2,1,0:T(8,128)(2,1)S(1)}, bf16[1,128,6144]{2,1,0:T(8,128)(2,1)}, u32[]{:S(2)}) copy-start(bf16[1,128,6144]{2,1,0:T(8,128)(2,1)} %param.4) | copy-start | bytes 4718596
  69.9 14.8 %all-to-all-start.3 = ((f32[8,32,128]{2,1,0:T(8,128)}), f32[8,32,128]{2,1,0:T(8,128)S(1)}, u32[]{:S(2)}, u32[]{:S(2)}) async-start(f32[8,32,128]{2,1,0:T(8,128)} %gram.1), calls=%async_computation.3 | async-start | bytes 262144 | tf_op jit(solution)/shard_map/all_to_all | solution.py:260
  73.3 0.9 copy-start.5
  75.1 13.1 %collective-permute-start.1 = (f32[96,128]{1,0:T(8,128)}, f32[96,128]{1,0:T(8,128)S(1)}, u32[]{:S(2)}, u32[]{:S(2)}) collective-permute-start(f32[96,128]{1,0:T(8,128)} %get-tuple-element.15), channel_id=1, source_target_pairs={{0,128},{128,0},{256,384},{384,256},{1,129},{129,1},{257,385},{385... | collective-permute-start | bytes 147464 | tf_op jit(solution)/shard_map/ppermute | solution.py:272
  77.4 10.8 %collective-permute-start.2 = (f32[96,128]{1,0:T(8,128)}, f32[96,128]{1,0:T(8,128)}, u32[]{:S(2)}, u32[]{:S(2)}) collective-permute-start(f32[96,128]{1,0:T(8,128)} %get-tuple-element.16), channel_id=1, source_target_pairs={{0,256},{128,384},{256,0},{384,128},{1,257},{129,385},{257,1},{385... | collective-permute-start | bytes 147464 | tf_op jit(solution)/shard_map/ppermute | solution.py:272
  80.9 7.3 %collective-permute-start.3 = (f32[96,128]{1,0:T(8,128)}, f32[96,128]{1,0:T(8,128)}, u32[]{:S(2)}, u32[]{:S(2)}) collective-permute-start(f32[96,128]{1,0:T(8,128)} %get-tuple-element.17), channel_id=1, source_target_pairs={{0,384},{128,256},{256,128},{384,0},{1,385},{129,257},{257,129},{3... | collective-permute-start | bytes 147464 | tf_op jit(solution)/shard_map/ppermute | solution.py:272
  119.2 12.1 %collective-permute-start.4 = (bf16[32,48,128]{2,1,0:T(8,128)(2,1)}, bf16[32,48,128]{2,1,0:T(8,128)(2,1)}, u32[]{:S(2)}, u32[]{:S(2)}) collective-permute-start(bf16[32,48,128]{2,1,0:T(8,128)(2,1)} %all_to_all.33.factor_ref), channel_id=1, source_target_pairs={{0,8},{8,0},{1,9},{9,1},{2,10},{10,2},{3,11},{11,3},{4,12},{12,4},... | collective-permute-start | bytes 1179656 | tf_op jit(solution)/shard_map/ppermute | solution.py:280
Sparse Core Ops, SparseCore 0:
  29.9 39.7 reduce-scatter.1

commit v5 on v4

--- a/solution.py
+++ b/solution.py
@@ -14,37 +14,43 @@
 PLANE = ("x", "y")
 REPLICA = ("x", "y", "core")
 LIGHT = pl.CostEstimate(flops=0, bytes_accessed=0, transcendentals=0)
-FULL = 60
 WEIGHT = pl.CostEstimate(flops=10**11, bytes_accessed=2**21, transcendentals=0)
 
 
-def merge_kernel(core_ref, grad_hbm, error_hbm, out_hbm, grad, error, merged, sems):
-    parts, _, half = out_hbm.shape
-    copies = []
+def merge_kernel(core_ref, grad, error, out_ref):
+    parts, _, half = out_ref.shape
     for i in range(parts):
         at = pl.ds(pl.multiple_of((2 * i + core_ref[0]) * half, half), half)
-        copies.append(
-            [
-                pltpu.make_async_copy(src.at[:, at], dst.at[i], sems.at[j, i])
-                for j, (src, dst) in enumerate(((grad_hbm, grad), (error_hbm, error)))
-            ]
-        )
-        for copy in copies[-1]:
-            copy.start()
-    sent = []
-    for i in range(parts):
-        for copy in copies[i]:
-            copy.wait()
-        merged[i] = (grad[i].astype(F32) + error[i].astype(F32)).astype(BF16)
-        sent.append(pltpu.make_async_copy(merged.at[i], out_hbm.at[i], sems.at[2, i]))
-        sent[-1].start()
-    for copy in sent:
-        copy.wait()
-
-
-def pair_kernel(keep_ref, took_ref, out_ref):
-    for i in range(out_ref.shape[0]):
-        out_ref[i] = keep_ref[i].astype(F32) + took_ref[i].astype(F32)
+        out_ref[i] = (grad[:, at].astype(F32) + error[:, at].astype(F32)).astype(BF16)
+
+
+def halve_kernel(bit_ref, hold_ref, took_ref, hold_out, give_out):
+    many = hold_out.shape[0]
+    for out, bit in ((give_out, 1 - bit_ref[0]), (hold_out, bit_ref[0])):
+        for j in range(many):
+            i = bit * many + j
+            out[j] = hold_ref[i].astype(F32) + took_ref[i].astype(F32)
+
+
+def turn_kernel(bit_ref, hold_ref, took_ref, hold_out, give_out):
+    turned = (hold_ref[0] + took_ref[0]).T
+    many = turned.shape[0] // 2
+    low, high = turned[:many], turned[many:]
+
+    @pl.when(bit_ref[0] == 0)
+    def _():
+        hold_out[0], give_out[0] = low, high
+
+    @pl.when(bit_ref[0] != 0)
+    def _():
+        hold_out[0], give_out[0] = high, low
+
+
+def split_kernel(bit_ref, hold_ref, took_ref, hold_out, give_out):
+    many = hold_out.shape[1]
+    for out, bit in ((give_out, 1 - bit_ref[0]), (hold_out, bit_ref[0])):
+        at = pl.ds(pl.multiple_of(bit * many, many), many)
+        out[0] = hold_ref[0, at, :] + took_ref[0, at, :]
 
 
 def left_kernel(factor_ref, keep_ref, took_ref, out_ref):
@@ -140,23 +146,9 @@
     round_ref[...] = factor_ref[...].T.astype(BF16)
 
 
-def fan_kernel(place_ref, slab_ref, *out_refs):
-    turned = slab_ref[...].T
-    fold = turned.shape[0] // len(out_refs)
-    for i in range(len(out_refs)):
-        for j, out_ref in enumerate(out_refs):
-            @pl.when(i == place_ref[0] ^ j)
-            def _():
-                out_ref[...] = turned[fold * i : fold * (i + 1)]
-
-
-def right_kernel(round_ref, own_ref, *rest):
-    *others, out_ref = rest
-    slab = own_ref[...]
-    for other in others:
-        slab = slab + other[...]
+def right_kernel(round_ref, hold_ref, took_ref, out_ref):
     term = jnp.dot(
-        slab, round_ref[...].astype(F32),
+        hold_ref[0] + took_ref[0], round_ref[...].astype(F32),
         precision=lax.Precision.HIGHEST, preferred_element_type=F32,
     )
     packed = jnp.concatenate(jnp.split(term, 2, axis=0), axis=1)
@@ -176,7 +168,7 @@
     def factor(part):
         pieces = []
         for x in range(inner):
-            piece = factor_ref[x * parts + part]
+            piece = factor_ref[owner(part, x)]
             pieces += [piece[:, :rank], piece[:, rank:]]
         return jnp.concatenate(pieces, axis=0)
 
@@ -201,6 +193,12 @@
         copy.wait()
 
 
+def owner(block, quarter):
+    x = block // 4 + 2 * (block // 2 % 2)
+    y = block % 2 + 2 * (quarter // 2) + 4 * (quarter % 2)
+    return 8 * x + y
+
+
 def call(kernel, name, out_shape, in_specs, out_specs=VMEM, scratch_shapes=(), limit=4, cost=None, aliases=None):
     return pl.pallas_call(
         kernel,
@@ -220,8 +218,7 @@
 
 
 def local(sizes, grad, error, q_in):
-    across, along, shards, cores = sizes["x"], sizes["y"], sizes["z"], sizes["core"]
-    planes = across * along
+    planes, shards, cores = sizes["x"] * sizes["y"], sizes["z"], sizes["core"]
     replicas = planes * cores
     grad, error = grad[0], error[0]
     height, width = grad.shape
@@ -231,50 +228,76 @@
     swap = [(0, 1), (1, 0)]
     array = jax.ShapeDtypeStruct
 
-    pieces = array((along, height, half), BF16)
-    staged = pltpu.VMEM((height, width), BF16)
+    blocks = width // cols
+    pieces = array((blocks, height, half), BF16)
 
     def merge(which, name, cost):
         return call(
-            merge_kernel, name, pieces, [SMEM, HBM, HBM], HBM,
-            [pltpu.VMEM(pieces.shape, BF16)] * 3 + [pltpu.SemaphoreType.DMA((3, along))],
-            limit=FULL, cost=cost,
+            merge_kernel, name, pieces, [SMEM, VMEM, VMEM], limit=12, cost=cost
         )(which.reshape(1), grad, error)
 
     give, keep = merge(1 - core, "give", LIGHT), merge(core, "keep", WEIGHT)
     took = lax.ppermute(give, "core", swap)
-    pair = call(pair_kernel, "pair", array(pieces.shape, F32), [VMEM, VMEM], limit=8, cost=LIGHT)(keep, took)
-    slab = lax.psum_scatter(pair, "y", scatter_dimension=0, tiled=True)[0]
+
+    def halve(kernel, name, axis, bit, hold, took, shape):
+        place = (lax.axis_index(axis) // bit % 2).reshape(1)
+        out = array(shape, F32)
+        return call(kernel, name, [out, out], [SMEM, VMEM, VMEM], [VMEM, VMEM], limit=8)(
+            place, hold, took
+        )
+
+    def trade(give, axis, bit):
+        return lax.ppermute(give, axis, [(i, i ^ bit) for i in range(sizes[axis])])
+
+    def after(first, *then):
+        return lax.optimization_barrier((first, *then))
+
+    hold, give = halve(
+        halve_kernel, "pair", "x", 1, keep, took, (blocks // 2, height, half)
+    )
+    took_a = trade(give, "x", 1)
 
     q_mine = lax.dynamic_slice_in_dim(q_in.T, core * half, half, 1)
     q_all = spread(q_mine, "z", shards)
+    q_all, hold = after(q_all, hold)
     left = call(left_kernel, "left", array((rank, height), F32), [VMEM] * 3, limit=8, cost=WEIGHT)(
         q_all, keep, took
     )
     left_row = lax.all_to_all(left.reshape(replicas, -1, height), REPLICA, 0, 0).sum(0)
+    hold, give = halve(
+        halve_kernel, "halve_x", "x", 2, hold, took_a, (blocks // 4, height, half)
+    )
+    left_row, hold, give = after(left_row, hold, give)
+    took_b = trade(give, "x", 2)
     left_sum = spread(left_row, REPLICA, replicas).reshape(rank, height)
+    hold, give = halve(
+        halve_kernel, "halve_y", "y", 1, hold, took_b, (blocks // 8, height, half)
+    )
+    left_sum, hold, give = after(left_sum, hold, give)
+    took_c = trade(give, "y", 1)
 
     gram = call(gram_kernel, "gram", array((shards, rank // 2, 2 * rank), F32), [VMEM])(
         left_sum
     )
     grams = lax.all_to_all(gram, "z", 0, 0)
+    hold, give = halve(
+        turn_kernel, "turn", "y", 2, hold, took_c, (1, half // 2, height)
+    )
+    took_d = trade(give, "y", 2)
+    hold, give = halve(
+        split_kernel, "split", "y", 4, hold, took_d, (1, half // 4, height)
+    )
+    took_e = trade(give, "y", 4)
     p_factor, p_round = call(
         factor_kernel, "factor",
         [array((rank, height), F32), array((height, rank), BF16)],
         [VMEM, VMEM], [VMEM, VMEM],
     )(grams, left_sum)
 
-    fold = half // across
-    own, *give = call(
-        fan_kernel, "fan", [array((fold, height), F32)] * across, [SMEM, VMEM], [VMEM] * across
-    )(lax.axis_index("x").reshape(1), slab)
-    others = [
-        lax.ppermute(part, "x", [(i, i ^ j) for i in range(across)])
-        for j, part in enumerate(give, 1)
-    ]
+    fold = half // 4
     term = call(
-        right_kernel, "right", array((shards, fold // 2, 2 * rank), F32), [VMEM] * (1 + across)
-    )(p_round, own, *others)
+        right_kernel, "right", array((shards, fold // 2, 2 * rank), F32), [VMEM] * 3
+    )(p_round, hold, took_e)
     q_mine = (lax.all_to_all(term, "z", 0, 0).sum(0) / replicas).astype(BF16)
     q_own = spread(q_mine, PLANE, planes)
     q_other = lax.ppermute(q_own, "core", swap)
@@ -285,7 +308,7 @@
             decode_kernel, name,
             [array((height, width), BF16), array((rank, cols if before else half), BF16)],
             [SMEM] + [VMEM] * 4 + ([HBM, VMEM] if before else []), [HBM, VMEM],
-            [pltpu.VMEM(pieces.shape, BF16), pltpu.SemaphoreType.DMA((along,))],
+            [pltpu.VMEM(pieces.shape, BF16), pltpu.SemaphoreType.DMA((blocks,))],
             limit=12, aliases={5: 0} if before else None,
         )(jnp.stack([which, z]), p_round, factor, grad, error, *before)
 

time: 142 us -> 152 us (1.070)
  blocking collectives: 64.2 us -> 29.9 us
  waiting for transfers between devices: 4.15 us -> 29.1 us
  starting transfers between devices: 36.4 us -> 56.6 us
  between operations: 14.3 us -> 0.95 us
  local copies, waits for them, and re-layouts: 3.81 us -> 15.4 us
    all_to_all x1 -> x0, blocking collectives: 20.7 us -> none  [local(): lax.all_to_all(left.reshape(replicas, -1, height), REPLICA, 0, 0).sum(0)]
    ppermute x3 -> x5, waiting for transfers between devices: 0.01 us -> 13.4 us  [trade(): return lax.ppermute(give, axis, [(i, i ^ bit) for i in range(sizes[axis])])]
    all_to_all x2 -> x1, blocking collectives: 28.5 us -> 15.1 us  [spread(): lax.all_to_all(jnp.broadcast_to(block[None], (count, *block.shape)), axes...]
    all_to_all x0 -> x1, starting transfers between devices: none -> 11.5 us  [local(): lax.all_to_all(left.reshape(replicas, -1, height), REPLICA, 0, 0).sum(0)]
    unnamed x12 -> x34, local copies, waits for them, and re-layouts: 2.95 us -> 13.9 us
    all_to_all x0 -> x1, waiting for transfers between devices: none -> 9.18 us  [local(): lax.all_to_all(left.reshape(replicas, -1, height), REPLICA, 0, 0).sum(0)]
    all_to_all x1 -> x2, starting transfers between devices: 10.9 us -> 16.6 us  [spread(): lax.all_to_all(jnp.broadcast_to(block[None], (count, *block.shape)), axes...]
    ppermute x3 -> x5, starting transfers between devices: 9.57 us -> 13.1 us  [trade(): return lax.ppermute(give, axis, [(i, i ^ bit) for i in range(sizes[axis])])]
  transfers between devices with their start and end apart: 8 -> 11, of which waited for: 1 -> 8; matrix products, arithmetic and copies ran while one was open for 0% -> 1% of each run, Pallas kernels for 10% -> 9%
where the time goes in v5:
time: 152 us; the launch traced here: 151 us
  starting transfers between devices  56.6 us (37%)
  blocking collectives  29.9 us (20%)
  waiting for transfers between devices  29.1 us (19%)
  Pallas kernels  17.6 us (12%)
  local copies, waits for them, and re-layouts  15.4 us (10%)
    all_to_all x2, starting transfers between devices, spread(): lax.all_to_all(jnp.broadcast_to(block[None], (count, *block.shape)), axes...  16.6 us
    all_to_all x1, blocking collectives, spread(): lax.all_to_all(jnp.broadcast_to(block[None], (count, *block.shape)), axes...  15.1 us
    all_to_all x1, blocking collectives, local(): q_mine = (lax.all_to_all(term, 'z', 0, 0).sum(0) / replicas).astype(BF16)  14.8 us
    unnamed x34, local copies, waits for them, and re-layouts  13.9 us
    ppermute x5, waiting for transfers between devices, trade(): return lax.ppermute(give, axis, [(i, i ^ bit) for i in range(sizes[axis])])  13.4 us
    ppermute x5, starting transfers between devices, trade(): return lax.ppermute(give, axis, [(i, i ^ bit) for i in range(sizes[axis])])  13.1 us
    all_to_all x1, starting transfers between devices, local(): lax.all_to_all(left.reshape(replicas, -1, height), REPLICA, 0, 0).sum(0)  11.5 us
    all_to_all x1, waiting for transfers between devices, local(): lax.all_to_all(left.reshape(replicas, -1, height), REPLICA, 0, 0).sum(0)  9.18 us
  transfers between devices with their start and end apart: 11, of which 8 were waited for; matrix products, arithmetic and copies ran while one was open for 1% of the time, Pallas kernels for 9%

profile of v5, /device:TPU:1, one launch (start us, length us, event | category | flops | bytes accessed | tf_op | source)
XLA Modules:
  0.0 150.8 jit_solution(6664904940185211879)
XLA Ops:
  0.7 0.9 copy-done
  1.5 0.8 broadcast_in_dim.10
  2.3 10.9 %all-to-all-start = ((bf16[8,64,384]{2,1,0:T(8,128)(2,1)}), bf16[8,64,384]{2,1,0:T(8,128)(2,1)}, u32[]{:S(2)}, u32[]{:S(2)}) async-start(bf16[8,64,384]{2,1,0:T(8,128)(2,1)} %broadcast_in_dim.10), calls=%async_computation | async-start | bytes 786432 | tf_op jit(solution)/shard_map/all_to_all | solution.py:217
  13.2 1.4 copy-done.1
  14.6 1.4 copy-done.3
  16.0 1.1 give.1
  17.1 2.9 %collective-permute-start = (bf16[8,128,384]{2,1,0:T(8,128)(2,1)}, bf16[8,128,384]{2,1,0:T(8,128)(2,1)S(1)}, u32[]{:S(2)}, u32[]{:S(2)}) collective-permute-start(bf16[8,128,384]{2,1,0:T(8,128)(2,1)} %give.1), channel_id=1, source_target_pairs={{0,8},{8,0},{1,9},{9,1},{2,10},{10,2},{3,11},{11,3},{4,12},{12,4},... | collective-permute-start | bytes 2359304 | tf_op jit(solution)/shard_map/ppermute | solution.py:240
  20.2 0.9 copy-done.7
  21.1 1.0 collective-permute-done.took_ref
  22.1 1.4 copy-done.8
  23.6 0.9 copy-done.16
  24.5 2.9 %all-to-all-done.factor_ref = bf16[8,64,384]{2,1,0:T(8,128)(2,1)} async-done(((bf16[8,64,384]{2,1,0:T(8,128)(2,1)}), bf16[8,64,384]{2,1,0:T(8,128)(2,1)}, u32[]{:S(2)}, u32[]{:S(2)}) %all-to-all-start) | async-done | bytes 393248 | tf_op jit(solution)/shard_map/all_to_all | solution.py:217
  27.5 3.1 %collective-permute-start.1 = (f32[4,128,384]{2,1,0:T(8,128)}, f32[4,128,384]{2,1,0:T(8,128)S(1)}, u32[]{:S(2)}, u32[]{:S(2)}) collective-permute-start(f32[4,128,384]{2,1,0:T(8,128)} %copy-done.16), channel_id=1, source_target_pairs={{0,128},{128,0},{256,384},{384,256},{1,129},{129,1},{257,385},{385... | collective-permute-start | bytes 2359304 | tf_op jit(solution)/shard_map/ppermute | solution.py:250
  30.6 1.1 copy-done.6
  31.7 1.1 copy-done.9
  32.9 2.2 %left.1 = f32[64,128]{1,0:T(8,128)} custom-call(bf16[8,64,384]{2,1,0:T(8,128)(2,1)} %all-to-all-done.factor_ref, bf16[8,128,384]{2,1,0:T(8,128)(2,1)S(1)} %copy-done.9, bf16[8,128,384]{2,1,0:T(8,128)(2,1)S(1)} %copy-done.6), custom_call_target="tpu_custom_call" | custom-call | flops 99999997952 | bytes 2097152 | tf_op jit(solution)/shard_map/left/pallas_call | solution.py:263
  35.1 11.5 %all-to-all-start.1 = ((f32[64,1,128]{2,1,0:T(1,128)}), f32[64,1,128]{2,1,0:T(1,128)S(1)}, u32[]{:S(2)}, u32[]{:S(2)}) async-start(f32[64,1,128]{2,1,0:T(1,128)} %bitcast.8), calls=%async_computation.1 | async-start | bytes 65536 | tf_op jit(solution)/shard_map/all_to_all | solution.py:266
  46.7 9.2 %all-to-all-done.1 = f32[64,1,128]{2,1,0:T(1,128)S(1)} async-done(((f32[64,1,128]{2,1,0:T(1,128)}), f32[64,1,128]{2,1,0:T(1,128)S(1)}, u32[]{:S(2)}, u32[]{:S(2)}) %all-to-all-start.1) | async-done | bytes 32800 | tf_op jit(solution)/shard_map/all_to_all | solution.py:266
  55.9 0.8 halve_x.1
  56.8 0.7 copy-done.10
  57.5 3.0 %collective-permute-start.2 = (f32[2,128,384]{2,1,0:T(8,128)}, f32[2,128,384]{2,1,0:T(8,128)S(1)}, u32[]{:S(2)}, u32[]{:S(2)}) collective-permute-start(f32[2,128,384]{2,1,0:T(8,128)} %get-tuple-element.35), channel_id=1, source_target_pairs={{0,256},{128,384},{256,0},{384,128},{1,257},{129,385},{257,1},{385... | collective-permute-start | bytes 1179656 | tf_op jit(solution)/shard_map/ppermute | solution.py:250
  60.5 0.6 broadcast_in_dim.12
  61.1 5.7 %all-to-all-start.2 = ((f32[64,1,128]{2,1,0:T(1,128)}), f32[64,1,128]{2,1,0:T(1,128)S(1)}, u32[]{:S(2)}, u32[]{:S(2)}) async-start(f32[64,1,128]{2,1,0:T(1,128)} %broadcast_in_dim.12), calls=%async_computation.2 | async-start | bytes 65536 | tf_op jit(solution)/shard_map/all_to_all | solution.py:217
  66.9 4.2 %collective-permute-done.2.took_ref = f32[2,128,384]{2,1,0:T(8,128)S(1)} collective-permute-done((f32[2,128,384]{2,1,0:T(8,128)}, f32[2,128,384]{2,1,0:T(8,128)S(1)}, u32[]{:S(2)}, u32[]{:S(2)}) %collective-permute-start.2) | collective-permute-done | bytes 393248 | tf_op jit(solution)/shard_map/ppermute | solution.py:250
  71.1 1.0 copy-done.11
  72.1 0.7 halve_y.1
  72.8 0.7 copy-done.12
  73.5 2.6 %all-to-all-done.2 = f32[64,1,128]{2,1,0:T(1,128)S(1)} async-done(((f32[64,1,128]{2,1,0:T(1,128)}), f32[64,1,128]{2,1,0:T(1,128)S(1)}, u32[]{:S(2)}, u32[]{:S(2)}) %all-to-all-start.2) | async-done | bytes 32800 | tf_op jit(solution)/shard_map/all_to_all | solution.py:217
  76.1 2.3 %collective-permute-start.3 = (f32[1,128,384]{2,1,0:T(8,128)}, f32[1,128,384]{2,1,0:T(8,128)}, u32[]{:S(2)}, u32[]{:S(2)}) collective-permute-start(f32[1,128,384]{2,1,0:T(8,128)} %get-tuple-element.41), channel_id=1, source_target_pairs={{0,16},{16,0},{32,48},{48,32},{64,80},{80,64},{96,112},{112,96},{1... | collective-permute-start | bytes 589832 | tf_op jit(solution)/shard_map/ppermute | solution.py:250
  78.4 0.9 gram.1
  79.3 4.0 %all-to-all-start.3 = ((f32[8,32,128]{2,1,0:T(8,128)}), f32[8,32,128]{2,1,0:T(8,128)S(1)}, u32[]{:S(2)}, u32[]{:S(2)}) async-start(f32[8,32,128]{2,1,0:T(8,128)} %gram.1), calls=%async_computation.3 | async-start | bytes 262144 | tf_op jit(solution)/shard_map/all_to_all | solution.py:282
  83.3 0.8 collective-permute-done.3.took_ref
  84.1 0.9 copy-done.13
  85.0 1.7 %turn.1 = (f32[1,192,128]{2,1,0:T(8,128)S(1)}, f32[1,192,128]{2,1,0:T(8,128)}) custom-call(s32[1]{0:T(128)} %bitcast.15.bit_ref, f32[1,128,384]{2,1,0:T(8,128)S(1)} %copy-done.13, f32[1,128,384]{2,1,0:T(8,128)} %collective-permute-done.3.took_ref), custom_call_target="tpu_custom_call" | custom-call | tf_op jit(solution)/shard_map/turn/pallas_call | solution.py:245
  86.7 2.3 %collective-permute-start.4 = (f32[1,192,128]{2,1,0:T(8,128)}, f32[1,192,128]{2,1,0:T(8,128)}, u32[]{:S(2)}, u32[]{:S(2)}) collective-permute-start(f32[1,192,128]{2,1,0:T(8,128)} %get-tuple-element.43), channel_id=1, source_target_pairs={{0,32},{16,48},{32,0},{48,16},{64,96},{80,112},{96,64},{112,80},{1... | collective-permute-start | bytes 294920 | tf_op jit(solution)/shard_map/ppermute | solution.py:250
  89.0 5.6 %collective-permute-done.4.took_ref = f32[1,192,128]{2,1,0:T(8,128)} collective-permute-done((f32[1,192,128]{2,1,0:T(8,128)}, f32[1,192,128]{2,1,0:T(8,128)}, u32[]{:S(2)}, u32[]{:S(2)}) %collective-permute-start.4) | collective-permute-done | bytes 98336 | tf_op jit(solution)/shard_map/ppermute | solution.py:250
  94.7 0.9 split.1
  95.6 0.6 copy-done.14
  96.2 2.5 %collective-permute-start.5 = (f32[1,96,128]{2,1,0:T(8,128)S(1)}, f32[1,96,128]{2,1,0:T(8,128)S(1)}, u32[]{:S(2)}, u32[]{:S(2)}) collective-permute-start(f32[1,96,128]{2,1,0:T(8,128)S(1)} %get-tuple-element.45), channel_id=1, source_target_pairs={{0,64},{16,80},{32,96},{48,112},{64,0},{80,16},{96,32},{112,48},{1... | collective-permute-start | bytes 147464 | tf_op jit(solution)/shard_map/ppermute | solution.py:250
  98.7 3.5 %factor.1 = (f32[64,128]{1,0:T(8,128)}, bf16[128,64]{1,0:T(8,128)(2,1)S(1)}) custom-call(f32[8,32,128]{2,1,0:T(8,128)S(1)} %all-to-all-done.3.grams_ref, f32[64,128]{1,0:T(8,128)S(1)} %bitcast.30), custom_call_target="tpu_custom_call" | custom-call | tf_op jit(solution)/shard_map/factor/pallas_call | solution.py:291
  102.1 2.8 %collective-permute-done.5.took_ref = f32[1,96,128]{2,1,0:T(8,128)S(1)} collective-permute-done((f32[1,96,128]{2,1,0:T(8,128)S(1)}, f32[1,96,128]{2,1,0:T(8,128)S(1)}, u32[]{:S(2)}, u32[]{:S(2)}) %collective-permute-start.5) | collective-permute-done | bytes 49184 | tf_op jit(solution)/shard_map/ppermute | solution.py:250
  104.9 0.8 copy-done.15
  106.0 14.8 %all_to_all.30 = f32[8,48,128]{2,1,0:T(8,128)} all-to-all(f32[8,48,128]{2,1,0:T(8,128)S(1)} %right.1), channel_id=1, replica_groups=mesh['x'=4,'y'=8,'core'=2,'z'=8] {'z'}, dimensions={0} | all-to-all | bytes 393216 | tf_op jit(solution)/shard_map/all_to_all | solution.py:301
  120.8 0.9 reduce_sum.22
  121.8 15.1 %all_to_all.31.factor_ref = bf16[32,48,128]{2,1,0:T(8,128)(2,1)} all-to-all(bf16[32,48,128]{2,1,0:T(8,128)(2,1)S(1)} %broadcast_in_dim.26), channel_id=1, replica_groups=mesh['x'=4,'y'=8,'core'=2,'z'=8] {'x','y'}, dimensions={0} | all-to-all | bytes 786432 | tf_op jit(solution)/shard_map/all_to_all | solution.py:217
  136.9 8.5 %collective-permute-start.6 = (bf16[32,48,128]{2,1,0:T(8,128)(2,1)}, bf16[32,48,128]{2,1,0:T(8,128)(2,1)}, u32[]{:S(2)}, u32[]{:S(2)}) collective-permute-start(bf16[32,48,128]{2,1,0:T(8,128)(2,1)} %all_to_all.31.factor_ref), channel_id=1, source_target_pairs={{0,8},{8,0},{1,9},{9,1},{2,10},{10,2},{3,11},{11,3},{4,12},{12,4},... | collective-permute-start | bytes 1179656 | tf_op jit(solution)/shard_map/ppermute | solution.py:303
  145.6 2.2 %own.1 = (bf16[128,6144]{1,0:T(8,128)(2,1)}, bf16[64,384]{1,0:T(8,128)(2,1)S(1)}) custom-call(s32[2]{0:T(128)S(1)} %pad_add_fusion.1.place_ref, bf16[128,64]{1,0:T(8,128)(2,1)S(1)} %get-tuple-element.39.round_ref, bf16[32,48,128]{2,1,0:T(8,128)(2,1)} %all_to_all.31.factor_ref, bf16[128,6144]{1,0:T(8,128)(2,1)S(1)} %bitcast.23, bf16[128,6144]{1,0:T(8,128)(2,1)S(1)} %bitcast.27), custom_call_target="tpu_custom_call" | custom-call | tf_op jit(solution)/shard_map/own/pallas_call | solution.py:307
  147.9 2.9 %other.1 = (bf16[128,6144]{1,0:T(8,128)(2,1)}, bf16[64,768]{1,0:T(8,128)(2,1)}) custom-call(s32[2]{0:T(128)S(1)} %pad_add_fusion.place_ref, bf16[128,64]{1,0:T(8,128)(2,1)S(1)} %get-tuple-element.39.round_ref, bf16[32,48,128]{2,1,0:T(8,128)(2,1)} %collective-permute-done.6.factor_ref, ...), custom_call_target="tpu_custom_call", output_to_operand_aliasing={{0}: (5, {})} | custom-call | tf_op jit(solution)/shard_map/other/pallas_call | solution.py:307
  (32 shorter events, 1.0 us)
Async XLA Ops:
  0.6 0.9 copy-start
  2.3 25.2 %all-to-all-start = ((bf16[8,64,384]{2,1,0:T(8,128)(2,1)}), bf16[8,64,384]{2,1,0:T(8,128)(2,1)}, u32[]{:S(2)}, u32[]{:S(2)}) async-start(bf16[8,64,384]{2,1,0:T(8,128)(2,1)} %broadcast_in_dim.10), calls=%async_computation | async-start | bytes 786432 | tf_op jit(solution)/shard_map/all_to_all | solution.py:217
  13.2 1.4 copy-start.1
  14.6 1.4 copy-start.3
  16.0 4.0 %copy-start.2 = (bf16[1,128,6144]{2,1,0:T(8,128)(2,1)S(1)}, bf16[1,128,6144]{2,1,0:T(8,128)(2,1)}, u32[]{:S(2)}) copy-start(bf16[1,128,6144]{2,1,0:T(8,128)(2,1)} %param.3) | copy-start | bytes 4718596
  17.1 5.0 %collective-permute-start = (bf16[8,128,384]{2,1,0:T(8,128)(2,1)}, bf16[8,128,384]{2,1,0:T(8,128)(2,1)S(1)}, u32[]{:S(2)}, u32[]{:S(2)}) collective-permute-start(bf16[8,128,384]{2,1,0:T(8,128)(2,1)} %give.1), channel_id=1, source_target_pairs={{0,8},{8,0},{1,9},{9,1},{2,10},{10,2},{3,11},{11,3},{4,12},{12,4},... | collective-permute-start | bytes 2359304 | tf_op jit(solution)/shard_map/ppermute | solution.py:240
  20.2 0.9 copy-start.7
  22.1 5.4 %copy-start.5 = (bf16[8,128,384]{2,1,0:T(8,128)(2,1)}, bf16[8,128,384]{2,1,0:T(8,128)(2,1)S(1)}, u32[]{:S(2)}) copy-start(bf16[8,128,384]{2,1,0:T(8,128)(2,1)S(1)} %collective-permute-done.took_ref) | copy-start | bytes 2359300
  22.1 1.4 copy-start.8
  23.6 0.9 copy-start.16
  27.5 28.4 %collective-permute-start.1 = (f32[4,128,384]{2,1,0:T(8,128)}, f32[4,128,384]{2,1,0:T(8,128)S(1)}, u32[]{:S(2)}, u32[]{:S(2)}) collective-permute-start(f32[4,128,384]{2,1,0:T(8,128)} %copy-done.16), channel_id=1, source_target_pairs={{0,128},{128,0},{256,384},{384,256},{1,129},{129,1},{257,385},{385... | collective-permute-start | bytes 2359304 | tf_op jit(solution)/shard_map/ppermute | solution.py:250
  30.6 1.1 copy-start.6
  31.7 1.1 copy-start.9
  35.1 20.8 %all-to-all-start.1 = ((f32[64,1,128]{2,1,0:T(1,128)}), f32[64,1,128]{2,1,0:T(1,128)S(1)}, u32[]{:S(2)}, u32[]{:S(2)}) async-start(f32[64,1,128]{2,1,0:T(1,128)} %bitcast.8), calls=%async_computation.1 | async-start | bytes 65536 | tf_op jit(solution)/shard_map/all_to_all | solution.py:266
  56.8 0.7 copy-start.10
  57.5 13.6 %collective-permute-start.2 = (f32[2,128,384]{2,1,0:T(8,128)}, f32[2,128,384]{2,1,0:T(8,128)S(1)}, u32[]{:S(2)}, u32[]{:S(2)}) collective-permute-start(f32[2,128,384]{2,1,0:T(8,128)} %get-tuple-element.35), channel_id=1, source_target_pairs={{0,256},{128,384},{256,0},{384,128},{1,257},{129,385},{257,1},{385... | collective-permute-start | bytes 1179656 | tf_op jit(solution)/shard_map/ppermute | solution.py:250
  61.1 14.9 %all-to-all-start.2 = ((f32[64,1,128]{2,1,0:T(1,128)}), f32[64,1,128]{2,1,0:T(1,128)S(1)}, u32[]{:S(2)}, u32[]{:S(2)}) async-start(f32[64,1,128]{2,1,0:T(1,128)} %broadcast_in_dim.12), calls=%async_computation.2 | async-start | bytes 65536 | tf_op jit(solution)/shard_map/all_to_all | solution.py:217
  71.1 1.0 copy-start.11
  72.8 0.7 copy-start.12
  76.1 8.0 %collective-permute-start.3 = (f32[1,128,384]{2,1,0:T(8,128)}, f32[1,128,384]{2,1,0:T(8,128)}, u32[]{:S(2)}, u32[]{:S(2)}) collective-permute-start(f32[1,128,384]{2,1,0:T(8,128)} %get-tuple-element.41), channel_id=1, source_target_pairs={{0,16},{16,0},{32,48},{48,32},{64,80},{80,64},{96,112},{112,96},{1... | collective-permute-start | bytes 589832 | tf_op jit(solution)/shard_map/ppermute | solution.py:250
  79.3 19.4 %all-to-all-start.3 = ((f32[8,32,128]{2,1,0:T(8,128)}), f32[8,32,128]{2,1,0:T(8,128)S(1)}, u32[]{:S(2)}, u32[]{:S(2)}) async-start(f32[8,32,128]{2,1,0:T(8,128)} %gram.1), calls=%async_computation.3 | async-start | bytes 262144 | tf_op jit(solution)/shard_map/all_to_all | solution.py:282
  83.3 62.4 %copy-start.4 = (bf16[1,128,6144]{2,1,0:T(8,128)(2,1)S(1)}, bf16[1,128,6144]{2,1,0:T(8,128)(2,1)}, u32[]{:S(2)}) copy-start(bf16[1,128,6144]{2,1,0:T(8,128)(2,1)} %param.4) | copy-start | bytes 4718596
  84.1 0.9 copy-start.13
  86.7 8.0 %collective-permute-start.4 = (f32[1,192,128]{2,1,0:T(8,128)}, f32[1,192,128]{2,1,0:T(8,128)}, u32[]{:S(2)}, u32[]{:S(2)}) collective-permute-start(f32[1,192,128]{2,1,0:T(8,128)} %get-tuple-element.43), channel_id=1, source_target_pairs={{0,32},{16,48},{32,0},{48,16},{64,96},{80,112},{96,64},{112,80},{1... | collective-permute-start | bytes 294920 | tf_op jit(solution)/shard_map/ppermute | solution.py:250
  95.6 0.6 copy-start.14
  96.2 8.8 %collective-permute-start.5 = (f32[1,96,128]{2,1,0:T(8,128)S(1)}, f32[1,96,128]{2,1,0:T(8,128)S(1)}, u32[]{:S(2)}, u32[]{:S(2)}) collective-permute-start(f32[1,96,128]{2,1,0:T(8,128)S(1)} %get-tuple-element.45), channel_id=1, source_target_pairs={{0,64},{16,80},{32,96},{48,112},{64,0},{80,16},{96,32},{112,48},{1... | collective-permute-start | bytes 147464 | tf_op jit(solution)/shard_map/ppermute | solution.py:250
  104.9 0.8 copy-start.15
  136.9 11.0 %collective-permute-start.6 = (bf16[32,48,128]{2,1,0:T(8,128)(2,1)}, bf16[32,48,128]{2,1,0:T(8,128)(2,1)}, u32[]{:S(2)}, u32[]{:S(2)}) collective-permute-start(bf16[32,48,128]{2,1,0:T(8,128)(2,1)} %all_to_all.31.factor_ref), channel_id=1, source_target_pairs={{0,8},{8,0},{1,9},{9,1},{2,10},{10,2},{3,11},{11,3},{4,12},{12,4},... | collective-permute-start | bytes 1179656 | tf_op jit(solution)/shard_map/ppermute | solution.py:303

commit v6 on v4

--- a/solution.py
+++ b/solution.py
@@ -14,12 +14,12 @@
 PLANE = ("x", "y")
 REPLICA = ("x", "y", "core")
 LIGHT = pl.CostEstimate(flops=0, bytes_accessed=0, transcendentals=0)
-FULL = 60
+FULL, MOST = 60, 52
 WEIGHT = pl.CostEstimate(flops=10**11, bytes_accessed=2**21, transcendentals=0)
 
 
-def merge_kernel(core_ref, grad_hbm, error_hbm, out_hbm, grad, error, merged, sems):
-    parts, _, half = out_hbm.shape
+def merge_kernel(core_ref, grad_hbm, error_hbm, out_ref, grad, error, sems):
+    parts, _, half = out_ref.shape
     copies = []
     for i in range(parts):
         at = pl.ds(pl.multiple_of((2 * i + core_ref[0]) * half, half), half)
@@ -31,20 +31,28 @@
         )
         for copy in copies[-1]:
             copy.start()
-    sent = []
     for i in range(parts):
         for copy in copies[i]:
             copy.wait()
-        merged[i] = (grad[i].astype(F32) + error[i].astype(F32)).astype(BF16)
-        sent.append(pltpu.make_async_copy(merged.at[i], out_hbm.at[i], sems.at[2, i]))
-        sent[-1].start()
-    for copy in sent:
-        copy.wait()
+        out_ref[i] = (grad[i].astype(F32) + error[i].astype(F32)).astype(BF16)
 
 
 def pair_kernel(keep_ref, took_ref, out_ref):
     for i in range(out_ref.shape[0]):
-        out_ref[i] = keep_ref[i].astype(F32) + took_ref[i].astype(F32)
+        out_ref[i] = (keep_ref[i].astype(F32) + took_ref[i].astype(F32)).T
+
+
+def slots_kernel(core_ref, factor_hbm, out_ref, sems):
+    many, _, half = out_ref.shape
+    at = pl.ds(pl.multiple_of(core_ref[0] * half, half), half)
+    copies = [
+        pltpu.make_async_copy(factor_hbm.at[:, at], out_ref.at[i], sems.at[i])
+        for i in range(many)
+    ]
+    for copy in copies:
+        copy.start()
+    for copy in copies:
+        copy.wait()
 
 
 def left_kernel(factor_ref, keep_ref, took_ref, out_ref):
@@ -140,21 +148,10 @@
     round_ref[...] = factor_ref[...].T.astype(BF16)
 
 
-def fan_kernel(place_ref, slab_ref, *out_refs):
-    turned = slab_ref[...].T
-    fold = turned.shape[0] // len(out_refs)
-    for i in range(len(out_refs)):
-        for j, out_ref in enumerate(out_refs):
-            @pl.when(i == place_ref[0] ^ j)
-            def _():
-                out_ref[...] = turned[fold * i : fold * (i + 1)]
-
-
-def right_kernel(round_ref, own_ref, *rest):
-    *others, out_ref = rest
-    slab = own_ref[...]
-    for other in others:
-        slab = slab + other[...]
+def right_kernel(slab_ref, round_ref, out_ref):
+    slab = slab_ref[0]
+    for i in range(1, slab_ref.shape[0]):
+        slab = slab + slab_ref[i]
     term = jnp.dot(
         slab, round_ref[...].astype(F32),
         precision=lax.Precision.HIGHEST, preferred_element_type=F32,
@@ -236,18 +233,21 @@
 
     def merge(which, name, cost):
         return call(
-            merge_kernel, name, pieces, [SMEM, HBM, HBM], HBM,
-            [pltpu.VMEM(pieces.shape, BF16)] * 3 + [pltpu.SemaphoreType.DMA((3, along))],
-            limit=FULL, cost=cost,
+            merge_kernel, name, pieces, [SMEM, HBM, HBM], VMEM,
+            [pltpu.VMEM(pieces.shape, BF16)] * 2 + [pltpu.SemaphoreType.DMA((2, along))],
+            limit=MOST, cost=cost,
         )(which.reshape(1), grad, error)
 
     give, keep = merge(1 - core, "give", LIGHT), merge(core, "keep", WEIGHT)
     took = lax.ppermute(give, "core", swap)
-    pair = call(pair_kernel, "pair", array(pieces.shape, F32), [VMEM, VMEM], limit=8, cost=LIGHT)(keep, took)
+    pair = call(pair_kernel, "pair", array((along, half, height), F32), [VMEM, VMEM], limit=12, cost=LIGHT)(keep, took)
     slab = lax.psum_scatter(pair, "y", scatter_dimension=0, tiled=True)[0]
 
-    q_mine = lax.dynamic_slice_in_dim(q_in.T, core * half, half, 1)
-    q_all = spread(q_mine, "z", shards)
+    q_mine = call(
+        slots_kernel, "slots", array((shards, rank, half), BF16), [SMEM, HBM], VMEM,
+        [pltpu.SemaphoreType.DMA((shards,))], limit=FULL,
+    )(core.reshape(1), q_in.T)
+    q_all = lax.all_to_all(q_mine, "z", 0, 0)
     left = call(left_kernel, "left", array((rank, height), F32), [VMEM] * 3, limit=8, cost=WEIGHT)(
         q_all, keep, took
     )
@@ -265,16 +265,10 @@
     )(grams, left_sum)
 
     fold = half // across
-    own, *give = call(
-        fan_kernel, "fan", [array((fold, height), F32)] * across, [SMEM, VMEM], [VMEM] * across
-    )(lax.axis_index("x").reshape(1), slab)
-    others = [
-        lax.ppermute(part, "x", [(i, i ^ j) for i in range(across)])
-        for j, part in enumerate(give, 1)
-    ]
+    slab = lax.all_to_all(slab.reshape(across, fold, height), "x", 0, 0)
     term = call(
-        right_kernel, "right", array((shards, fold // 2, 2 * rank), F32), [VMEM] * (1 + across)
-    )(p_round, own, *others)
+        right_kernel, "right", array((shards, fold // 2, 2 * rank), F32), [VMEM, VMEM]
+    )(slab, p_round)
     q_mine = (lax.all_to_all(term, "z", 0, 0).sum(0) / replicas).astype(BF16)
     q_own = spread(q_mine, PLANE, planes)
     q_other = lax.ppermute(q_own, "core", swap)

time: 142 us -> 134 us (0.944)
  starting transfers between devices: 36.4 us -> 24.6 us
  blocking collectives: 64.2 us -> 68.9 us
  waiting for transfers between devices: 4.15 us -> 8.01 us
  local copies, waits for them, and re-layouts: 3.81 us -> 0.85 us
  Pallas kernels: 18.1 us -> 16.2 us
    all_to_all x0 -> x1, blocking collectives: none -> 10.4 us  [local(): grams = lax.all_to_all(gram, 'z', 0, 0)]
    ppermute x3 -> x0, starting transfers between devices: 9.57 us -> none  [local(): lax.ppermute(part, 'x', [(i, i ^ j) for i in range(across)])]
    all_to_all x1, blocking collectives: 15 us -> 11.1 us  [local(): q_mine = (lax.all_to_all(term, 'z', 0, 0).sum(0) / replicas).astype(BF16)]
    all_to_all x2, waiting for transfers between devices: 4.1 us -> 7.75 us  [the longest x1 6.09 us: local(): q_all = lax.all_to_all(q_mine, 'z', 0, 0)]
    ppermute x1, starting transfers between devices: 9.7 us -> 7.47 us  [local(): q_other = lax.ppermute(q_own, 'core', swap)]
    unnamed x12 -> x10, local copies, waits for them, and re-layouts: 2.95 us -> 0.78 us
    all_to_all x2, blocking collectives: 28.5 us -> 26.8 us  [spread(): lax.all_to_all(jnp.broadcast_to(block[None], (count, *block.shape)), axes...]
  transfers between devices with their start and end apart: 8 -> 5, of which waited for: 1 -> 3; matrix products, arithmetic and copies ran while one was open for 0% -> 0% of each run, Pallas kernels for 10% -> 8%
where the time goes in v6:
time: 134 us; the launch traced here: 133 us
  blocking collectives  68.9 us (51%)
  starting transfers between devices  24.6 us (18%)
  Pallas kernels  16.2 us (12%)
  between operations  14.2 us (11%)
  waiting for transfers between devices  8.01 us (6%)
    all_to_all x2, blocking collectives, spread(): lax.all_to_all(jnp.broadcast_to(block[None], (count, *block.shape)), axes...  26.8 us
    all_to_all x1, blocking collectives, local(): lax.all_to_all(left.reshape(replicas, -1, height), REPLICA, 0, 0).sum(0)  20.7 us
    all_to_all x1, blocking collectives, local(): q_mine = (lax.all_to_all(term, 'z', 0, 0).sum(0) / replicas).astype(BF16)  11.1 us
    all_to_all x1, starting transfers between devices, local(): q_all = lax.all_to_all(q_mine, 'z', 0, 0)  10.9 us
    all_to_all x1, blocking collectives, local(): grams = lax.all_to_all(gram, 'z', 0, 0)  10.4 us
    ppermute x1, starting transfers between devices, local(): q_other = lax.ppermute(q_own, 'core', swap)  7.47 us
    all_to_all x1, waiting for transfers between devices, local(): q_all = lax.all_to_all(q_mine, 'z', 0, 0)  6.09 us
    pallas_call x2, Pallas kernels, decode(): call(decode_kernel, name, [array((height, width), BF16), array((rank, col...  4.67 us
  transfers between devices with their start and end apart: 5, of which 3 were waited for; matrix products, arithmetic and copies ran while one was open for 0% of the time, Pallas kernels for 8%

profile of v6, /device:TPU:1, one launch (start us, length us, event | category | flops | bytes accessed | tf_op | source)
XLA Modules:
  0.0 133.0 jit_solution(14285865232658758629)
XLA Ops:
  7.2 2.0 %slots.1 = bf16[8,64,384]{2,1,0:T(8,128)(2,1)} custom-call(s32[1]{0:T(128)} %bitcast.2.core_ref, bf16[64,768]{1,0:T(8,128)(2,1)} %bitcast.27), custom_call_target="tpu_custom_call" | custom-call | tf_op jit(solution)/shard_map/slots/pallas_call | solution.py:246
  9.2 10.9 %all-to-all-start = ((bf16[8,64,384]{2,1,0:T(8,128)(2,1)}), bf16[8,64,384]{2,1,0:T(8,128)(2,1)S(1)}, u32[]{:S(2)}, u32[]{:S(2)}) async-start(bf16[8,64,384]{2,1,0:T(8,128)(2,1)} %slots.1), calls=%async_computation | async-start | bytes 786432 | tf_op jit(solution)/shard_map/all_to_all | solution.py:250
  20.1 0.0 reduce-scatter.2.cloned.1.call-start
  20.1 1.6 %give.1 = bf16[8,128,384]{2,1,0:T(8,128)(2,1)S(1)} custom-call(s32[1]{0:T(128)} %bitcast.core_ref, bf16[128,6144]{1,0:T(8,128)(2,1)} %bitcast.14, bf16[128,6144]{1,0:T(8,128)(2,1)} %bitcast.18), custom_call_target="tpu_custom_call" | custom-call | tf_op jit(solution)/shard_map/give/pallas_call | solution.py:235
  21.8 2.9 %collective-permute-start = (bf16[8,128,384]{2,1,0:T(8,128)(2,1)S(1)}, bf16[8,128,384]{2,1,0:T(8,128)(2,1)S(1)}, u32[]{:S(2)}, u32[]{:S(2)}) collective-permute-start(bf16[8,128,384]{2,1,0:T(8,128)(2,1)S(1)} %give.1), channel_id=1, source_target_pairs={{0,8},{8,0},{1,9},{9,1},{2,10},{10,2},{3,11},{11,3},{4,12},{12,4},... | collective-permute-start | bytes 2359304 | tf_op jit(solution)/shard_map/ppermute | solution.py:242
  24.7 1.6 %keep.1.keep_ref = bf16[8,128,384]{2,1,0:T(8,128)(2,1)S(1)} custom-call(s32[1]{0:T(128)} %bitcast.2.core_ref, bf16[128,6144]{1,0:T(8,128)(2,1)} %bitcast.15, bf16[128,6144]{1,0:T(8,128)(2,1)} %bitcast.19), custom_call_target="tpu_custom_call" | custom-call | flops 99999997952 | bytes 2097152 | tf_op jit(solution)/shard_map/keep/pallas_call | solution.py:235
  26.3 0.2 collective-permute-done.took_ref
  26.5 1.6 %pair.1 = f32[8,384,128]{2,1,0:T(8,128)} custom-call(bf16[8,128,384]{2,1,0:T(8,128)(2,1)S(1)} %keep.1.keep_ref, bf16[8,128,384]{2,1,0:T(8,128)(2,1)S(1)} %collective-permute-done.took_ref), custom_call_target="tpu_custom_call" | custom-call | tf_op jit(solution)/shard_map/pair/pallas_call | solution.py:243
  28.2 0.0 reduce-scatter.2.cloned.1.call-update
  28.2 6.1 %all-to-all-done.factor_ref = bf16[8,64,384]{2,1,0:T(8,128)(2,1)S(1)} async-done(((bf16[8,64,384]{2,1,0:T(8,128)(2,1)}), bf16[8,64,384]{2,1,0:T(8,128)(2,1)S(1)}, u32[]{:S(2)}, u32[]{:S(2)}) %all-to-all-start) | async-done | bytes 393248 | tf_op jit(solution)/shard_map/all_to_all | solution.py:250
  34.3 0.6 left.1
  34.9 20.7 %all_to_all.35 = f32[64,1,128]{2,1,0:T(1,128)S(1)} all-to-all(f32[64,1,128]{2,1,0:T(1,128)S(1)} %bitcast.24), channel_id=1, replica_groups=mesh['x'=4,'y'=8,'core'=2,'z'=8] {'x','y','core'}, dimensions={0} | all-to-all | bytes 65536 | tf_op jit(solution)/shard_map/all_to_all | solution.py:254
  55.6 0.1 reduce_sum.18
  55.7 13.3 %all_to_all.36 = f32[64,1,128]{2,1,0:T(1,128)S(1)} all-to-all(f32[64,1,128]{2,1,0:T(1,128)S(1)} %broadcast_in_dim.6), channel_id=1, replica_groups=mesh['x'=4,'y'=8,'core'=2,'z'=8] {'x','y','core'}, dimensions={0} | all-to-all | bytes 65536 | tf_op jit(solution)/shard_map/all_to_all | solution.py:216
  69.0 0.0 copy-start.1
  69.0 0.2 gram.1
  69.3 0.0 copy-start
  69.3 10.4 %all_to_all.37.grams_ref = f32[8,32,128]{2,1,0:T(8,128)S(1)} all-to-all(f32[8,32,128]{2,1,0:T(8,128)S(1)} %gram.1), channel_id=1, replica_groups=mesh['x'=4,'y'=8,'core'=2,'z'=8] {'z'}, dimensions={0} | all-to-all | bytes 262144 | tf_op jit(solution)/shard_map/all_to_all | solution.py:260
  79.6 0.0 reduce-scatter.2.cloned.1.call-done
  79.6 3.4 %all-to-all-start.4 = ((f32[4,96,128]{2,1,0:T(8,128)}), f32[4,96,128]{2,1,0:T(8,128)S(1)}, u32[]{:S(2)}, u32[]{:S(2)}) async-start(f32[4,96,128]{2,1,0:T(8,128)} %bitcast.26), calls=%async_computation.5 | async-start | bytes 393216 | tf_op jit(solution)/shard_map/all_to_all | solution.py:268
  83.0 3.5 %factor.1 = (f32[64,128]{1,0:T(8,128)}, bf16[128,64]{1,0:T(8,128)(2,1)S(1)}) custom-call(f32[8,32,128]{2,1,0:T(8,128)S(1)} %all_to_all.37.grams_ref, f32[64,128]{1,0:T(8,128)S(1)} %bitcast.23), custom_call_target="tpu_custom_call" | custom-call | tf_op jit(solution)/shard_map/factor/pallas_call | solution.py:261
  86.5 0.0 copy-start.2
  86.5 1.7 %all-to-all-done.4.slab_ref = f32[4,96,128]{2,1,0:T(8,128)S(1)} async-done(((f32[4,96,128]{2,1,0:T(8,128)}), f32[4,96,128]{2,1,0:T(8,128)S(1)}, u32[]{:S(2)}, u32[]{:S(2)}) %all-to-all-start.4) | async-done | bytes 196640 | tf_op jit(solution)/shard_map/all_to_all | solution.py:268
  88.2 0.3 right.1
  88.4 11.1 %all_to_all.38 = f32[8,48,128]{2,1,0:T(8,128)S(1)} all-to-all(f32[8,48,128]{2,1,0:T(8,128)S(1)} %right.1), channel_id=1, replica_groups=mesh['x'=4,'y'=8,'core'=2,'z'=8] {'z'}, dimensions={0} | all-to-all | bytes 393216 | tf_op jit(solution)/shard_map/all_to_all | solution.py:272
  99.5 0.0 copy-done.2
  99.5 0.1 broadcast_in_dim.7
  99.6 13.5 %all_to_all.39.factor_ref = bf16[32,48,128]{2,1,0:T(8,128)(2,1)S(1)} all-to-all(bf16[32,48,128]{2,1,0:T(8,128)(2,1)S(1)} %broadcast_in_dim.7), channel_id=1, replica_groups=mesh['x'=4,'y'=8,'core'=2,'z'=8] {'x','y'}, dimensions={0} | all-to-all | bytes 786432 | tf_op jit(solution)/shard_map/all_to_all | solution.py:216
  113.1 7.5 %collective-permute-start.1 = (bf16[32,48,128]{2,1,0:T(8,128)(2,1)S(1)}, bf16[32,48,128]{2,1,0:T(8,128)(2,1)}, u32[]{:S(2)}, u32[]{:S(2)}) collective-permute-start(bf16[32,48,128]{2,1,0:T(8,128)(2,1)S(1)} %all_to_all.39.factor_ref), channel_id=1, source_target_pairs={{0,8},{8,0},{1,9},{9,1},{2,10},{10,2},{3,11},{11,3},{4,12},{12,4},... | collective-permute-start | bytes 1179656 | tf_op jit(solution)/shard_map/ppermute | solution.py:274
  120.5 0.1 pad_add_fusion.place_ref
  120.6 0.1 pad_add_fusion.1.place_ref
  120.7 0.0 copy-done.1
  120.7 0.0 copy-done
  120.7 0.0 copy-start.3
  120.7 0.8 copy-done.3
  121.5 0.0 copy-start.4
  121.5 1.8 %own.1 = (bf16[128,6144]{1,0:T(8,128)(2,1)}, bf16[64,384]{1,0:T(8,128)(2,1)S(1)}) custom-call(s32[2]{0:T(128)S(1)} %pad_add_fusion.1.place_ref, bf16[128,64]{1,0:T(8,128)(2,1)S(1)} %copy-done.3, bf16[32,48,128]{2,1,0:T(8,128)(2,1)S(1)} %all_to_all.39.factor_ref, bf16[128,6144]{1,0:T(8,128)(2,1)S(1)} %bitcast.16, bf16[128,6144]{1,0:T(8,128)(2,1)S(1)} %bitcast.20), custom_call_target="tpu_custom_call" | custom-call | tf_op jit(solution)/shard_map/own/pallas_call | solution.py:278
  123.2 0.0 collective-permute-done.1.factor_ref
  123.3 0.0 copy-done.4
  123.3 2.9 %other.1 = (bf16[128,6144]{1,0:T(8,128)(2,1)}, bf16[64,768]{1,0:T(8,128)(2,1)}) custom-call(s32[2]{0:T(128)S(1)} %pad_add_fusion.place_ref, bf16[128,64]{1,0:T(8,128)(2,1)S(1)} %copy-done.4, bf16[32,48,128]{2,1,0:T(8,128)(2,1)} %collective-permute-done.1.factor_ref, bf16[128,6144]{1,0:T(8,128)(2,1)S(1)} %bitcast.17, ...), custom_call_target="tpu_custom_call", output_to_operand_aliasing={{0}: (5, {})} | custom-call | tf_op jit(solution)/shard_map/other/pallas_call | solution.py:278
  (3 shorter events, 0.0 us)
Async XLA Ops:
  9.2 25.1 %all-to-all-start = ((bf16[8,64,384]{2,1,0:T(8,128)(2,1)}), bf16[8,64,384]{2,1,0:T(8,128)(2,1)S(1)}, u32[]{:S(2)}, u32[]{:S(2)}) async-start(bf16[8,64,384]{2,1,0:T(8,128)(2,1)} %slots.1), calls=%async_computation | async-start | bytes 786432 | tf_op jit(solution)/shard_map/all_to_all | solution.py:250
  20.1 59.6 %reduce-scatter.2.cloned.1.call-start = ((), (), s32[]{:S(2)}) async-start(), calls=%async_computation.8 | async-start | bytes 1769472 | tf_op jit(solution)/shard_map/reduce_scatter | solution.py:244
  21.8 4.8 %collective-permute-start = (bf16[8,128,384]{2,1,0:T(8,128)(2,1)S(1)}, bf16[8,128,384]{2,1,0:T(8,128)(2,1)S(1)}, u32[]{:S(2)}, u32[]{:S(2)}) collective-permute-start(bf16[8,128,384]{2,1,0:T(8,128)(2,1)S(1)} %give.1), channel_id=1, source_target_pairs={{0,8},{8,0},{1,9},{9,1},{2,10},{10,2},{3,11},{11,3},{4,12},{12,4},... | collective-permute-start | bytes 2359304 | tf_op jit(solution)/shard_map/ppermute | solution.py:242
  69.0 51.7 %copy-start.1 = (bf16[1,128,6144]{2,1,0:T(8,128)(2,1)S(1)}, bf16[1,128,6144]{2,1,0:T(8,128)(2,1)}, u32[]{:S(2)}) copy-start(bf16[1,128,6144]{2,1,0:T(8,128)(2,1)} %param.4) | copy-start | bytes 4718596
  69.3 51.4 %copy-start = (bf16[1,128,6144]{2,1,0:T(8,128)(2,1)S(1)}, bf16[1,128,6144]{2,1,0:T(8,128)(2,1)}, u32[]{:S(2)}) copy-start(bf16[1,128,6144]{2,1,0:T(8,128)(2,1)} %param.3) | copy-start | bytes 4718596
  79.6 8.5 %all-to-all-start.4 = ((f32[4,96,128]{2,1,0:T(8,128)}), f32[4,96,128]{2,1,0:T(8,128)S(1)}, u32[]{:S(2)}, u32[]{:S(2)}) async-start(f32[4,96,128]{2,1,0:T(8,128)} %bitcast.26), calls=%async_computation.5 | async-start | bytes 393216 | tf_op jit(solution)/shard_map/all_to_all | solution.py:268
  86.5 13.0 %copy-start.2 = (bf16[128,64]{1,0:T(8,128)(2,1)}, bf16[128,64]{1,0:T(8,128)(2,1)S(1)}, u32[]{:S(2)}) copy-start(bf16[128,64]{1,0:T(8,128)(2,1)S(1)} %get-tuple-element.9.round_ref) | copy-start | bytes 49156
  113.1 10.2 %collective-permute-start.1 = (bf16[32,48,128]{2,1,0:T(8,128)(2,1)S(1)}, bf16[32,48,128]{2,1,0:T(8,128)(2,1)}, u32[]{:S(2)}, u32[]{:S(2)}) collective-permute-start(bf16[32,48,128]{2,1,0:T(8,128)(2,1)S(1)} %all_to_all.39.factor_ref), channel_id=1, source_target_pairs={{0,8},{8,0},{1,9},{9,1},{2,10},{10,2},{3,11},{11,3},{4,12},{12,4},... | collective-permute-start | bytes 1179656 | tf_op jit(solution)/shard_map/ppermute | solution.py:274
  120.7 0.8 copy-start.3
  121.5 1.8 %copy-start.4 = (bf16[128,64]{1,0:T(8,128)(2,1)S(1)}, bf16[128,64]{1,0:T(8,128)(2,1)}, u32[]{:S(2)}) copy-start(bf16[128,64]{1,0:T(8,128)(2,1)} %copy-done.2) | copy-start | bytes 49156
Sparse Core Ops, SparseCore 0:
  28.3 40.3 reduce-scatter.1

commit v7 on v6

--- a/solution.py
+++ b/solution.py
@@ -42,11 +42,11 @@
         out_ref[i] = (keep_ref[i].astype(F32) + took_ref[i].astype(F32)).T
 
 
-def slots_kernel(core_ref, factor_hbm, out_ref, sems):
-    many, _, half = out_ref.shape
+def slots_kernel(core_ref, factor_hbm, out_hbm, sems):
+    many, _, half = out_hbm.shape
     at = pl.ds(pl.multiple_of(core_ref[0] * half, half), half)
     copies = [
-        pltpu.make_async_copy(factor_hbm.at[:, at], out_ref.at[i], sems.at[i])
+        pltpu.make_async_copy(factor_hbm.at[:, at], out_hbm.at[i], sems.at[i])
         for i in range(many)
     ]
     for copy in copies:
@@ -64,11 +64,24 @@
             factor_ref[i], both, (((1,), (1,)), ((), ())), preferred_element_type=F32
         )
         total = term if total is None else total + term
-    out_ref[...] = total[:, :height] + total[:, height:]
-
-
-def gram_kernel(left_ref, out_ref):
-    left = left_ref[...]
+    total = total[:, :height] + total[:, height:]
+    for i in range(out_ref.shape[0]):
+        out_ref[i] = total
+
+
+def sum_kernel(parts_ref, out_ref):
+    total = parts_ref[0]
+    for i in range(1, parts_ref.shape[0]):
+        total = total + parts_ref[i]
+    for i in range(out_ref.shape[0]):
+        out_ref[i] = total
+
+
+def gram_kernel(parts_ref, left_ref, out_ref):
+    left = parts_ref[0]
+    for i in range(1, parts_ref.shape[0]):
+        left = left + parts_ref[i]
+    left_ref[...] = left
     gram = lax.dot_general(
         left, left, (((1,), (1,)), ((), ())),
         precision=lax.Precision.HIGHEST, preferred_element_type=F32,
@@ -162,7 +175,7 @@
 
 
 def decode_kernel(place_ref, round_ref, factor_ref, grad, error, *rest):
-    *before, out_hbm, next_ref, out, sems = rest
+    *before, out_hbm, next_hbm, out, turned, sems = rest
     planes, fold, lanes = factor_ref.shape
     rank, half = lanes // 2, out.shape[-1]
     inner = half // (2 * fold)
@@ -177,7 +190,14 @@
             pieces += [piece[:, :rank], piece[:, rank:]]
         return jnp.concatenate(pieces, axis=0)
 
-    sent = []
+    mine = factor(place_ref[1]).astype(F32).T.astype(BF16)
+    if before:
+        for at, part in ((which, mine), (1 - which, before[1][...])):
+            turned[:, pl.ds(pl.multiple_of(at * half, half), half)] = part
+    else:
+        turned[...] = mine
+    sent = [pltpu.make_async_copy(turned, next_hbm, sems.at[parts])]
+    sent[-1].start()
     for i in range(parts):
         decoded = lax.dot_general(
             rounded, factor(i), (((1,), (1,)), ((), ())), preferred_element_type=F32
@@ -188,12 +208,6 @@
         ).astype(BF16)
         sent.append(pltpu.make_async_copy(out.at[i], out_hbm.at[:, at], sems.at[i]))
         sent[-1].start()
-    turned = factor(place_ref[1]).astype(F32).T.astype(BF16)
-    if before:
-        for at, part in ((which, turned), (1 - which, before[1][...])):
-            next_ref[:, pl.ds(pl.multiple_of(at * half, half), half)] = part
-    else:
-        next_ref[...] = turned
     for copy in sent:
         copy.wait()
 
@@ -244,19 +258,23 @@
     slab = lax.psum_scatter(pair, "y", scatter_dimension=0, tiled=True)[0]
 
     q_mine = call(
-        slots_kernel, "slots", array((shards, rank, half), BF16), [SMEM, HBM], VMEM,
+        slots_kernel, "slots", array((shards, rank, half), BF16), [SMEM, HBM], HBM,
         [pltpu.SemaphoreType.DMA((shards,))], limit=FULL,
     )(core.reshape(1), q_in.T)
     q_all = lax.all_to_all(q_mine, "z", 0, 0)
-    left = call(left_kernel, "left", array((rank, height), F32), [VMEM] * 3, limit=8, cost=WEIGHT)(
-        q_all, keep, took
-    )
-    left_row = lax.all_to_all(left.reshape(replicas, -1, height), REPLICA, 0, 0).sum(0)
-    left_sum = spread(left_row, REPLICA, replicas).reshape(rank, height)
-
-    gram = call(gram_kernel, "gram", array((shards, rank // 2, 2 * rank), F32), [VMEM])(
-        left_sum
-    )
+    first, second = ("x", "core"), "y"
+    left = call(
+        left_kernel, "left", array((across * cores, rank, height), F32), [VMEM] * 3,
+        limit=8, cost=WEIGHT,
+    )(q_all, keep, took)
+    left = lax.all_to_all(left, first, 0, 0)
+    left = call(sum_kernel, "sum", array((along, rank, height), F32), [VMEM])(left)
+    left = lax.all_to_all(left, second, 0, 0)
+    left_sum, gram = call(
+        gram_kernel, "gram",
+        [array((rank, height), F32), array((shards, rank // 2, 2 * rank), F32)],
+        [VMEM], [VMEM, VMEM],
+    )(left)
     grams = lax.all_to_all(gram, "z", 0, 0)
     p_factor, p_round = call(
         factor_kernel, "factor",
@@ -275,11 +293,14 @@
 
 
     def decode(which, name, factor, *before):
+        out = (rank, cols if before else half)
         return call(
-            decode_kernel, name,
-            [array((height, width), BF16), array((rank, cols if before else half), BF16)],
-            [SMEM] + [VMEM] * 4 + ([HBM, VMEM] if before else []), [HBM, VMEM],
-            [pltpu.VMEM(pieces.shape, BF16), pltpu.SemaphoreType.DMA((along,))],
+            decode_kernel, name, [array((height, width), BF16), array(out, BF16)],
+            [SMEM] + [VMEM] * 4 + ([HBM, VMEM] if before else []), [HBM, HBM],
+            [
+                pltpu.VMEM(pieces.shape, BF16), pltpu.VMEM(out, BF16),
+                pltpu.SemaphoreType.DMA((along + 1,)),
+            ],
             limit=12, aliases={5: 0} if before else None,
         )(jnp.stack([which, z]), p_round, factor, grad, error, *before)
 

time: 134 us -> 148 us (1.10)
  Pallas kernels: 16.2 us -> 26.9 us
  starting transfers between devices: 24.6 us -> 27.3 us
    all_to_all x1 -> x2, blocking collectives: 20.7 us -> 32.6 us  [the longest x1 20.5 us: local(): left = lax.all_to_all(left, second, 0, 0)]
    all_to_all x2 -> x1, blocking collectives: 26.8 us -> 15.3 us  [spread(): lax.all_to_all(jnp.broadcast_to(block[None], (count, *block.shape)), axes...]
    pallas_call x1, Pallas kernels: 2.04 us -> 13.1 us  [local(): call(slots_kernel, 'slots', array((shards, rank, half), BF16), [SMEM, HBM...]
    ppermute x1, starting transfers between devices: 7.47 us -> 10.1 us  [local(): q_other = lax.ppermute(q_own, 'core', swap)]
    pallas_call x4 -> x5, Pallas kernels: 5.5 us -> 5.14 us  [the longest x2 4.28 us: decode(): call(decode_kernel, name, [array((height, width), BF16), array(out, BF16)...]
where the time goes in v7:
time: 148 us; the launch traced here: 147 us
  blocking collectives  69.5 us (47%)
  starting transfers between devices  27.3 us (18%)
  Pallas kernels  26.9 us (18%)
  between operations  14.2 us (10%)
  waiting for transfers between devices  8.03 us (5%)
    all_to_all x1, blocking collectives, local(): left = lax.all_to_all(left, second, 0, 0)  20.5 us
    all_to_all x1, blocking collectives, spread(): lax.all_to_all(jnp.broadcast_to(block[None], (count, *block.shape)), axes...  15.3 us
    pallas_call x1, Pallas kernels, local(): call(slots_kernel, 'slots', array((shards, rank, half), BF16), [SMEM, HBM...  13.1 us
    all_to_all x1, blocking collectives, local(): left = lax.all_to_all(left, first, 0, 0)  12 us
    all_to_all x1, blocking collectives, local(): q_mine = (lax.all_to_all(term, 'z', 0, 0).sum(0) / replicas).astype(BF16)  11 us
    all_to_all x1, starting transfers between devices, local(): q_all = lax.all_to_all(q_mine, 'z', 0, 0)  10.9 us
    all_to_all x1, blocking collectives, local(): grams = lax.all_to_all(gram, 'z', 0, 0)  10.6 us
    ppermute x1, starting transfers between devices, local(): q_other = lax.ppermute(q_own, 'core', swap)  10.1 us
  transfers between devices with their start and end apart: 5, of which 3 were waited for; matrix products, arithmetic and copies ran while one was open for 0% of the time, Pallas kernels for 8%

profile of v7, /device:TPU:1, one launch (start us, length us, event | category | flops | bytes accessed | tf_op | source)
XLA Modules:
  0.0 146.8 jit_solution(4394353997194510187)
XLA Ops:
  7.2 13.1 %slots.1 = bf16[8,64,384]{2,1,0:T(8,128)(2,1)} custom-call(s32[1]{0:T(128)} %bitcast.2.core_ref, bf16[64,768]{1,0:T(8,128)(2,1)} %bitcast.20), custom_call_target="tpu_custom_call" | custom-call | tf_op jit(solution)/shard_map/slots/pallas_call | solution.py:260
  20.3 10.9 %all-to-all-start = ((bf16[8,64,384]{2,1,0:T(8,128)(2,1)}), bf16[8,64,384]{2,1,0:T(8,128)(2,1)S(1)}, u32[]{:S(2)}, u32[]{:S(2)}) async-start(bf16[8,64,384]{2,1,0:T(8,128)(2,1)} %slots.1), calls=%async_computation | async-start | bytes 786432 | tf_op jit(solution)/shard_map/all_to_all | solution.py:264
  31.1 0.0 reduce-scatter.2.cloned.1.call-start
  31.2 1.6 %give.1 = bf16[8,128,384]{2,1,0:T(8,128)(2,1)S(1)} custom-call(s32[1]{0:T(128)} %bitcast.core_ref, bf16[128,6144]{1,0:T(8,128)(2,1)} %bitcast.10, bf16[128,6144]{1,0:T(8,128)(2,1)} %bitcast.14), custom_call_target="tpu_custom_call" | custom-call | tf_op jit(solution)/shard_map/give/pallas_call | solution.py:249
  32.8 2.9 %collective-permute-start = (bf16[8,128,384]{2,1,0:T(8,128)(2,1)S(1)}, bf16[8,128,384]{2,1,0:T(8,128)(2,1)S(1)}, u32[]{:S(2)}, u32[]{:S(2)}) collective-permute-start(bf16[8,128,384]{2,1,0:T(8,128)(2,1)S(1)} %give.1), channel_id=1, source_target_pairs={{0,8},{8,0},{1,9},{9,1},{2,10},{10,2},{3,11},{11,3},{4,12},{12,4},... | collective-permute-start | bytes 2359304 | tf_op jit(solution)/shard_map/ppermute | solution.py:256
  35.7 1.6 %keep.1.keep_ref = bf16[8,128,384]{2,1,0:T(8,128)(2,1)S(1)} custom-call(s32[1]{0:T(128)} %bitcast.2.core_ref, bf16[128,6144]{1,0:T(8,128)(2,1)} %bitcast.11, bf16[128,6144]{1,0:T(8,128)(2,1)} %bitcast.15), custom_call_target="tpu_custom_call" | custom-call | flops 99999997952 | bytes 2097152 | tf_op jit(solution)/shard_map/keep/pallas_call | solution.py:249
  37.4 0.2 collective-permute-done.took_ref
  37.6 1.6 %pair.1 = f32[8,384,128]{2,1,0:T(8,128)} custom-call(bf16[8,128,384]{2,1,0:T(8,128)(2,1)S(1)} %keep.1.keep_ref, bf16[8,128,384]{2,1,0:T(8,128)(2,1)S(1)} %collective-permute-done.took_ref), custom_call_target="tpu_custom_call" | custom-call | tf_op jit(solution)/shard_map/pair/pallas_call | solution.py:257
  39.2 0.0 reduce-scatter.2.cloned.1.call-update
  39.2 6.1 %all-to-all-done.factor_ref = bf16[8,64,384]{2,1,0:T(8,128)(2,1)S(1)} async-done(((bf16[8,64,384]{2,1,0:T(8,128)(2,1)}), bf16[8,64,384]{2,1,0:T(8,128)(2,1)S(1)}, u32[]{:S(2)}, u32[]{:S(2)}) %all-to-all-start) | async-done | bytes 393248 | tf_op jit(solution)/shard_map/all_to_all | solution.py:264
  45.3 0.6 left.1
  45.9 12.0 %all_to_all.35.parts_ref = f32[8,64,128]{2,1,0:T(8,128)S(1)} all-to-all(f32[8,64,128]{2,1,0:T(8,128)S(1)} %left.1), channel_id=1, replica_groups=mesh['x'=4,'y'=8,'core'=2,'z'=8] {'x','core'}, dimensions={0} | all-to-all | bytes 524288 | tf_op jit(solution)/shard_map/all_to_all | solution.py:270
  58.0 20.5 %all_to_all.36.parts_ref = f32[8,64,128]{2,1,0:T(8,128)S(1)} all-to-all(f32[8,64,128]{2,1,0:T(8,128)S(1)} %sum.1), channel_id=1, replica_groups=mesh['x'=4,'y'=8,'core'=2,'z'=8] {'y'}, dimensions={0} | all-to-all | bytes 524288 | tf_op jit(solution)/shard_map/all_to_all | solution.py:272
  78.5 0.0 copy-start.1
  78.5 0.2 gram.1
  78.8 0.0 copy-start
  78.8 10.6 %all_to_all.37.grams_ref = f32[8,32,128]{2,1,0:T(8,128)S(1)} all-to-all(f32[8,32,128]{2,1,0:T(8,128)S(1)} %get-tuple-element.11), channel_id=1, replica_groups=mesh['x'=4,'y'=8,'core'=2,'z'=8] {'z'}, dimensions={0} | all-to-all | bytes 262144 | tf_op jit(solution)/shard_map/all_to_all | solution.py:278
  89.4 0.0 reduce-scatter.2.cloned.1.call-done
  89.4 3.4 %all-to-all-start.4 = ((f32[4,96,128]{2,1,0:T(8,128)}), f32[4,96,128]{2,1,0:T(8,128)S(1)}, u32[]{:S(2)}, u32[]{:S(2)}) async-start(f32[4,96,128]{2,1,0:T(8,128)} %bitcast.19), calls=%async_computation.5 | async-start | bytes 393216 | tf_op jit(solution)/shard_map/all_to_all | solution.py:286
  92.8 3.5 %factor.1 = (f32[64,128]{1,0:T(8,128)}, bf16[128,64]{1,0:T(8,128)(2,1)S(1)}) custom-call(f32[8,32,128]{2,1,0:T(8,128)S(1)} %all_to_all.37.grams_ref, f32[64,128]{1,0:T(8,128)S(1)} %get-tuple-element.12.left_ref), custom_call_target="tpu_custom_call" | custom-call | tf_op jit(solution)/shard_map/factor/pallas_call | solution.py:279
  96.2 0.0 copy-start.2
  96.2 1.7 %all-to-all-done.4.slab_ref = f32[4,96,128]{2,1,0:T(8,128)S(1)} async-done(((f32[4,96,128]{2,1,0:T(8,128)}), f32[4,96,128]{2,1,0:T(8,128)S(1)}, u32[]{:S(2)}, u32[]{:S(2)}) %all-to-all-start.4) | async-done | bytes 196640 | tf_op jit(solution)/shard_map/all_to_all | solution.py:286
  97.9 0.3 right.1
  98.2 11.0 %all_to_all.38 = f32[8,48,128]{2,1,0:T(8,128)S(1)} all-to-all(f32[8,48,128]{2,1,0:T(8,128)S(1)} %right.1), channel_id=1, replica_groups=mesh['x'=4,'y'=8,'core'=2,'z'=8] {'z'}, dimensions={0} | all-to-all | bytes 393216 | tf_op jit(solution)/shard_map/all_to_all | solution.py:290
  109.2 0.0 copy-done.2
  109.2 0.1 broadcast_in_dim.4
  109.3 15.3 %all_to_all.39.factor_ref = bf16[32,48,128]{2,1,0:T(8,128)(2,1)S(1)} all-to-all(bf16[32,48,128]{2,1,0:T(8,128)(2,1)S(1)} %broadcast_in_dim.4), channel_id=1, replica_groups=mesh['x'=4,'y'=8,'core'=2,'z'=8] {'x','y'}, dimensions={0} | all-to-all | bytes 786432 | tf_op jit(solution)/shard_map/all_to_all | solution.py:230
  124.6 10.1 %collective-permute-start.1 = (bf16[32,48,128]{2,1,0:T(8,128)(2,1)S(1)}, bf16[32,48,128]{2,1,0:T(8,128)(2,1)}, u32[]{:S(2)}, u32[]{:S(2)}) collective-permute-start(bf16[32,48,128]{2,1,0:T(8,128)(2,1)S(1)} %all_to_all.39.factor_ref), channel_id=1, source_target_pairs={{0,8},{8,0},{1,9},{9,1},{2,10},{10,2},{3,11},{11,3},{4,12},{12,4},... | collective-permute-start | bytes 1179656 | tf_op jit(solution)/shard_map/ppermute | solution.py:292
  134.7 0.1 pad_add_fusion.place_ref
  134.8 0.1 pad_add_fusion.1.place_ref
  134.9 0.0 copy-done.1
  134.9 0.0 copy-done
  134.9 0.0 copy-start.3
  134.9 0.8 copy-done.3
  135.6 0.0 copy-start.4
  135.6 2.0 %own.1 = (bf16[128,6144]{1,0:T(8,128)(2,1)}, bf16[64,384]{1,0:T(8,128)(2,1)S(1)}) custom-call(s32[2]{0:T(128)S(1)} %pad_add_fusion.1.place_ref, bf16[128,64]{1,0:T(8,128)(2,1)S(1)} %copy-done.3, bf16[32,48,128]{2,1,0:T(8,128)(2,1)S(1)} %all_to_all.39.factor_ref, bf16[128,6144]{1,0:T(8,128)(2,1)S(1)} %bitcast.12, bf16[128,6144]{1,0:T(8,128)(2,1)S(1)} %bitcast.16), custom_call_target="tpu_custom_call" | custom-call | tf_op jit(solution)/shard_map/own/pallas_call | solution.py:297
  137.6 0.0 collective-permute-done.1.factor_ref
  137.7 0.0 copy-done.4
  137.7 2.3 %other.1 = (bf16[128,6144]{1,0:T(8,128)(2,1)}, bf16[64,768]{1,0:T(8,128)(2,1)}) custom-call(s32[2]{0:T(128)S(1)} %pad_add_fusion.place_ref, bf16[128,64]{1,0:T(8,128)(2,1)S(1)} %copy-done.4, bf16[32,48,128]{2,1,0:T(8,128)(2,1)} %collective-permute-done.1.factor_ref, bf16[128,6144]{1,0:T(8,128)(2,1)S(1)} %bitcast.13, ...), custom_call_target="tpu_custom_call", output_to_operand_aliasing={{0}: (5, {})} | custom-call | tf_op jit(solution)/shard_map/other/pallas_call | solution.py:297
  (3 shorter events, 0.0 us)
Async XLA Ops:
  20.3 25.1 %all-to-all-start = ((bf16[8,64,384]{2,1,0:T(8,128)(2,1)}), bf16[8,64,384]{2,1,0:T(8,128)(2,1)S(1)}, u32[]{:S(2)}, u32[]{:S(2)}) async-start(bf16[8,64,384]{2,1,0:T(8,128)(2,1)} %slots.1), calls=%async_computation | async-start | bytes 786432 | tf_op jit(solution)/shard_map/all_to_all | solution.py:264
  31.1 58.2 %reduce-scatter.2.cloned.1.call-start = ((), (), s32[]{:S(2)}) async-start(), calls=%async_computation.8 | async-start | bytes 1769472 | tf_op jit(solution)/shard_map/reduce_scatter | solution.py:258
  32.8 4.8 %collective-permute-start = (bf16[8,128,384]{2,1,0:T(8,128)(2,1)S(1)}, bf16[8,128,384]{2,1,0:T(8,128)(2,1)S(1)}, u32[]{:S(2)}, u32[]{:S(2)}) collective-permute-start(bf16[8,128,384]{2,1,0:T(8,128)(2,1)S(1)} %give.1), channel_id=1, source_target_pairs={{0,8},{8,0},{1,9},{9,1},{2,10},{10,2},{3,11},{11,3},{4,12},{12,4},... | collective-permute-start | bytes 2359304 | tf_op jit(solution)/shard_map/ppermute | solution.py:256
  78.5 56.3 %copy-start.1 = (bf16[1,128,6144]{2,1,0:T(8,128)(2,1)S(1)}, bf16[1,128,6144]{2,1,0:T(8,128)(2,1)}, u32[]{:S(2)}) copy-start(bf16[1,128,6144]{2,1,0:T(8,128)(2,1)} %param.4) | copy-start | bytes 4718596
  78.8 56.1 %copy-start = (bf16[1,128,6144]{2,1,0:T(8,128)(2,1)S(1)}, bf16[1,128,6144]{2,1,0:T(8,128)(2,1)}, u32[]{:S(2)}) copy-start(bf16[1,128,6144]{2,1,0:T(8,128)(2,1)} %param.3) | copy-start | bytes 4718596
  89.4 8.5 %all-to-all-start.4 = ((f32[4,96,128]{2,1,0:T(8,128)}), f32[4,96,128]{2,1,0:T(8,128)S(1)}, u32[]{:S(2)}, u32[]{:S(2)}) async-start(f32[4,96,128]{2,1,0:T(8,128)} %bitcast.19), calls=%async_computation.5 | async-start | bytes 393216 | tf_op jit(solution)/shard_map/all_to_all | solution.py:286
  96.2 13.0 %copy-start.2 = (bf16[128,64]{1,0:T(8,128)(2,1)}, bf16[128,64]{1,0:T(8,128)(2,1)S(1)}, u32[]{:S(2)}) copy-start(bf16[128,64]{1,0:T(8,128)(2,1)S(1)} %get-tuple-element.13.round_ref) | copy-start | bytes 49156
  124.6 13.1 %collective-permute-start.1 = (bf16[32,48,128]{2,1,0:T(8,128)(2,1)S(1)}, bf16[32,48,128]{2,1,0:T(8,128)(2,1)}, u32[]{:S(2)}, u32[]{:S(2)}) collective-permute-start(bf16[32,48,128]{2,1,0:T(8,128)(2,1)S(1)} %all_to_all.39.factor_ref), channel_id=1, source_target_pairs={{0,8},{8,0},{1,9},{9,1},{2,10},{10,2},{3,11},{11,3},{4,12},{12,4},... | collective-permute-start | bytes 1179656 | tf_op jit(solution)/shard_map/ppermute | solution.py:292
  134.9 0.8 copy-start.3
  135.6 2.0 %copy-start.4 = (bf16[128,64]{1,0:T(8,128)(2,1)S(1)}, bf16[128,64]{1,0:T(8,128)(2,1)}, u32[]{:S(2)}) copy-start(bf16[128,64]{1,0:T(8,128)(2,1)} %copy-done.2) | copy-start | bytes 49156
Sparse Core Ops, SparseCore 0:
  39.4 42.7 reduce-scatter.1

commit v8 on v6

--- a/solution.py
+++ b/solution.py
@@ -14,7 +14,6 @@
 PLANE = ("x", "y")
 REPLICA = ("x", "y", "core")
 LIGHT = pl.CostEstimate(flops=0, bytes_accessed=0, transcendentals=0)
-FULL, MOST = 60, 52
 WEIGHT = pl.CostEstimate(flops=10**11, bytes_accessed=2**21, transcendentals=0)
 
 
@@ -42,12 +41,14 @@
         out_ref[i] = (keep_ref[i].astype(F32) + took_ref[i].astype(F32)).T
 
 
-def slots_kernel(core_ref, factor_hbm, out_ref, sems):
-    many, _, half = out_ref.shape
+def slots_kernel(core_ref, factor_hbm, out_hbm, mine, sems):
+    many, _, half = out_hbm.shape
     at = pl.ds(pl.multiple_of(core_ref[0] * half, half), half)
+    read = pltpu.make_async_copy(factor_hbm.at[:, at], mine, sems.at[many])
+    read.start()
+    read.wait()
     copies = [
-        pltpu.make_async_copy(factor_hbm.at[:, at], out_ref.at[i], sems.at[i])
-        for i in range(many)
+        pltpu.make_async_copy(mine, out_hbm.at[i], sems.at[i]) for i in range(many)
     ]
     for copy in copies:
         copy.start()
@@ -161,14 +162,20 @@
         out_ref[i] = packed
 
 
-def decode_kernel(place_ref, round_ref, factor_ref, grad, error, *rest):
-    *before, out_hbm, next_ref, out, sems = rest
+def decode_kernel(first, place_ref, round_ref, factor_ref, grad, error, *rest):
+    if first:
+        out_hbm, next_ref, rounded_ref, out, sems = rest
+    else:
+        _, half_ref, out_hbm, next_hbm, next_ref, out, sems = rest
+        rounded_ref = round_ref
     planes, fold, lanes = factor_ref.shape
     rank, half = lanes // 2, out.shape[-1]
     inner = half // (2 * fold)
     parts = planes // inner
     which = place_ref[0]
-    rounded = round_ref[...]
+    if first:
+        fetch = pltpu.make_async_copy(round_ref, rounded_ref, sems.at[parts])
+        fetch.start()
 
     def factor(part):
         pieces = []
@@ -177,7 +184,17 @@
             pieces += [piece[:, :rank], piece[:, rank:]]
         return jnp.concatenate(pieces, axis=0)
 
+    mine = factor(place_ref[1]).astype(F32).T.astype(BF16)
     sent = []
+    if first:
+        next_ref[...] = mine
+        fetch.wait()
+    else:
+        for at, part in ((which, mine), (1 - which, half_ref[...])):
+            next_ref[:, pl.ds(pl.multiple_of(at * half, half), half)] = part
+        sent.append(pltpu.make_async_copy(next_ref, next_hbm, sems.at[parts]))
+        sent[-1].start()
+    rounded = rounded_ref[...]
     for i in range(parts):
         decoded = lax.dot_general(
             rounded, factor(i), (((1,), (1,)), ((), ())), preferred_element_type=F32
@@ -188,12 +205,6 @@
         ).astype(BF16)
         sent.append(pltpu.make_async_copy(out.at[i], out_hbm.at[:, at], sems.at[i]))
         sent[-1].start()
-    turned = factor(place_ref[1]).astype(F32).T.astype(BF16)
-    if before:
-        for at, part in ((which, turned), (1 - which, before[1][...])):
-            next_ref[:, pl.ds(pl.multiple_of(at * half, half), half)] = part
-    else:
-        next_ref[...] = turned
     for copy in sent:
         copy.wait()
 
@@ -212,6 +223,10 @@
     )
 
 
+def in_hbm(x):
+    return pltpu.with_memory_space_constraint(x, pltpu.HBM)
+
+
 def spread(block, axes, count):
     return lax.all_to_all(jnp.broadcast_to(block[None], (count, *block.shape)), axes, 0, 0)
 
@@ -229,14 +244,13 @@
     array = jax.ShapeDtypeStruct
 
     pieces = array((along, height, half), BF16)
-    staged = pltpu.VMEM((height, width), BF16)
 
     def merge(which, name, cost):
         return call(
             merge_kernel, name, pieces, [SMEM, HBM, HBM], VMEM,
             [pltpu.VMEM(pieces.shape, BF16)] * 2 + [pltpu.SemaphoreType.DMA((2, along))],
-            limit=MOST, cost=cost,
-        )(which.reshape(1), grad, error)
+            limit=12, cost=cost,
+        )(which.reshape(1), in_hbm(grad), in_hbm(error))
 
     give, keep = merge(1 - core, "give", LIGHT), merge(core, "keep", WEIGHT)
     took = lax.ppermute(give, "core", swap)
@@ -244,9 +258,9 @@
     slab = lax.psum_scatter(pair, "y", scatter_dimension=0, tiled=True)[0]
 
     q_mine = call(
-        slots_kernel, "slots", array((shards, rank, half), BF16), [SMEM, HBM], VMEM,
-        [pltpu.SemaphoreType.DMA((shards,))], limit=FULL,
-    )(core.reshape(1), q_in.T)
+        slots_kernel, "slots", array((shards, rank, half), BF16), [SMEM, HBM], HBM,
+        [pltpu.VMEM((rank, half), BF16), pltpu.SemaphoreType.DMA((shards + 1,))],
+    )(core.reshape(1), in_hbm(q_in.T))
     q_all = lax.all_to_all(q_mine, "z", 0, 0)
     left = call(left_kernel, "left", array((rank, height), F32), [VMEM] * 3, limit=8, cost=WEIGHT)(
         q_all, keep, took
@@ -274,16 +288,18 @@
     q_other = lax.ppermute(q_own, "core", swap)
 
 
-    def decode(which, name, factor, *before):
-        return call(
-            decode_kernel, name,
-            [array((height, width), BF16), array((rank, cols if before else half), BF16)],
-            [SMEM] + [VMEM] * 4 + ([HBM, VMEM] if before else []), [HBM, VMEM],
-            [pltpu.VMEM(pieces.shape, BF16), pltpu.SemaphoreType.DMA((along,))],
-            limit=12, aliases={5: 0} if before else None,
-        )(jnp.stack([which, z]), p_round, factor, grad, error, *before)
-
-    new_error, q_next = decode(1 - core, "other", q_other, *decode(core, "own", q_own))
+    errors, halves = array((height, width), BF16), array((rank, half), BF16)
+    staged = [pltpu.VMEM(pieces.shape, BF16), pltpu.SemaphoreType.DMA((along + 1,))]
+    new_error, q_half, rounded = call(
+        functools.partial(decode_kernel, True), "own", [errors, halves, p_round],
+        [SMEM, HBM] + [VMEM] * 3, [HBM, VMEM, VMEM], staged, limit=12,
+    )(jnp.stack([core, z]), in_hbm(p_round), q_own, grad, error)
+    new_error, q_next = call(
+        functools.partial(decode_kernel, False), "other",
+        [errors, array((rank, cols), BF16)],
+        [SMEM] + [VMEM] * 4 + [HBM, VMEM], [HBM, HBM],
+        [pltpu.VMEM((rank, cols), BF16)] + staged, limit=12, aliases={5: 0},
+    )(jnp.stack([1 - core, z]), rounded, q_other, grad, error, new_error, q_half)
     return new_error[None], p_factor.T, q_next.T
 
 

time: 134 us -> 133 us (level)
  transfers between devices with their start and end apart: 5 -> 5, of which waited for: 3 -> 3; matrix products, arithmetic and copies ran while one was open for 0% -> 0% of each run, Pallas kernels for 8% -> 9%
where the time goes in v8:
time: 133 us; the launch traced here: 132 us
  blocking collectives  68.9 us (52%)
  starting transfers between devices  24.6 us (18%)
  Pallas kernels  15.9 us (12%)
  between operations  14.2 us (11%)
  waiting for transfers between devices  8.03 us (6%)
    all_to_all x2, blocking collectives, spread(): lax.all_to_all(jnp.broadcast_to(block[None], (count, *block.shape)), axes...  26.7 us
    all_to_all x1, blocking collectives, local(): lax.all_to_all(left.reshape(replicas, -1, height), REPLICA, 0, 0).sum(0)  20.7 us
    all_to_all x1, blocking collectives, local(): q_mine = (lax.all_to_all(term, 'z', 0, 0).sum(0) / replicas).astype(BF16)  11.1 us
    all_to_all x1, starting transfers between devices, local(): q_all = lax.all_to_all(q_mine, 'z', 0, 0)  10.9 us
    all_to_all x1, blocking collectives, local(): grams = lax.all_to_all(gram, 'z', 0, 0)  10.4 us
    ppermute x1, starting transfers between devices, local(): q_other = lax.ppermute(q_own, 'core', swap)  7.47 us
    all_to_all x1, waiting for transfers between devices, local(): q_all = lax.all_to_all(q_mine, 'z', 0, 0)  6.11 us
    pallas_call x1, Pallas kernels, local(): call(factor_kernel, 'factor', [array((rank, height), F32), array((height,...  3.48 us
  transfers between devices with their start and end apart: 5, of which 3 were waited for; matrix products, arithmetic and copies ran while one was open for 0% of the time, Pallas kernels for 9%

profile of v8, /device:TPU:1, one launch (start us, length us, event | category | flops | bytes accessed | tf_op | source)
XLA Modules:
  0.0 132.0 jit_solution(11581128317084066544)
XLA Ops:
  7.2 1.6 %slots.1 = bf16[8,64,384]{2,1,0:T(8,128)(2,1)} custom-call(s32[1]{0:T(128)} %bitcast.2.core_ref, bf16[64,768]{1,0:T(8,128)(2,1)} %bitcast.27), custom_call_target="tpu_custom_call" | custom-call | tf_op jit(solution)/shard_map/slots/pallas_call | solution.py:260
  8.8 10.9 %all-to-all-start = ((bf16[8,64,384]{2,1,0:T(8,128)(2,1)}), bf16[8,64,384]{2,1,0:T(8,128)(2,1)S(1)}, u32[]{:S(2)}, u32[]{:S(2)}) async-start(bf16[8,64,384]{2,1,0:T(8,128)(2,1)} %slots.1), calls=%async_computation | async-start | bytes 786432 | tf_op jit(solution)/shard_map/all_to_all | solution.py:264
  19.7 0.0 reduce-scatter.2.cloned.1.call-start
  19.7 1.6 %give.1 = bf16[8,128,384]{2,1,0:T(8,128)(2,1)S(1)} custom-call(s32[1]{0:T(128)} %bitcast.core_ref, bf16[128,6144]{1,0:T(8,128)(2,1)} %bitcast.14, bf16[128,6144]{1,0:T(8,128)(2,1)} %bitcast.18), custom_call_target="tpu_custom_call" | custom-call | tf_op jit(solution)/shard_map/give/pallas_call | solution.py:249
  21.4 2.9 %collective-permute-start = (bf16[8,128,384]{2,1,0:T(8,128)(2,1)S(1)}, bf16[8,128,384]{2,1,0:T(8,128)(2,1)S(1)}, u32[]{:S(2)}, u32[]{:S(2)}) collective-permute-start(bf16[8,128,384]{2,1,0:T(8,128)(2,1)S(1)} %give.1), channel_id=1, source_target_pairs={{0,8},{8,0},{1,9},{9,1},{2,10},{10,2},{3,11},{11,3},{4,12},{12,4},... | collective-permute-start | bytes 2359304 | tf_op jit(solution)/shard_map/ppermute | solution.py:256
  24.3 1.6 %keep.1.keep_ref = bf16[8,128,384]{2,1,0:T(8,128)(2,1)S(1)} custom-call(s32[1]{0:T(128)} %bitcast.2.core_ref, bf16[128,6144]{1,0:T(8,128)(2,1)} %bitcast.15, bf16[128,6144]{1,0:T(8,128)(2,1)} %bitcast.19), custom_call_target="tpu_custom_call" | custom-call | flops 99999997952 | bytes 2097152 | tf_op jit(solution)/shard_map/keep/pallas_call | solution.py:249
  25.9 0.2 collective-permute-done.took_ref
  26.1 1.6 %pair.1 = f32[8,384,128]{2,1,0:T(8,128)} custom-call(bf16[8,128,384]{2,1,0:T(8,128)(2,1)S(1)} %keep.1.keep_ref, bf16[8,128,384]{2,1,0:T(8,128)(2,1)S(1)} %collective-permute-done.took_ref), custom_call_target="tpu_custom_call" | custom-call | tf_op jit(solution)/shard_map/pair/pallas_call | solution.py:257
  27.8 0.0 reduce-scatter.2.cloned.1.call-update
  27.8 6.1 %all-to-all-done.factor_ref = bf16[8,64,384]{2,1,0:T(8,128)(2,1)S(1)} async-done(((bf16[8,64,384]{2,1,0:T(8,128)(2,1)}), bf16[8,64,384]{2,1,0:T(8,128)(2,1)S(1)}, u32[]{:S(2)}, u32[]{:S(2)}) %all-to-all-start) | async-done | bytes 393248 | tf_op jit(solution)/shard_map/all_to_all | solution.py:264
  33.9 0.6 left.1
  34.5 20.7 %all_to_all.35 = f32[64,1,128]{2,1,0:T(1,128)S(1)} all-to-all(f32[64,1,128]{2,1,0:T(1,128)S(1)} %bitcast.24), channel_id=1, replica_groups=mesh['x'=4,'y'=8,'core'=2,'z'=8] {'x','y','core'}, dimensions={0} | all-to-all | bytes 65536 | tf_op jit(solution)/shard_map/all_to_all | solution.py:268
  55.2 0.1 reduce_sum.18
  55.3 13.3 %all_to_all.36 = f32[64,1,128]{2,1,0:T(1,128)S(1)} all-to-all(f32[64,1,128]{2,1,0:T(1,128)S(1)} %broadcast_in_dim.6), channel_id=1, replica_groups=mesh['x'=4,'y'=8,'core'=2,'z'=8] {'x','y','core'}, dimensions={0} | all-to-all | bytes 65536 | tf_op jit(solution)/shard_map/all_to_all | solution.py:231
  68.6 0.0 copy-start.1
  68.6 0.2 gram.1
  68.9 0.0 copy-start
  68.9 10.4 %all_to_all.37.grams_ref = f32[8,32,128]{2,1,0:T(8,128)S(1)} all-to-all(f32[8,32,128]{2,1,0:T(8,128)S(1)} %gram.1), channel_id=1, replica_groups=mesh['x'=4,'y'=8,'core'=2,'z'=8] {'z'}, dimensions={0} | all-to-all | bytes 262144 | tf_op jit(solution)/shard_map/all_to_all | solution.py:274
  79.2 0.0 reduce-scatter.2.cloned.1.call-done
  79.2 3.4 %all-to-all-start.4 = ((f32[4,96,128]{2,1,0:T(8,128)}), f32[4,96,128]{2,1,0:T(8,128)S(1)}, u32[]{:S(2)}, u32[]{:S(2)}) async-start(f32[4,96,128]{2,1,0:T(8,128)} %bitcast.26), calls=%async_computation.5 | async-start | bytes 393216 | tf_op jit(solution)/shard_map/all_to_all | solution.py:282
  82.6 3.5 %factor.1 = (f32[64,128]{1,0:T(8,128)}, bf16[128,64]{1,0:T(8,128)(2,1)S(1)}) custom-call(f32[8,32,128]{2,1,0:T(8,128)S(1)} %all_to_all.37.grams_ref, f32[64,128]{1,0:T(8,128)S(1)} %bitcast.23), custom_call_target="tpu_custom_call" | custom-call | tf_op jit(solution)/shard_map/factor/pallas_call | solution.py:275
  86.1 0.0 copy-start.2
  86.1 1.7 %all-to-all-done.4.slab_ref = f32[4,96,128]{2,1,0:T(8,128)S(1)} async-done(((f32[4,96,128]{2,1,0:T(8,128)}), f32[4,96,128]{2,1,0:T(8,128)S(1)}, u32[]{:S(2)}, u32[]{:S(2)}) %all-to-all-start.4) | async-done | bytes 196640 | tf_op jit(solution)/shard_map/all_to_all | solution.py:282
  87.8 0.3 right.1
  88.0 11.1 %all_to_all.38 = f32[8,48,128]{2,1,0:T(8,128)S(1)} all-to-all(f32[8,48,128]{2,1,0:T(8,128)S(1)} %right.1), channel_id=1, replica_groups=mesh['x'=4,'y'=8,'core'=2,'z'=8] {'z'}, dimensions={0} | all-to-all | bytes 393216 | tf_op jit(solution)/shard_map/all_to_all | solution.py:286
  99.1 0.0 copy-done.2
  99.1 0.1 broadcast_in_dim.7
  99.2 13.4 %all_to_all.39.factor_ref = bf16[32,48,128]{2,1,0:T(8,128)(2,1)S(1)} all-to-all(bf16[32,48,128]{2,1,0:T(8,128)(2,1)S(1)} %broadcast_in_dim.7), channel_id=1, replica_groups=mesh['x'=4,'y'=8,'core'=2,'z'=8] {'x','y'}, dimensions={0} | all-to-all | bytes 786432 | tf_op jit(solution)/shard_map/all_to_all | solution.py:231
  112.6 7.5 %collective-permute-start.1 = (bf16[32,48,128]{2,1,0:T(8,128)(2,1)S(1)}, bf16[32,48,128]{2,1,0:T(8,128)(2,1)}, u32[]{:S(2)}, u32[]{:S(2)}) collective-permute-start(bf16[32,48,128]{2,1,0:T(8,128)(2,1)S(1)} %all_to_all.39.factor_ref), channel_id=1, source_target_pairs={{0,8},{8,0},{1,9},{9,1},{2,10},{10,2},{3,11},{11,3},{4,12},{12,4},... | collective-permute-start | bytes 1179656 | tf_op jit(solution)/shard_map/ppermute | solution.py:288
  120.1 0.1 pad_add_fusion.place_ref
  120.2 0.1 pad_add_fusion.1.place_ref
  120.3 0.0 copy-done.1
  120.3 0.0 copy-done
  120.3 2.6 %own.1 = (bf16[128,6144]{1,0:T(8,128)(2,1)}, bf16[64,384]{1,0:T(8,128)(2,1)S(1)}, bf16[128,64]{1,0:T(8,128)(2,1)S(1)}) custom-call(s32[2]{0:T(128)S(1)} %pad_add_fusion.1.place_ref, bf16[128,64]{1,0:T(8,128)(2,1)} %copy-done.2, bf16[32,48,128]{2,1,0:T(8,128)(2,1)S(1)} %all_to_all.39.factor_ref, bf16[128,6144]{1,0:T(8,128)(2,1)S(1)} %bitcast.16, ...), custom_call_target="tpu_custom_call" | custom-call | tf_op jit(solution)/shard_map/own/pallas_call | solution.py:293
  122.8 0.0 collective-permute-done.1.factor_ref
  122.8 2.3 %other.1 = (bf16[128,6144]{1,0:T(8,128)(2,1)}, bf16[64,768]{1,0:T(8,128)(2,1)}) custom-call(s32[2]{0:T(128)S(1)} %pad_add_fusion.place_ref, bf16[128,64]{1,0:T(8,128)(2,1)S(1)} %get-tuple-element.11.round_ref, bf16[32,48,128]{2,1,0:T(8,128)(2,1)} %collective-permute-done.1.factor_ref, ...), custom_call_target="tpu_custom_call", output_to_operand_aliasing={{0}: (5, {})} | custom-call | tf_op jit(solution)/shard_map/other/pallas_call | solution.py:297
  (3 shorter events, 0.0 us)
Async XLA Ops:
  8.8 25.1 %all-to-all-start = ((bf16[8,64,384]{2,1,0:T(8,128)(2,1)}), bf16[8,64,384]{2,1,0:T(8,128)(2,1)S(1)}, u32[]{:S(2)}, u32[]{:S(2)}) async-start(bf16[8,64,384]{2,1,0:T(8,128)(2,1)} %slots.1), calls=%async_computation | async-start | bytes 786432 | tf_op jit(solution)/shard_map/all_to_all | solution.py:264
  19.7 59.5 %reduce-scatter.2.cloned.1.call-start = ((), (), s32[]{:S(2)}) async-start(), calls=%async_computation.8 | async-start | bytes 1769472 | tf_op jit(solution)/shard_map/reduce_scatter | solution.py:258
  21.4 4.8 %collective-permute-start = (bf16[8,128,384]{2,1,0:T(8,128)(2,1)S(1)}, bf16[8,128,384]{2,1,0:T(8,128)(2,1)S(1)}, u32[]{:S(2)}, u32[]{:S(2)}) collective-permute-start(bf16[8,128,384]{2,1,0:T(8,128)(2,1)S(1)} %give.1), channel_id=1, source_target_pairs={{0,8},{8,0},{1,9},{9,1},{2,10},{10,2},{3,11},{11,3},{4,12},{12,4},... | collective-permute-start | bytes 2359304 | tf_op jit(solution)/shard_map/ppermute | solution.py:256
  68.6 51.7 %copy-start.1 = (bf16[1,128,6144]{2,1,0:T(8,128)(2,1)S(1)}, bf16[1,128,6144]{2,1,0:T(8,128)(2,1)}, u32[]{:S(2)}) copy-start(bf16[1,128,6144]{2,1,0:T(8,128)(2,1)} %param.4) | copy-start | bytes 4718596
  68.9 51.4 %copy-start = (bf16[1,128,6144]{2,1,0:T(8,128)(2,1)S(1)}, bf16[1,128,6144]{2,1,0:T(8,128)(2,1)}, u32[]{:S(2)}) copy-start(bf16[1,128,6144]{2,1,0:T(8,128)(2,1)} %param.3) | copy-start | bytes 4718596
  79.2 8.5 %all-to-all-start.4 = ((f32[4,96,128]{2,1,0:T(8,128)}), f32[4,96,128]{2,1,0:T(8,128)S(1)}, u32[]{:S(2)}, u32[]{:S(2)}) async-start(f32[4,96,128]{2,1,0:T(8,128)} %bitcast.26), calls=%async_computation.5 | async-start | bytes 393216 | tf_op jit(solution)/shard_map/all_to_all | solution.py:282
  86.1 13.0 %copy-start.2 = (bf16[128,64]{1,0:T(8,128)(2,1)}, bf16[128,64]{1,0:T(8,128)(2,1)S(1)}, u32[]{:S(2)}) copy-start(bf16[128,64]{1,0:T(8,128)(2,1)S(1)} %get-tuple-element.10.round_ref) | copy-start | bytes 49156
  112.6 10.2 %collective-permute-start.1 = (bf16[32,48,128]{2,1,0:T(8,128)(2,1)S(1)}, bf16[32,48,128]{2,1,0:T(8,128)(2,1)}, u32[]{:S(2)}, u32[]{:S(2)}) collective-permute-start(bf16[32,48,128]{2,1,0:T(8,128)(2,1)S(1)} %all_to_all.39.factor_ref), channel_id=1, source_target_pairs={{0,8},{8,0},{1,9},{9,1},{2,10},{10,2},{3,11},{11,3},{4,12},{12,4},... | collective-permute-start | bytes 1179656 | tf_op jit(solution)/shard_map/ppermute | solution.py:288
Sparse Core Ops, SparseCore 0:
  27.9 40.3 reduce-scatter.1

commit v9 on v8

--- a/solution.py
+++ b/solution.py
@@ -17,43 +17,56 @@
 WEIGHT = pl.CostEstimate(flops=10**11, bytes_accessed=2**21, transcendentals=0)
 
 
-def merge_kernel(core_ref, grad_hbm, error_hbm, out_ref, grad, error, sems):
-    parts, _, half = out_ref.shape
+def fetch_half(which, many, half, sources, places, sems):
     copies = []
-    for i in range(parts):
-        at = pl.ds(pl.multiple_of((2 * i + core_ref[0]) * half, half), half)
+    for i in range(many):
+        at = pl.ds(pl.multiple_of((2 * i + which) * half, half), half)
         copies.append(
             [
-                pltpu.make_async_copy(src.at[:, at], dst.at[i], sems.at[j, i])
-                for j, (src, dst) in enumerate(((grad_hbm, grad), (error_hbm, error)))
+                pltpu.make_async_copy(source.at[:, at], place.at[i], sems.at[j, i])
+                for j, (source, place) in enumerate(zip(sources, places))
             ]
         )
         for copy in copies[-1]:
             copy.start()
-    for i in range(parts):
-        for copy in copies[i]:
+    return copies
+
+
+def merge(copies, grad, error, out_ref):
+    for i, pair in enumerate(copies):
+        for copy in pair:
             copy.wait()
         out_ref[i] = (grad[i].astype(F32) + error[i].astype(F32)).astype(BF16)
+
+
+def open_kernel(core_ref, factor_hbm, grad_hbm, error_hbm, slots_hbm, give_ref, mine, grad, error, sems):
+    many, _, half = give_ref.shape
+    core = core_ref[0]
+    at = pl.ds(pl.multiple_of(core * half, half), half)
+    read = pltpu.make_async_copy(factor_hbm.at[:, at], mine, sems.at[2, 0])
+    read.start()
+    copies = fetch_half(1 - core, many, half, (grad_hbm, error_hbm), (grad, error), sems)
+    read.wait()
+    slots = [
+        pltpu.make_async_copy(mine, slots_hbm.at[i], sems.at[3, i]) for i in range(many)
+    ]
+    for copy in slots:
+        copy.start()
+    merge(copies, grad, error, give_ref)
+    for copy in slots:
+        copy.wait()
+
+
+def keep_kernel(core_ref, grad_hbm, error_hbm, keep_ref, grad, error, sems):
+    many, _, half = keep_ref.shape
+    sources, places = (grad_hbm, error_hbm), (grad, error)
+    copies = fetch_half(core_ref[0], many, half, sources, places, sems)
+    merge(copies, grad, error, keep_ref)
 
 
 def pair_kernel(keep_ref, took_ref, out_ref):
     for i in range(out_ref.shape[0]):
         out_ref[i] = (keep_ref[i].astype(F32) + took_ref[i].astype(F32)).T
-
-
-def slots_kernel(core_ref, factor_hbm, out_hbm, mine, sems):
-    many, _, half = out_hbm.shape
-    at = pl.ds(pl.multiple_of(core_ref[0] * half, half), half)
-    read = pltpu.make_async_copy(factor_hbm.at[:, at], mine, sems.at[many])
-    read.start()
-    read.wait()
-    copies = [
-        pltpu.make_async_copy(mine, out_hbm.at[i], sems.at[i]) for i in range(many)
-    ]
-    for copy in copies:
-        copy.start()
-    for copy in copies:
-        copy.wait()
 
 
 def left_kernel(factor_ref, keep_ref, took_ref, out_ref):
@@ -245,23 +258,23 @@
 
     pieces = array((along, height, half), BF16)
 
-    def merge(which, name, cost):
-        return call(
-            merge_kernel, name, pieces, [SMEM, HBM, HBM], VMEM,
-            [pltpu.VMEM(pieces.shape, BF16)] * 2 + [pltpu.SemaphoreType.DMA((2, along))],
-            limit=12, cost=cost,
-        )(which.reshape(1), in_hbm(grad), in_hbm(error))
-
-    give, keep = merge(1 - core, "give", LIGHT), merge(core, "keep", WEIGHT)
+    own_core = core.reshape(1)
+    held = [pltpu.VMEM(pieces.shape, BF16)] * 2
+    slots, give = call(
+        open_kernel, "open", [array((shards, rank, half), BF16), pieces],
+        [SMEM, HBM, HBM, HBM], [HBM, VMEM],
+        [pltpu.VMEM((rank, half), BF16)] + held + [pltpu.SemaphoreType.DMA((4, along))],
+        limit=12, cost=LIGHT,
+    )(own_core, in_hbm(q_in.T), in_hbm(grad), in_hbm(error))
+    keep = call(
+        keep_kernel, "keep", pieces, [SMEM, HBM, HBM], VMEM,
+        held + [pltpu.SemaphoreType.DMA((2, along))], limit=12, cost=WEIGHT,
+    )(own_core, in_hbm(grad), in_hbm(error))
     took = lax.ppermute(give, "core", swap)
     pair = call(pair_kernel, "pair", array((along, half, height), F32), [VMEM, VMEM], limit=12, cost=LIGHT)(keep, took)
     slab = lax.psum_scatter(pair, "y", scatter_dimension=0, tiled=True)[0]
 
-    q_mine = call(
-        slots_kernel, "slots", array((shards, rank, half), BF16), [SMEM, HBM], HBM,
-        [pltpu.VMEM((rank, half), BF16), pltpu.SemaphoreType.DMA((shards + 1,))],
-    )(core.reshape(1), in_hbm(q_in.T))
-    q_all = lax.all_to_all(q_mine, "z", 0, 0)
+    q_all = lax.all_to_all(slots, "z", 0, 0)
     left = call(left_kernel, "left", array((rank, height), F32), [VMEM] * 3, limit=8, cost=WEIGHT)(
         q_all, keep, took
     )

time: 133 us -> 133 us (level)
  waiting for transfers between devices: 8.03 us -> 9.67 us
  Pallas kernels: 15.9 us -> 14.5 us
    all_to_all x1, waiting for transfers between devices: 6.11 us -> 7.75 us  [local(): q_all = lax.all_to_all(slots, 'z', 0, 0)]
    pallas_call x3 -> x2, Pallas kernels: 4.91 us -> 3.47 us  [the longest x1 1.83 us: local(): call(open_kernel, 'open', [array((shards, rank, half), BF16), pieces], [S...]
  transfers between devices with their start and end apart: 5 -> 5, of which waited for: 3 -> 3; matrix products, arithmetic and copies ran while one was open for 0% -> 0% of each run, Pallas kernels for 9% -> 8%
where the time goes in v9:
time: 133 us; the launch traced here: 132 us
  blocking collectives  68.9 us (52%)
  starting transfers between devices  24.7 us (19%)
  Pallas kernels  14.5 us (11%)
  between operations  14.2 us (11%)
  waiting for transfers between devices  9.67 us (7%)
    all_to_all x2, blocking collectives, spread(): lax.all_to_all(jnp.broadcast_to(block[None], (count, *block.shape)), axes...  26.8 us
    all_to_all x1, blocking collectives, local(): lax.all_to_all(left.reshape(replicas, -1, height), REPLICA, 0, 0).sum(0)  20.7 us
    all_to_all x1, blocking collectives, local(): q_mine = (lax.all_to_all(term, 'z', 0, 0).sum(0) / replicas).astype(BF16)  11.1 us
    all_to_all x1, starting transfers between devices, local(): q_all = lax.all_to_all(slots, 'z', 0, 0)  10.9 us
    all_to_all x1, blocking collectives, local(): grams = lax.all_to_all(gram, 'z', 0, 0)  10.4 us
    all_to_all x1, waiting for transfers between devices, local(): q_all = lax.all_to_all(slots, 'z', 0, 0)  7.75 us
    ppermute x1, starting transfers between devices, local(): q_other = lax.ppermute(q_own, 'core', swap)  7.53 us
    pallas_call x1, Pallas kernels, local(): call(factor_kernel, 'factor', [array((rank, height), F32), array((height,...  3.48 us
  transfers between devices with their start and end apart: 5, of which 3 were waited for; matrix products, arithmetic and copies ran while one was open for 0% of the time, Pallas kernels for 8%

profile of v9, /device:TPU:1, one launch (start us, length us, event | category | flops | bytes accessed | tf_op | source)
XLA Modules:
  0.0 132.2 jit_solution(9560926015435068449)
XLA Ops:
  7.2 1.8 %open.1 = (bf16[8,64,384]{2,1,0:T(8,128)(2,1)}, bf16[8,128,384]{2,1,0:T(8,128)(2,1)S(1)}) custom-call(s32[1]{0:T(128)} %bitcast.2.core_ref, bf16[64,768]{1,0:T(8,128)(2,1)} %bitcast.27, bf16[128,6144]{1,0:T(8,128)(2,1)} %bitcast.14, bf16[128,6144]{1,0:T(8,128)(2,1)} %bitcast.18), custom_call_target="tpu_custom_call" | custom-call | tf_op jit(solution)/shard_map/open/pallas_call | solution.py:263
  9.0 10.9 %all-to-all-start = ((bf16[8,64,384]{2,1,0:T(8,128)(2,1)}), bf16[8,64,384]{2,1,0:T(8,128)(2,1)S(1)}, u32[]{:S(2)}, u32[]{:S(2)}) async-start(bf16[8,64,384]{2,1,0:T(8,128)(2,1)} %get-tuple-element.12), calls=%async_computation | async-start | bytes 786432 | tf_op jit(solution)/shard_map/all_to_all | solution.py:277
  19.9 0.0 reduce-scatter.2.cloned.1.call-start
  19.9 2.9 %collective-permute-start = (bf16[8,128,384]{2,1,0:T(8,128)(2,1)S(1)}, bf16[8,128,384]{2,1,0:T(8,128)(2,1)S(1)}, u32[]{:S(2)}, u32[]{:S(2)}) collective-permute-start(bf16[8,128,384]{2,1,0:T(8,128)(2,1)S(1)} %get-tuple-element.13), channel_id=1, source_target_pairs={{0,8},{8,0},{1,9},{9,1},{2,10},{10,2},{3,11},{11,3},{4,12},{12,4},... | collective-permute-start | bytes 2359304 | tf_op jit(solution)/shard_map/ppermute | solution.py:273
  22.8 1.6 %keep.1.keep_ref = bf16[8,128,384]{2,1,0:T(8,128)(2,1)S(1)} custom-call(s32[1]{0:T(128)} %bitcast.2.core_ref, bf16[128,6144]{1,0:T(8,128)(2,1)} %bitcast.15, bf16[128,6144]{1,0:T(8,128)(2,1)} %bitcast.19), custom_call_target="tpu_custom_call" | custom-call | flops 99999997952 | bytes 2097152 | tf_op jit(solution)/shard_map/keep/pallas_call | solution.py:269
  24.4 0.2 collective-permute-done.took_ref
  24.7 1.6 %pair.1 = f32[8,384,128]{2,1,0:T(8,128)} custom-call(bf16[8,128,384]{2,1,0:T(8,128)(2,1)S(1)} %keep.1.keep_ref, bf16[8,128,384]{2,1,0:T(8,128)(2,1)S(1)} %collective-permute-done.took_ref), custom_call_target="tpu_custom_call" | custom-call | tf_op jit(solution)/shard_map/pair/pallas_call | solution.py:274
  26.3 0.0 reduce-scatter.2.cloned.1.call-update
  26.3 7.8 %all-to-all-done.factor_ref = bf16[8,64,384]{2,1,0:T(8,128)(2,1)S(1)} async-done(((bf16[8,64,384]{2,1,0:T(8,128)(2,1)}), bf16[8,64,384]{2,1,0:T(8,128)(2,1)S(1)}, u32[]{:S(2)}, u32[]{:S(2)}) %all-to-all-start) | async-done | bytes 393248 | tf_op jit(solution)/shard_map/all_to_all | solution.py:277
  34.1 0.6 left.1
  34.7 20.7 %all_to_all.35 = f32[64,1,128]{2,1,0:T(1,128)S(1)} all-to-all(f32[64,1,128]{2,1,0:T(1,128)S(1)} %bitcast.24), channel_id=1, replica_groups=mesh['x'=4,'y'=8,'core'=2,'z'=8] {'x','y','core'}, dimensions={0} | all-to-all | bytes 65536 | tf_op jit(solution)/shard_map/all_to_all | solution.py:281
  55.3 0.1 reduce_sum.18
  55.5 13.4 %all_to_all.36 = f32[64,1,128]{2,1,0:T(1,128)S(1)} all-to-all(f32[64,1,128]{2,1,0:T(1,128)S(1)} %broadcast_in_dim.6), channel_id=1, replica_groups=mesh['x'=4,'y'=8,'core'=2,'z'=8] {'x','y','core'}, dimensions={0} | all-to-all | bytes 65536 | tf_op jit(solution)/shard_map/all_to_all | solution.py:244
  68.9 0.0 copy-start.1
  68.9 0.2 gram.1
  69.1 0.0 copy-start
  69.1 10.4 %all_to_all.37.grams_ref = f32[8,32,128]{2,1,0:T(8,128)S(1)} all-to-all(f32[8,32,128]{2,1,0:T(8,128)S(1)} %gram.1), channel_id=1, replica_groups=mesh['x'=4,'y'=8,'core'=2,'z'=8] {'z'}, dimensions={0} | all-to-all | bytes 262144 | tf_op jit(solution)/shard_map/all_to_all | solution.py:287
  79.5 0.0 reduce-scatter.2.cloned.1.call-done
  79.5 3.4 %all-to-all-start.4 = ((f32[4,96,128]{2,1,0:T(8,128)}), f32[4,96,128]{2,1,0:T(8,128)S(1)}, u32[]{:S(2)}, u32[]{:S(2)}) async-start(f32[4,96,128]{2,1,0:T(8,128)} %bitcast.26), calls=%async_computation.5 | async-start | bytes 393216 | tf_op jit(solution)/shard_map/all_to_all | solution.py:295
  82.9 3.5 %factor.1 = (f32[64,128]{1,0:T(8,128)}, bf16[128,64]{1,0:T(8,128)(2,1)S(1)}) custom-call(f32[8,32,128]{2,1,0:T(8,128)S(1)} %all_to_all.37.grams_ref, f32[64,128]{1,0:T(8,128)S(1)} %bitcast.23), custom_call_target="tpu_custom_call" | custom-call | tf_op jit(solution)/shard_map/factor/pallas_call | solution.py:288
  86.4 0.0 copy-start.2
  86.4 1.7 %all-to-all-done.4.slab_ref = f32[4,96,128]{2,1,0:T(8,128)S(1)} async-done(((f32[4,96,128]{2,1,0:T(8,128)}), f32[4,96,128]{2,1,0:T(8,128)S(1)}, u32[]{:S(2)}, u32[]{:S(2)}) %all-to-all-start.4) | async-done | bytes 196640 | tf_op jit(solution)/shard_map/all_to_all | solution.py:295
  88.0 0.3 right.1
  88.3 11.1 %all_to_all.38 = f32[8,48,128]{2,1,0:T(8,128)S(1)} all-to-all(f32[8,48,128]{2,1,0:T(8,128)S(1)} %right.1), channel_id=1, replica_groups=mesh['x'=4,'y'=8,'core'=2,'z'=8] {'z'}, dimensions={0} | all-to-all | bytes 393216 | tf_op jit(solution)/shard_map/all_to_all | solution.py:299
  99.4 0.0 copy-done.2
  99.4 0.1 broadcast_in_dim.7
  99.5 13.4 %all_to_all.39.factor_ref = bf16[32,48,128]{2,1,0:T(8,128)(2,1)S(1)} all-to-all(bf16[32,48,128]{2,1,0:T(8,128)(2,1)S(1)} %broadcast_in_dim.7), channel_id=1, replica_groups=mesh['x'=4,'y'=8,'core'=2,'z'=8] {'x','y'}, dimensions={0} | all-to-all | bytes 786432 | tf_op jit(solution)/shard_map/all_to_all | solution.py:244
  112.8 7.5 %collective-permute-start.1 = (bf16[32,48,128]{2,1,0:T(8,128)(2,1)S(1)}, bf16[32,48,128]{2,1,0:T(8,128)(2,1)}, u32[]{:S(2)}, u32[]{:S(2)}) collective-permute-start(bf16[32,48,128]{2,1,0:T(8,128)(2,1)S(1)} %all_to_all.39.factor_ref), channel_id=1, source_target_pairs={{0,8},{8,0},{1,9},{9,1},{2,10},{10,2},{3,11},{11,3},{4,12},{12,4},... | collective-permute-start | bytes 1179656 | tf_op jit(solution)/shard_map/ppermute | solution.py:301
  120.4 0.1 pad_add_fusion.1.place_ref
  120.4 0.1 pad_add_fusion.place_ref
  120.5 0.0 copy-done.1
  120.5 0.0 copy-done
  120.5 2.6 %own.1 = (bf16[128,6144]{1,0:T(8,128)(2,1)}, bf16[64,384]{1,0:T(8,128)(2,1)S(1)}, bf16[128,64]{1,0:T(8,128)(2,1)S(1)}) custom-call(s32[2]{0:T(128)S(1)} %pad_add_fusion.1.place_ref, bf16[128,64]{1,0:T(8,128)(2,1)} %copy-done.2, bf16[32,48,128]{2,1,0:T(8,128)(2,1)S(1)} %all_to_all.39.factor_ref, bf16[128,6144]{1,0:T(8,128)(2,1)S(1)} %bitcast.16, ...), custom_call_target="tpu_custom_call" | custom-call | tf_op jit(solution)/shard_map/own/pallas_call | solution.py:306
  123.1 0.0 collective-permute-done.1.factor_ref
  123.1 2.3 %other.1 = (bf16[128,6144]{1,0:T(8,128)(2,1)}, bf16[64,768]{1,0:T(8,128)(2,1)}) custom-call(s32[2]{0:T(128)S(1)} %pad_add_fusion.place_ref, bf16[128,64]{1,0:T(8,128)(2,1)S(1)} %get-tuple-element.15.round_ref, bf16[32,48,128]{2,1,0:T(8,128)(2,1)} %collective-permute-done.1.factor_ref, ...), custom_call_target="tpu_custom_call", output_to_operand_aliasing={{0}: (5, {})} | custom-call | tf_op jit(solution)/shard_map/other/pallas_call | solution.py:310
  (3 shorter events, 0.0 us)
Async XLA Ops:
  9.0 25.1 %all-to-all-start = ((bf16[8,64,384]{2,1,0:T(8,128)(2,1)}), bf16[8,64,384]{2,1,0:T(8,128)(2,1)S(1)}, u32[]{:S(2)}, u32[]{:S(2)}) async-start(bf16[8,64,384]{2,1,0:T(8,128)(2,1)} %get-tuple-element.12), calls=%async_computation | async-start | bytes 786432 | tf_op jit(solution)/shard_map/all_to_all | solution.py:277
  19.9 59.6 %reduce-scatter.2.cloned.1.call-start = ((), (), s32[]{:S(2)}) async-start(), calls=%async_computation.8 | async-start | bytes 1769472 | tf_op jit(solution)/shard_map/reduce_scatter | solution.py:275
  19.9 4.8 %collective-permute-start = (bf16[8,128,384]{2,1,0:T(8,128)(2,1)S(1)}, bf16[8,128,384]{2,1,0:T(8,128)(2,1)S(1)}, u32[]{:S(2)}, u32[]{:S(2)}) collective-permute-start(bf16[8,128,384]{2,1,0:T(8,128)(2,1)S(1)} %get-tuple-element.13), channel_id=1, source_target_pairs={{0,8},{8,0},{1,9},{9,1},{2,10},{10,2},{3,11},{11,3},{4,12},{12,4},... | collective-permute-start | bytes 2359304 | tf_op jit(solution)/shard_map/ppermute | solution.py:273
  68.9 51.7 %copy-start.1 = (bf16[1,128,6144]{2,1,0:T(8,128)(2,1)S(1)}, bf16[1,128,6144]{2,1,0:T(8,128)(2,1)}, u32[]{:S(2)}) copy-start(bf16[1,128,6144]{2,1,0:T(8,128)(2,1)} %param.4) | copy-start | bytes 4718596
  69.1 51.4 %copy-start = (bf16[1,128,6144]{2,1,0:T(8,128)(2,1)S(1)}, bf16[1,128,6144]{2,1,0:T(8,128)(2,1)}, u32[]{:S(2)}) copy-start(bf16[1,128,6144]{2,1,0:T(8,128)(2,1)} %param.3) | copy-start | bytes 4718596
  79.5 8.5 %all-to-all-start.4 = ((f32[4,96,128]{2,1,0:T(8,128)}), f32[4,96,128]{2,1,0:T(8,128)S(1)}, u32[]{:S(2)}, u32[]{:S(2)}) async-start(f32[4,96,128]{2,1,0:T(8,128)} %bitcast.26), calls=%async_computation.5 | async-start | bytes 393216 | tf_op jit(solution)/shard_map/all_to_all | solution.py:295
  86.4 13.0 %copy-start.2 = (bf16[128,64]{1,0:T(8,128)(2,1)}, bf16[128,64]{1,0:T(8,128)(2,1)S(1)}, u32[]{:S(2)}) copy-start(bf16[128,64]{1,0:T(8,128)(2,1)S(1)} %get-tuple-element.14.round_ref) | copy-start | bytes 49156
  112.8 10.3 %collective-permute-start.1 = (bf16[32,48,128]{2,1,0:T(8,128)(2,1)S(1)}, bf16[32,48,128]{2,1,0:T(8,128)(2,1)}, u32[]{:S(2)}, u32[]{:S(2)}) collective-permute-start(bf16[32,48,128]{2,1,0:T(8,128)(2,1)S(1)} %all_to_all.39.factor_ref), channel_id=1, source_target_pairs={{0,8},{8,0},{1,9},{9,1},{2,10},{10,2},{3,11},{11,3},{4,12},{12,4},... | collective-permute-start | bytes 1179656 | tf_op jit(solution)/shard_map/ppermute | solution.py:301
Sparse Core Ops, SparseCore 0:
  26.5 40.3 reduce-scatter.1

commit v10 on v9

--- a/solution.py
+++ b/solution.py
@@ -177,18 +177,28 @@
 
 def decode_kernel(first, place_ref, round_ref, factor_ref, grad, error, *rest):
     if first:
-        out_hbm, next_ref, rounded_ref, out, sems = rest
+        out, next_ref, rounded_ref, sems = rest
     else:
-        _, half_ref, out_hbm, next_hbm, next_ref, out, sems = rest
+        early, half_ref, out_hbm, next_hbm, next_ref, out, sems = rest
         rounded_ref = round_ref
     planes, fold, lanes = factor_ref.shape
     rank, half = lanes // 2, out.shape[-1]
     inner = half // (2 * fold)
     parts = planes // inner
     which = place_ref[0]
+
+    def columns(i, core):
+        return pl.ds(pl.multiple_of((2 * i + core) * half, half), half)
+
+    sent = []
     if first:
-        fetch = pltpu.make_async_copy(round_ref, rounded_ref, sems.at[parts])
+        fetch = pltpu.make_async_copy(round_ref, rounded_ref, sems.at[0])
         fetch.start()
+    else:
+        for i in range(parts):
+            to = out_hbm.at[:, columns(i, 1 - which)]
+            sent.append(pltpu.make_async_copy(early.at[i], to, sems.at[parts + 1 + i]))
+            sent[-1].start()
 
     def factor(part):
         pieces = []
@@ -198,7 +208,6 @@
         return jnp.concatenate(pieces, axis=0)
 
     mine = factor(place_ref[1]).astype(F32).T.astype(BF16)
-    sent = []
     if first:
         next_ref[...] = mine
         fetch.wait()
@@ -212,17 +221,18 @@
         decoded = lax.dot_general(
             rounded, factor(i), (((1,), (1,)), ((), ())), preferred_element_type=F32
         )
-        at = pl.ds(pl.multiple_of((2 * i + which) * half, half), half)
+        at = columns(i, which)
         out[i] = (
             grad[:, at].astype(F32) + error[:, at].astype(F32) - decoded
         ).astype(BF16)
-        sent.append(pltpu.make_async_copy(out.at[i], out_hbm.at[:, at], sems.at[i]))
-        sent[-1].start()
+        if not first:
+            sent.append(pltpu.make_async_copy(out.at[i], out_hbm.at[:, at], sems.at[i]))
+            sent[-1].start()
     for copy in sent:
         copy.wait()
 
 
-def call(kernel, name, out_shape, in_specs, out_specs=VMEM, scratch_shapes=(), limit=4, cost=None, aliases=None):
+def call(kernel, name, out_shape, in_specs, out_specs=VMEM, scratch_shapes=(), limit=4, cost=None):
     return pl.pallas_call(
         kernel,
         in_specs=in_specs,
@@ -230,7 +240,6 @@
         out_shape=out_shape,
         scratch_shapes=scratch_shapes,
         cost_estimate=cost,
-        input_output_aliases=aliases or {},
         compiler_params=pltpu.CompilerParams(vmem_limit_bytes=limit * 2**20),
         name=name,
     )
@@ -301,18 +310,21 @@
     q_other = lax.ppermute(q_own, "core", swap)
 
 
-    errors, halves = array((height, width), BF16), array((rank, half), BF16)
-    staged = [pltpu.VMEM(pieces.shape, BF16), pltpu.SemaphoreType.DMA((along + 1,))]
-    new_error, q_half, rounded = call(
-        functools.partial(decode_kernel, True), "own", [errors, halves, p_round],
-        [SMEM, HBM] + [VMEM] * 3, [HBM, VMEM, VMEM], staged, limit=12,
+    early, q_half, rounded = call(
+        functools.partial(decode_kernel, True), "own",
+        [pieces, array((rank, half), BF16), p_round],
+        [SMEM, HBM] + [VMEM] * 3, [VMEM] * 3, [pltpu.SemaphoreType.DMA((1,))], limit=12,
     )(jnp.stack([core, z]), in_hbm(p_round), q_own, grad, error)
     new_error, q_next = call(
         functools.partial(decode_kernel, False), "other",
-        [errors, array((rank, cols), BF16)],
-        [SMEM] + [VMEM] * 4 + [HBM, VMEM], [HBM, HBM],
-        [pltpu.VMEM((rank, cols), BF16)] + staged, limit=12, aliases={5: 0},
-    )(jnp.stack([1 - core, z]), rounded, q_other, grad, error, new_error, q_half)
+        [array((height, width), BF16), array((rank, cols), BF16)],
+        [SMEM] + [VMEM] * 6, [HBM, HBM],
+        [
+            pltpu.VMEM((rank, cols), BF16), pltpu.VMEM(pieces.shape, BF16),
+            pltpu.SemaphoreType.DMA((2 * along + 1,)),
+        ],
+        limit=12,
+    )(jnp.stack([1 - core, z]), rounded, q_other, grad, error, early, q_half)
     return new_error[None], p_factor.T, q_next.T
 
 

time: 133 us -> 133 us (level)
  transfers between devices with their start and end apart: 5 -> 5, of which waited for: 3 -> 3; matrix products, arithmetic and copies ran while one was open for 0% -> 0% of each run, Pallas kernels for 8% -> 7%
where the time goes in v10:
time: 133 us; the launch traced here: 132 us
  blocking collectives  68.9 us (52%)
  starting transfers between devices  24.7 us (19%)
  between operations  14.2 us (11%)
  Pallas kernels  13.9 us (10%)
  waiting for transfers between devices  9.67 us (7%)
    all_to_all x2, blocking collectives, spread(): lax.all_to_all(jnp.broadcast_to(block[None], (count, *block.shape)), axes...  26.8 us
    all_to_all x1, blocking collectives, local(): lax.all_to_all(left.reshape(replicas, -1, height), REPLICA, 0, 0).sum(0)  20.7 us
    all_to_all x1, blocking collectives, local(): q_mine = (lax.all_to_all(term, 'z', 0, 0).sum(0) / replicas).astype(BF16)  11.1 us
    all_to_all x1, starting transfers between devices, local(): q_all = lax.all_to_all(slots, 'z', 0, 0)  10.9 us
    all_to_all x1, blocking collectives, local(): grams = lax.all_to_all(gram, 'z', 0, 0)  10.4 us
    all_to_all x1, waiting for transfers between devices, local(): q_all = lax.all_to_all(slots, 'z', 0, 0)  7.75 us
    ppermute x1, starting transfers between devices, local(): q_other = lax.ppermute(q_own, 'core', swap)  7.53 us
    pallas_call x1, Pallas kernels, local(): call(factor_kernel, 'factor', [array((rank, height), F32), array((height,...  3.48 us
  transfers between devices with their start and end apart: 5, of which 3 were waited for; matrix products, arithmetic and copies ran while one was open for 0% of the time, Pallas kernels for 7%

profile of v10, /device:TPU:1, one launch (start us, length us, event | category | flops | bytes accessed | tf_op | source)
XLA Modules:
  0.0 131.7 jit_solution(4955258352803181880)
XLA Ops:
  7.2 1.8 %open.1 = (bf16[8,64,384]{2,1,0:T(8,128)(2,1)}, bf16[8,128,384]{2,1,0:T(8,128)(2,1)S(1)}) custom-call(s32[1]{0:T(128)} %bitcast.2.core_ref, bf16[64,768]{1,0:T(8,128)(2,1)} %bitcast.26, bf16[128,6144]{1,0:T(8,128)(2,1)} %bitcast.14, bf16[128,6144]{1,0:T(8,128)(2,1)} %bitcast.18), custom_call_target="tpu_custom_call" | custom-call | tf_op jit(solution)/shard_map/open/pallas_call | solution.py:272
  9.0 10.9 %all-to-all-start = ((bf16[8,64,384]{2,1,0:T(8,128)(2,1)}), bf16[8,64,384]{2,1,0:T(8,128)(2,1)S(1)}, u32[]{:S(2)}, u32[]{:S(2)}) async-start(bf16[8,64,384]{2,1,0:T(8,128)(2,1)} %get-tuple-element.12), calls=%async_computation | async-start | bytes 786432 | tf_op jit(solution)/shard_map/all_to_all | solution.py:286
  19.9 0.0 reduce-scatter.2.cloned.1.call-start
  19.9 2.9 %collective-permute-start = (bf16[8,128,384]{2,1,0:T(8,128)(2,1)S(1)}, bf16[8,128,384]{2,1,0:T(8,128)(2,1)S(1)}, u32[]{:S(2)}, u32[]{:S(2)}) collective-permute-start(bf16[8,128,384]{2,1,0:T(8,128)(2,1)S(1)} %get-tuple-element.13), channel_id=1, source_target_pairs={{0,8},{8,0},{1,9},{9,1},{2,10},{10,2},{3,11},{11,3},{4,12},{12,4},... | collective-permute-start | bytes 2359304 | tf_op jit(solution)/shard_map/ppermute | solution.py:282
  22.8 1.6 %keep.1.keep_ref = bf16[8,128,384]{2,1,0:T(8,128)(2,1)S(1)} custom-call(s32[1]{0:T(128)} %bitcast.2.core_ref, bf16[128,6144]{1,0:T(8,128)(2,1)} %bitcast.15, bf16[128,6144]{1,0:T(8,128)(2,1)} %bitcast.19), custom_call_target="tpu_custom_call" | custom-call | flops 99999997952 | bytes 2097152 | tf_op jit(solution)/shard_map/keep/pallas_call | solution.py:278
  24.4 0.2 collective-permute-done.took_ref
  24.7 1.6 %pair.1 = f32[8,384,128]{2,1,0:T(8,128)} custom-call(bf16[8,128,384]{2,1,0:T(8,128)(2,1)S(1)} %keep.1.keep_ref, bf16[8,128,384]{2,1,0:T(8,128)(2,1)S(1)} %collective-permute-done.took_ref), custom_call_target="tpu_custom_call" | custom-call | tf_op jit(solution)/shard_map/pair/pallas_call | solution.py:283
  26.3 0.0 reduce-scatter.2.cloned.1.call-update
  26.3 7.8 %all-to-all-done.factor_ref = bf16[8,64,384]{2,1,0:T(8,128)(2,1)S(1)} async-done(((bf16[8,64,384]{2,1,0:T(8,128)(2,1)}), bf16[8,64,384]{2,1,0:T(8,128)(2,1)S(1)}, u32[]{:S(2)}, u32[]{:S(2)}) %all-to-all-start) | async-done | bytes 393248 | tf_op jit(solution)/shard_map/all_to_all | solution.py:286
  34.1 0.6 left.1
  34.7 20.7 %all_to_all.35 = f32[64,1,128]{2,1,0:T(1,128)S(1)} all-to-all(f32[64,1,128]{2,1,0:T(1,128)S(1)} %bitcast.24), channel_id=1, replica_groups=mesh['x'=4,'y'=8,'core'=2,'z'=8] {'x','y','core'}, dimensions={0} | all-to-all | bytes 65536 | tf_op jit(solution)/shard_map/all_to_all | solution.py:290
  55.3 0.1 reduce_sum.18
  55.5 13.4 %all_to_all.36 = f32[64,1,128]{2,1,0:T(1,128)S(1)} all-to-all(f32[64,1,128]{2,1,0:T(1,128)S(1)} %broadcast_in_dim.6), channel_id=1, replica_groups=mesh['x'=4,'y'=8,'core'=2,'z'=8] {'x','y','core'}, dimensions={0} | all-to-all | bytes 65536 | tf_op jit(solution)/shard_map/all_to_all | solution.py:253
  68.9 0.0 copy-start.1
  68.9 0.2 gram.1
  69.1 0.0 copy-start
  69.1 10.4 %all_to_all.37.grams_ref = f32[8,32,128]{2,1,0:T(8,128)S(1)} all-to-all(f32[8,32,128]{2,1,0:T(8,128)S(1)} %gram.1), channel_id=1, replica_groups=mesh['x'=4,'y'=8,'core'=2,'z'=8] {'z'}, dimensions={0} | all-to-all | bytes 262144 | tf_op jit(solution)/shard_map/all_to_all | solution.py:296
  79.5 0.0 reduce-scatter.2.cloned.1.call-done
  79.5 3.4 %all-to-all-start.4 = ((f32[4,96,128]{2,1,0:T(8,128)}), f32[4,96,128]{2,1,0:T(8,128)S(1)}, u32[]{:S(2)}, u32[]{:S(2)}) async-start(f32[4,96,128]{2,1,0:T(8,128)} %bitcast.25), calls=%async_computation.5 | async-start | bytes 393216 | tf_op jit(solution)/shard_map/all_to_all | solution.py:304
  82.9 3.5 %factor.1 = (f32[64,128]{1,0:T(8,128)}, bf16[128,64]{1,0:T(8,128)(2,1)S(1)}) custom-call(f32[8,32,128]{2,1,0:T(8,128)S(1)} %all_to_all.37.grams_ref, f32[64,128]{1,0:T(8,128)S(1)} %bitcast.23), custom_call_target="tpu_custom_call" | custom-call | tf_op jit(solution)/shard_map/factor/pallas_call | solution.py:297
  86.4 0.0 copy-start.2
  86.4 1.7 %all-to-all-done.4.slab_ref = f32[4,96,128]{2,1,0:T(8,128)S(1)} async-done(((f32[4,96,128]{2,1,0:T(8,128)}), f32[4,96,128]{2,1,0:T(8,128)S(1)}, u32[]{:S(2)}, u32[]{:S(2)}) %all-to-all-start.4) | async-done | bytes 196640 | tf_op jit(solution)/shard_map/all_to_all | solution.py:304
  88.0 0.3 right.1
  88.3 11.1 %all_to_all.38 = f32[8,48,128]{2,1,0:T(8,128)S(1)} all-to-all(f32[8,48,128]{2,1,0:T(8,128)S(1)} %right.1), channel_id=1, replica_groups=mesh['x'=4,'y'=8,'core'=2,'z'=8] {'z'}, dimensions={0} | all-to-all | bytes 393216 | tf_op jit(solution)/shard_map/all_to_all | solution.py:308
  99.4 0.0 copy-done.2
  99.4 0.1 broadcast_in_dim.7
  99.5 13.4 %all_to_all.39.factor_ref = bf16[32,48,128]{2,1,0:T(8,128)(2,1)S(1)} all-to-all(bf16[32,48,128]{2,1,0:T(8,128)(2,1)S(1)} %broadcast_in_dim.7), channel_id=1, replica_groups=mesh['x'=4,'y'=8,'core'=2,'z'=8] {'x','y'}, dimensions={0} | all-to-all | bytes 786432 | tf_op jit(solution)/shard_map/all_to_all | solution.py:253
  112.8 7.5 %collective-permute-start.1 = (bf16[32,48,128]{2,1,0:T(8,128)(2,1)S(1)}, bf16[32,48,128]{2,1,0:T(8,128)(2,1)}, u32[]{:S(2)}, u32[]{:S(2)}) collective-permute-start(bf16[32,48,128]{2,1,0:T(8,128)(2,1)S(1)} %all_to_all.39.factor_ref), channel_id=1, source_target_pairs={{0,8},{8,0},{1,9},{9,1},{2,10},{10,2},{3,11},{11,3},{4,12},{12,4},... | collective-permute-start | bytes 1179656 | tf_op jit(solution)/shard_map/ppermute | solution.py:310
  120.4 0.1 pad_add_fusion.1.place_ref
  120.4 0.1 pad_add_fusion.place_ref
  120.5 0.0 copy-done.1
  120.5 0.0 copy-done
  120.5 1.8 %own.1 = (bf16[8,128,384]{2,1,0:T(8,128)(2,1)S(1)}, bf16[64,384]{1,0:T(8,128)(2,1)S(1)}, bf16[128,64]{1,0:T(8,128)(2,1)S(1)}) custom-call(s32[2]{0:T(128)S(1)} %pad_add_fusion.1.place_ref, bf16[128,64]{1,0:T(8,128)(2,1)} %copy-done.2, bf16[32,48,128]{2,1,0:T(8,128)(2,1)S(1)} %all_to_all.39.factor_ref, bf16[128,6144]{1,0:T(8,128)(2,1)S(1)} %bitcast.16, ...), custom_call_target="tpu_custom_call" | custom-call | tf_op jit(solution)/shard_map/own/pallas_call | solution.py:313
  122.4 0.0 collective-permute-done.1.factor_ref
  122.4 2.4 %other.1 = (bf16[128,6144]{1,0:T(8,128)(2,1)}, bf16[64,768]{1,0:T(8,128)(2,1)}) custom-call(s32[2]{0:T(128)S(1)} %pad_add_fusion.place_ref, bf16[128,64]{1,0:T(8,128)(2,1)S(1)} %get-tuple-element.15.round_ref, bf16[32,48,128]{2,1,0:T(8,128)(2,1)} %collective-permute-done.1.factor_ref, bf16[128,6144]{1,0:T(8,128)(2,1)S(1)} %bitcast.17, ...), custom_call_target="tpu_custom_call" | custom-call | tf_op jit(solution)/shard_map/other/pallas_call | solution.py:318
  (3 shorter events, 0.0 us)
Async XLA Ops:
  9.0 25.1 %all-to-all-start = ((bf16[8,64,384]{2,1,0:T(8,128)(2,1)}), bf16[8,64,384]{2,1,0:T(8,128)(2,1)S(1)}, u32[]{:S(2)}, u32[]{:S(2)}) async-start(bf16[8,64,384]{2,1,0:T(8,128)(2,1)} %get-tuple-element.12), calls=%async_computation | async-start | bytes 786432 | tf_op jit(solution)/shard_map/all_to_all | solution.py:286
  19.9 59.6 %reduce-scatter.2.cloned.1.call-start = ((), (), s32[]{:S(2)}) async-start(), calls=%async_computation.8 | async-start | bytes 1769472 | tf_op jit(solution)/shard_map/reduce_scatter | solution.py:284
  19.9 4.8 %collective-permute-start = (bf16[8,128,384]{2,1,0:T(8,128)(2,1)S(1)}, bf16[8,128,384]{2,1,0:T(8,128)(2,1)S(1)}, u32[]{:S(2)}, u32[]{:S(2)}) collective-permute-start(bf16[8,128,384]{2,1,0:T(8,128)(2,1)S(1)} %get-tuple-element.13), channel_id=1, source_target_pairs={{0,8},{8,0},{1,9},{9,1},{2,10},{10,2},{3,11},{11,3},{4,12},{12,4},... | collective-permute-start | bytes 2359304 | tf_op jit(solution)/shard_map/ppermute | solution.py:282
  68.9 51.7 %copy-start.1 = (bf16[1,128,6144]{2,1,0:T(8,128)(2,1)S(1)}, bf16[1,128,6144]{2,1,0:T(8,128)(2,1)}, u32[]{:S(2)}) copy-start(bf16[1,128,6144]{2,1,0:T(8,128)(2,1)} %param.4) | copy-start | bytes 4718596
  69.1 51.4 %copy-start = (bf16[1,128,6144]{2,1,0:T(8,128)(2,1)S(1)}, bf16[1,128,6144]{2,1,0:T(8,128)(2,1)}, u32[]{:S(2)}) copy-start(bf16[1,128,6144]{2,1,0:T(8,128)(2,1)} %param.3) | copy-start | bytes 4718596
  79.5 8.5 %all-to-all-start.4 = ((f32[4,96,128]{2,1,0:T(8,128)}), f32[4,96,128]{2,1,0:T(8,128)S(1)}, u32[]{:S(2)}, u32[]{:S(2)}) async-start(f32[4,96,128]{2,1,0:T(8,128)} %bitcast.25), calls=%async_computation.5 | async-start | bytes 393216 | tf_op jit(solution)/shard_map/all_to_all | solution.py:304
  86.4 13.0 %copy-start.2 = (bf16[128,64]{1,0:T(8,128)(2,1)}, bf16[128,64]{1,0:T(8,128)(2,1)S(1)}, u32[]{:S(2)}) copy-start(bf16[128,64]{1,0:T(8,128)(2,1)S(1)} %get-tuple-element.14.round_ref) | copy-start | bytes 49156
  112.8 9.5 %collective-permute-start.1 = (bf16[32,48,128]{2,1,0:T(8,128)(2,1)S(1)}, bf16[32,48,128]{2,1,0:T(8,128)(2,1)}, u32[]{:S(2)}, u32[]{:S(2)}) collective-permute-start(bf16[32,48,128]{2,1,0:T(8,128)(2,1)S(1)} %all_to_all.39.factor_ref), channel_id=1, source_target_pairs={{0,8},{8,0},{1,9},{9,1},{2,10},{10,2},{3,11},{11,3},{4,12},{12,4},... | collective-permute-start | bytes 1179656 | tf_op jit(solution)/shard_map/ppermute | solution.py:310
Sparse Core Ops, SparseCore 0:
  26.5 40.3 reduce-scatter.1

commit v11 on v10

--- a/solution.py
+++ b/solution.py
@@ -13,6 +13,7 @@
 HBM = pl.BlockSpec(memory_space=pltpu.HBM)
 PLANE = ("x", "y")
 REPLICA = ("x", "y", "core")
+SPREAD = ("core", "y", "x")
 LIGHT = pl.CostEstimate(flops=0, bytes_accessed=0, transcendentals=0)
 WEIGHT = pl.CostEstimate(flops=10**11, bytes_accessed=2**21, transcendentals=0)
 
@@ -175,7 +176,7 @@
         out_ref[i] = packed
 
 
-def decode_kernel(first, place_ref, round_ref, factor_ref, grad, error, *rest):
+def decode_kernel(first, core_ref, z_ref, round_ref, factor_ref, grad, error, *rest):
     if first:
         out, next_ref, rounded_ref, sems = rest
     else:
@@ -185,7 +186,7 @@
     rank, half = lanes // 2, out.shape[-1]
     inner = half // (2 * fold)
     parts = planes // inner
-    which = place_ref[0]
+    which = core_ref[0] if first else 1 - core_ref[0]
 
     def columns(i, core):
         return pl.ds(pl.multiple_of((2 * i + core) * half, half), half)
@@ -207,7 +208,7 @@
             pieces += [piece[:, :rank], piece[:, rank:]]
         return jnp.concatenate(pieces, axis=0)
 
-    mine = factor(place_ref[1]).astype(F32).T.astype(BF16)
+    mine = factor(z_ref[0]).astype(F32).T.astype(BF16)
     if first:
         next_ref[...] = mine
         fetch.wait()
@@ -287,8 +288,8 @@
     left = call(left_kernel, "left", array((rank, height), F32), [VMEM] * 3, limit=8, cost=WEIGHT)(
         q_all, keep, took
     )
-    left_row = lax.all_to_all(left.reshape(replicas, -1, height), REPLICA, 0, 0).sum(0)
-    left_sum = spread(left_row, REPLICA, replicas).reshape(rank, height)
+    left_row = lax.all_to_all(left.reshape(replicas, -1, height), SPREAD, 0, 0).sum(0)
+    left_sum = spread(left_row, SPREAD, replicas).reshape(rank, height)
 
     gram = call(gram_kernel, "gram", array((shards, rank // 2, 2 * rank), F32), [VMEM])(
         left_sum
@@ -313,18 +314,18 @@
     early, q_half, rounded = call(
         functools.partial(decode_kernel, True), "own",
         [pieces, array((rank, half), BF16), p_round],
-        [SMEM, HBM] + [VMEM] * 3, [VMEM] * 3, [pltpu.SemaphoreType.DMA((1,))], limit=12,
-    )(jnp.stack([core, z]), in_hbm(p_round), q_own, grad, error)
+        [SMEM, SMEM, HBM] + [VMEM] * 3, [VMEM] * 3, [pltpu.SemaphoreType.DMA((1,))], limit=12,
+    )(own_core, z.reshape(1), in_hbm(p_round), q_own, grad, error)
     new_error, q_next = call(
         functools.partial(decode_kernel, False), "other",
         [array((height, width), BF16), array((rank, cols), BF16)],
-        [SMEM] + [VMEM] * 6, [HBM, HBM],
+        [SMEM, SMEM] + [VMEM] * 6, [HBM, HBM],
         [
             pltpu.VMEM((rank, cols), BF16), pltpu.VMEM(pieces.shape, BF16),
             pltpu.SemaphoreType.DMA((2 * along + 1,)),
         ],
         limit=12,
-    )(jnp.stack([1 - core, z]), rounded, q_other, grad, error, early, q_half)
+    )(own_core, z.reshape(1), rounded, q_other, grad, error, early, q_half)
     return new_error[None], p_factor.T, q_next.T
 
 

time: 133 us -> 133 us (level)
  transfers between devices with their start and end apart: 5 -> 5, of which waited for: 3 -> 4; matrix products, arithmetic and copies ran while one was open for 0% -> 0% of each run, Pallas kernels for 7% -> 7%
where the time goes in v11:
time: 133 us; the launch traced here: 132 us
  blocking collectives  69.4 us (52%)
  starting transfers between devices  25.2 us (19%)
  between operations  14.2 us (11%)
  Pallas kernels  13.4 us (10%)
  waiting for transfers between devices  9.8 us (7%)
    all_to_all x2, blocking collectives, spread(): lax.all_to_all(jnp.broadcast_to(block[None], (count, *block.shape)), axes...  27 us
    all_to_all x1, blocking collectives, local(): lax.all_to_all(left.reshape(replicas, -1, height), SPREAD, 0, 0).sum(0)  20.5 us
    all_to_all x1, blocking collectives, local(): q_mine = (lax.all_to_all(term, 'z', 0, 0).sum(0) / replicas).astype(BF16)  11.1 us
    all_to_all x1, starting transfers between devices, local(): q_all = lax.all_to_all(slots, 'z', 0, 0)  10.9 us
    all_to_all x1, blocking collectives, local(): grams = lax.all_to_all(gram, 'z', 0, 0)  10.7 us
    ppermute x1, starting transfers between devices, local(): q_other = lax.ppermute(q_own, 'core', swap)  8.03 us
    all_to_all x1, waiting for transfers between devices, local(): q_all = lax.all_to_all(slots, 'z', 0, 0)  7.75 us
    pallas_call x1, Pallas kernels, local(): call(factor_kernel, 'factor', [array((rank, height), F32), array((height,...  3.48 us
  transfers between devices with their start and end apart: 5, of which 4 were waited for; matrix products, arithmetic and copies ran while one was open for 0% of the time, Pallas kernels for 7%

profile of v11, /device:TPU:1, one launch (start us, length us, event | category | flops | bytes accessed | tf_op | source)
XLA Modules:
  0.0 132.1 jit_solution(13141044120620908158)
XLA Ops:
  7.2 1.8 %open.1 = (bf16[8,64,384]{2,1,0:T(8,128)(2,1)}, bf16[8,128,384]{2,1,0:T(8,128)(2,1)S(1)}) custom-call(s32[1]{0:T(128)} %bitcast.core_ref, bf16[64,768]{1,0:T(8,128)(2,1)} %bitcast.25, bf16[128,6144]{1,0:T(8,128)(2,1)} %bitcast.13, bf16[128,6144]{1,0:T(8,128)(2,1)} %bitcast.17), custom_call_target="tpu_custom_call" | custom-call | tf_op jit(solution)/shard_map/open/pallas_call | solution.py:273
  9.0 10.9 %all-to-all-start = ((bf16[8,64,384]{2,1,0:T(8,128)(2,1)}), bf16[8,64,384]{2,1,0:T(8,128)(2,1)S(1)}, u32[]{:S(2)}, u32[]{:S(2)}) async-start(bf16[8,64,384]{2,1,0:T(8,128)(2,1)} %get-tuple-element.12), calls=%async_computation | async-start | bytes 786432 | tf_op jit(solution)/shard_map/all_to_all | solution.py:287
  19.9 0.0 reduce-scatter.2.cloned.1.call-start
  19.9 2.9 %collective-permute-start = (bf16[8,128,384]{2,1,0:T(8,128)(2,1)S(1)}, bf16[8,128,384]{2,1,0:T(8,128)(2,1)S(1)}, u32[]{:S(2)}, u32[]{:S(2)}) collective-permute-start(bf16[8,128,384]{2,1,0:T(8,128)(2,1)S(1)} %get-tuple-element.13), channel_id=1, source_target_pairs={{0,8},{8,0},{1,9},{9,1},{2,10},{10,2},{3,11},{11,3},{4,12},{12,4},... | collective-permute-start | bytes 2359304 | tf_op jit(solution)/shard_map/ppermute | solution.py:283
  22.8 1.6 %keep.1.keep_ref = bf16[8,128,384]{2,1,0:T(8,128)(2,1)S(1)} custom-call(s32[1]{0:T(128)} %bitcast.core_ref, bf16[128,6144]{1,0:T(8,128)(2,1)} %bitcast.14, bf16[128,6144]{1,0:T(8,128)(2,1)} %bitcast.18), custom_call_target="tpu_custom_call" | custom-call | flops 99999997952 | bytes 2097152 | tf_op jit(solution)/shard_map/keep/pallas_call | solution.py:279
  24.4 0.2 collective-permute-done.took_ref
  24.7 1.6 %pair.1 = f32[8,384,128]{2,1,0:T(8,128)} custom-call(bf16[8,128,384]{2,1,0:T(8,128)(2,1)S(1)} %keep.1.keep_ref, bf16[8,128,384]{2,1,0:T(8,128)(2,1)S(1)} %collective-permute-done.took_ref), custom_call_target="tpu_custom_call" | custom-call | tf_op jit(solution)/shard_map/pair/pallas_call | solution.py:284
  26.3 0.0 reduce-scatter.2.cloned.1.call-update
  26.3 7.8 %all-to-all-done.factor_ref = bf16[8,64,384]{2,1,0:T(8,128)(2,1)S(1)} async-done(((bf16[8,64,384]{2,1,0:T(8,128)(2,1)}), bf16[8,64,384]{2,1,0:T(8,128)(2,1)S(1)}, u32[]{:S(2)}, u32[]{:S(2)}) %all-to-all-start) | async-done | bytes 393248 | tf_op jit(solution)/shard_map/all_to_all | solution.py:287
  34.1 0.6 left.1
  34.7 20.5 %all_to_all.35 = f32[64,1,128]{2,1,0:T(1,128)S(1)} all-to-all(f32[64,1,128]{2,1,0:T(1,128)S(1)} %bitcast.23), channel_id=1, replica_groups=mesh['x'=4,'y'=8,'core'=2,'z'=8] {'core','y','x'}, dimensions={0} | all-to-all | bytes 65536 | tf_op jit(solution)/shard_map/all_to_all | solution.py:291
  55.2 0.1 reduce_sum.18
  55.3 13.2 %all_to_all.36 = f32[64,1,128]{2,1,0:T(1,128)S(1)} all-to-all(f32[64,1,128]{2,1,0:T(1,128)S(1)} %broadcast_in_dim.6), channel_id=1, replica_groups=mesh['x'=4,'y'=8,'core'=2,'z'=8] {'core','y','x'}, dimensions={0} | all-to-all | bytes 65536 | tf_op jit(solution)/shard_map/all_to_all | solution.py:254
  68.5 0.0 copy-start.1
  68.5 0.2 gram.1
  68.8 0.0 copy-start
  68.8 10.7 %all_to_all.37.grams_ref = f32[8,32,128]{2,1,0:T(8,128)S(1)} all-to-all(f32[8,32,128]{2,1,0:T(8,128)S(1)} %gram.1), channel_id=1, replica_groups=mesh['x'=4,'y'=8,'core'=2,'z'=8] {'z'}, dimensions={0} | all-to-all | bytes 262144 | tf_op jit(solution)/shard_map/all_to_all | solution.py:297
  79.5 0.0 reduce-scatter.2.cloned.1.call-done
  79.5 3.4 %all-to-all-start.4 = ((f32[4,96,128]{2,1,0:T(8,128)}), f32[4,96,128]{2,1,0:T(8,128)S(1)}, u32[]{:S(2)}, u32[]{:S(2)}) async-start(f32[4,96,128]{2,1,0:T(8,128)} %bitcast.24), calls=%async_computation.5 | async-start | bytes 393216 | tf_op jit(solution)/shard_map/all_to_all | solution.py:305
  82.9 3.5 %factor.1 = (f32[64,128]{1,0:T(8,128)}, bf16[128,64]{1,0:T(8,128)(2,1)S(1)}) custom-call(f32[8,32,128]{2,1,0:T(8,128)S(1)} %all_to_all.37.grams_ref, f32[64,128]{1,0:T(8,128)S(1)} %bitcast.22), custom_call_target="tpu_custom_call" | custom-call | tf_op jit(solution)/shard_map/factor/pallas_call | solution.py:298
  86.3 0.0 copy-start.2
  86.4 1.7 %all-to-all-done.4.slab_ref = f32[4,96,128]{2,1,0:T(8,128)S(1)} async-done(((f32[4,96,128]{2,1,0:T(8,128)}), f32[4,96,128]{2,1,0:T(8,128)S(1)}, u32[]{:S(2)}, u32[]{:S(2)}) %all-to-all-start.4) | async-done | bytes 196640 | tf_op jit(solution)/shard_map/all_to_all | solution.py:305
  88.0 0.3 right.1
  88.3 11.1 %all_to_all.38 = f32[8,48,128]{2,1,0:T(8,128)S(1)} all-to-all(f32[8,48,128]{2,1,0:T(8,128)S(1)} %right.1), channel_id=1, replica_groups=mesh['x'=4,'y'=8,'core'=2,'z'=8] {'z'}, dimensions={0} | all-to-all | bytes 393216 | tf_op jit(solution)/shard_map/all_to_all | solution.py:309
  99.4 0.0 copy-done.2
  99.5 0.1 broadcast_in_dim.7
  99.5 13.9 %all_to_all.39.factor_ref = bf16[32,48,128]{2,1,0:T(8,128)(2,1)S(1)} all-to-all(bf16[32,48,128]{2,1,0:T(8,128)(2,1)S(1)} %broadcast_in_dim.7), channel_id=1, replica_groups=mesh['x'=4,'y'=8,'core'=2,'z'=8] {'x','y'}, dimensions={0} | all-to-all | bytes 786432 | tf_op jit(solution)/shard_map/all_to_all | solution.py:254
  113.4 8.0 %collective-permute-start.1 = (bf16[32,48,128]{2,1,0:T(8,128)(2,1)S(1)}, bf16[32,48,128]{2,1,0:T(8,128)(2,1)}, u32[]{:S(2)}, u32[]{:S(2)}) collective-permute-start(bf16[32,48,128]{2,1,0:T(8,128)(2,1)S(1)} %all_to_all.39.factor_ref), channel_id=1, source_target_pairs={{0,8},{8,0},{1,9},{9,1},{2,10},{10,2},{3,11},{11,3},{4,12},{12,4},... | collective-permute-start | bytes 1179656 | tf_op jit(solution)/shard_map/ppermute | solution.py:311
  121.4 0.0 copy-done.1
  121.4 0.0 copy-done
  121.4 1.3 own.1
  122.7 0.1 collective-permute-done.1.factor_ref
  122.9 2.4 %other.1 = (bf16[128,6144]{1,0:T(8,128)(2,1)}, bf16[64,768]{1,0:T(8,128)(2,1)}) custom-call(s32[1]{0:T(128)} %bitcast.core_ref, s32[1]{0:T(128)} %bitcast.1.z_ref, bf16[128,64]{1,0:T(8,128)(2,1)S(1)} %get-tuple-element.15.round_ref, bf16[32,48,128]{2,1,0:T(8,128)(2,1)} %collective-permute-done.1.factor_ref, bf16[128,6144]{1,0:T(8,128)(2,1)S(1)} %bitcast.16, ...), custom_call_target="tpu_custom_call" | custom-call | tf_op jit(solution)/shard_map/other/pallas_call | solution.py:319
  (3 shorter events, 0.0 us)
Async XLA Ops:
  9.0 25.1 %all-to-all-start = ((bf16[8,64,384]{2,1,0:T(8,128)(2,1)}), bf16[8,64,384]{2,1,0:T(8,128)(2,1)S(1)}, u32[]{:S(2)}, u32[]{:S(2)}) async-start(bf16[8,64,384]{2,1,0:T(8,128)(2,1)} %get-tuple-element.12), calls=%async_computation | async-start | bytes 786432 | tf_op jit(solution)/shard_map/all_to_all | solution.py:287
  19.9 59.6 %reduce-scatter.2.cloned.1.call-start = ((), (), s32[]{:S(2)}) async-start(), calls=%async_computation.8 | async-start | bytes 1769472 | tf_op jit(solution)/shard_map/reduce_scatter | solution.py:285
  19.9 4.8 %collective-permute-start = (bf16[8,128,384]{2,1,0:T(8,128)(2,1)S(1)}, bf16[8,128,384]{2,1,0:T(8,128)(2,1)S(1)}, u32[]{:S(2)}, u32[]{:S(2)}) collective-permute-start(bf16[8,128,384]{2,1,0:T(8,128)(2,1)S(1)} %get-tuple-element.13), channel_id=1, source_target_pairs={{0,8},{8,0},{1,9},{9,1},{2,10},{10,2},{3,11},{11,3},{4,12},{12,4},... | collective-permute-start | bytes 2359304 | tf_op jit(solution)/shard_map/ppermute | solution.py:283
  68.5 52.9 %copy-start.1 = (bf16[1,128,6144]{2,1,0:T(8,128)(2,1)S(1)}, bf16[1,128,6144]{2,1,0:T(8,128)(2,1)}, u32[]{:S(2)}) copy-start(bf16[1,128,6144]{2,1,0:T(8,128)(2,1)} %param.4) | copy-start | bytes 4718596
  68.8 52.7 %copy-start = (bf16[1,128,6144]{2,1,0:T(8,128)(2,1)S(1)}, bf16[1,128,6144]{2,1,0:T(8,128)(2,1)}, u32[]{:S(2)}) copy-start(bf16[1,128,6144]{2,1,0:T(8,128)(2,1)} %param.3) | copy-start | bytes 4718596
  79.5 8.5 %all-to-all-start.4 = ((f32[4,96,128]{2,1,0:T(8,128)}), f32[4,96,128]{2,1,0:T(8,128)S(1)}, u32[]{:S(2)}, u32[]{:S(2)}) async-start(f32[4,96,128]{2,1,0:T(8,128)} %bitcast.24), calls=%async_computation.5 | async-start | bytes 393216 | tf_op jit(solution)/shard_map/all_to_all | solution.py:305
  86.3 13.1 %copy-start.2 = (bf16[128,64]{1,0:T(8,128)(2,1)}, bf16[128,64]{1,0:T(8,128)(2,1)S(1)}, u32[]{:S(2)}) copy-start(bf16[128,64]{1,0:T(8,128)(2,1)S(1)} %get-tuple-element.14.round_ref) | copy-start | bytes 49156
  113.4 9.5 %collective-permute-start.1 = (bf16[32,48,128]{2,1,0:T(8,128)(2,1)S(1)}, bf16[32,48,128]{2,1,0:T(8,128)(2,1)}, u32[]{:S(2)}, u32[]{:S(2)}) collective-permute-start(bf16[32,48,128]{2,1,0:T(8,128)(2,1)S(1)} %all_to_all.39.factor_ref), channel_id=1, source_target_pairs={{0,8},{8,0},{1,9},{9,1},{2,10},{10,2},{3,11},{11,3},{4,12},{12,4},... | collective-permute-start | bytes 1179656 | tf_op jit(solution)/shard_map/ppermute | solution.py:311
Sparse Core Ops, SparseCore 0:
  26.5 40.4 reduce-scatter.1

commit v12 on v11

--- a/solution.py
+++ b/solution.py
@@ -13,7 +13,6 @@
 HBM = pl.BlockSpec(memory_space=pltpu.HBM)
 PLANE = ("x", "y")
 REPLICA = ("x", "y", "core")
-SPREAD = ("core", "y", "x")
 LIGHT = pl.CostEstimate(flops=0, bytes_accessed=0, transcendentals=0)
 WEIGHT = pl.CostEstimate(flops=10**11, bytes_accessed=2**21, transcendentals=0)
 
@@ -288,8 +287,8 @@
     left = call(left_kernel, "left", array((rank, height), F32), [VMEM] * 3, limit=8, cost=WEIGHT)(
         q_all, keep, took
     )
-    left_row = lax.all_to_all(left.reshape(replicas, -1, height), SPREAD, 0, 0).sum(0)
-    left_sum = spread(left_row, SPREAD, replicas).reshape(rank, height)
+    left_row = lax.all_to_all(left.reshape(replicas, -1, height), REPLICA, 0, 0).sum(0)
+    left_sum = spread(left_row, REPLICA, replicas).reshape(rank, height)
 
     gram = call(gram_kernel, "gram", array((shards, rank // 2, 2 * rank), F32), [VMEM])(
         left_sum

time: 133 us -> 132 us (level)
  no operation moved by 1% of the time
where the time goes in v12:
time: 132 us; the launch traced here: 131 us
  blocking collectives  68.9 us (52%)
  starting transfers between devices  24.7 us (19%)
  between operations  14.2 us (11%)
  Pallas kernels  13.4 us (10%)
  waiting for transfers between devices  9.8 us (7%)
    all_to_all x2, blocking collectives, spread(): lax.all_to_all(jnp.broadcast_to(block[None], (count, *block.shape)), axes...  26.8 us
    all_to_all x1, blocking collectives, local(): lax.all_to_all(left.reshape(replicas, -1, height), REPLICA, 0, 0).sum(0)  20.7 us
    all_to_all x1, blocking collectives, local(): q_mine = (lax.all_to_all(term, 'z', 0, 0).sum(0) / replicas).astype(BF16)  11.1 us
    all_to_all x1, starting transfers between devices, local(): q_all = lax.all_to_all(slots, 'z', 0, 0)  10.9 us
    all_to_all x1, blocking collectives, local(): grams = lax.all_to_all(gram, 'z', 0, 0)  10.4 us
    all_to_all x1, waiting for transfers between devices, local(): q_all = lax.all_to_all(slots, 'z', 0, 0)  7.75 us
    ppermute x1, starting transfers between devices, local(): q_other = lax.ppermute(q_own, 'core', swap)  7.53 us
    pallas_call x1, Pallas kernels, local(): call(factor_kernel, 'factor', [array((rank, height), F32), array((height,...  3.48 us
  transfers between devices with their start and end apart: 5, of which 4 were waited for; matrix products, arithmetic and copies ran while one was open for 0% of the time, Pallas kernels for 7%

profile of v12, /device:TPU:1, one launch (start us, length us, event | category | flops | bytes accessed | tf_op | source)
XLA Modules:
  0.0 131.1 jit_solution(18122777961901604947)
XLA Ops:
  7.2 1.8 %open.1 = (bf16[8,64,384]{2,1,0:T(8,128)(2,1)}, bf16[8,128,384]{2,1,0:T(8,128)(2,1)S(1)}) custom-call(s32[1]{0:T(128)} %bitcast.core_ref, bf16[64,768]{1,0:T(8,128)(2,1)} %bitcast.25, bf16[128,6144]{1,0:T(8,128)(2,1)} %bitcast.13, bf16[128,6144]{1,0:T(8,128)(2,1)} %bitcast.17), custom_call_target="tpu_custom_call" | custom-call | tf_op jit(solution)/shard_map/open/pallas_call | solution.py:272
  9.0 10.9 %all-to-all-start = ((bf16[8,64,384]{2,1,0:T(8,128)(2,1)}), bf16[8,64,384]{2,1,0:T(8,128)(2,1)S(1)}, u32[]{:S(2)}, u32[]{:S(2)}) async-start(bf16[8,64,384]{2,1,0:T(8,128)(2,1)} %get-tuple-element.12), calls=%async_computation | async-start | bytes 786432 | tf_op jit(solution)/shard_map/all_to_all | solution.py:286
  19.9 0.0 reduce-scatter.2.cloned.1.call-start
  19.9 2.9 %collective-permute-start = (bf16[8,128,384]{2,1,0:T(8,128)(2,1)S(1)}, bf16[8,128,384]{2,1,0:T(8,128)(2,1)S(1)}, u32[]{:S(2)}, u32[]{:S(2)}) collective-permute-start(bf16[8,128,384]{2,1,0:T(8,128)(2,1)S(1)} %get-tuple-element.13), channel_id=1, source_target_pairs={{0,8},{8,0},{1,9},{9,1},{2,10},{10,2},{3,11},{11,3},{4,12},{12,4},... | collective-permute-start | bytes 2359304 | tf_op jit(solution)/shard_map/ppermute | solution.py:282
  22.8 1.6 %keep.1.keep_ref = bf16[8,128,384]{2,1,0:T(8,128)(2,1)S(1)} custom-call(s32[1]{0:T(128)} %bitcast.core_ref, bf16[128,6144]{1,0:T(8,128)(2,1)} %bitcast.14, bf16[128,6144]{1,0:T(8,128)(2,1)} %bitcast.18), custom_call_target="tpu_custom_call" | custom-call | flops 99999997952 | bytes 2097152 | tf_op jit(solution)/shard_map/keep/pallas_call | solution.py:278
  24.4 0.2 collective-permute-done.took_ref
  24.7 1.6 %pair.1 = f32[8,384,128]{2,1,0:T(8,128)} custom-call(bf16[8,128,384]{2,1,0:T(8,128)(2,1)S(1)} %keep.1.keep_ref, bf16[8,128,384]{2,1,0:T(8,128)(2,1)S(1)} %collective-permute-done.took_ref), custom_call_target="tpu_custom_call" | custom-call | tf_op jit(solution)/shard_map/pair/pallas_call | solution.py:283
  26.3 0.0 reduce-scatter.2.cloned.1.call-update
  26.3 7.8 %all-to-all-done.factor_ref = bf16[8,64,384]{2,1,0:T(8,128)(2,1)S(1)} async-done(((bf16[8,64,384]{2,1,0:T(8,128)(2,1)}), bf16[8,64,384]{2,1,0:T(8,128)(2,1)S(1)}, u32[]{:S(2)}, u32[]{:S(2)}) %all-to-all-start) | async-done | bytes 393248 | tf_op jit(solution)/shard_map/all_to_all | solution.py:286
  34.1 0.6 left.1
  34.7 20.7 %all_to_all.35 = f32[64,1,128]{2,1,0:T(1,128)S(1)} all-to-all(f32[64,1,128]{2,1,0:T(1,128)S(1)} %bitcast.23), channel_id=1, replica_groups=mesh['x'=4,'y'=8,'core'=2,'z'=8] {'x','y','core'}, dimensions={0} | all-to-all | bytes 65536 | tf_op jit(solution)/shard_map/all_to_all | solution.py:290
  55.3 0.1 reduce_sum.18
  55.5 13.4 %all_to_all.36 = f32[64,1,128]{2,1,0:T(1,128)S(1)} all-to-all(f32[64,1,128]{2,1,0:T(1,128)S(1)} %broadcast_in_dim.6), channel_id=1, replica_groups=mesh['x'=4,'y'=8,'core'=2,'z'=8] {'x','y','core'}, dimensions={0} | all-to-all | bytes 65536 | tf_op jit(solution)/shard_map/all_to_all | solution.py:253
  68.9 0.0 copy-start.1
  68.9 0.2 gram.1
  69.1 0.0 copy-start
  69.1 10.4 %all_to_all.37.grams_ref = f32[8,32,128]{2,1,0:T(8,128)S(1)} all-to-all(f32[8,32,128]{2,1,0:T(8,128)S(1)} %gram.1), channel_id=1, replica_groups=mesh['x'=4,'y'=8,'core'=2,'z'=8] {'z'}, dimensions={0} | all-to-all | bytes 262144 | tf_op jit(solution)/shard_map/all_to_all | solution.py:296
  79.5 0.0 reduce-scatter.2.cloned.1.call-done
  79.5 3.4 %all-to-all-start.4 = ((f32[4,96,128]{2,1,0:T(8,128)}), f32[4,96,128]{2,1,0:T(8,128)S(1)}, u32[]{:S(2)}, u32[]{:S(2)}) async-start(f32[4,96,128]{2,1,0:T(8,128)} %bitcast.24), calls=%async_computation.5 | async-start | bytes 393216 | tf_op jit(solution)/shard_map/all_to_all | solution.py:304
  82.9 3.5 %factor.1 = (f32[64,128]{1,0:T(8,128)}, bf16[128,64]{1,0:T(8,128)(2,1)S(1)}) custom-call(f32[8,32,128]{2,1,0:T(8,128)S(1)} %all_to_all.37.grams_ref, f32[64,128]{1,0:T(8,128)S(1)} %bitcast.22), custom_call_target="tpu_custom_call" | custom-call | tf_op jit(solution)/shard_map/factor/pallas_call | solution.py:297
  86.4 0.0 copy-start.2
  86.4 1.7 %all-to-all-done.4.slab_ref = f32[4,96,128]{2,1,0:T(8,128)S(1)} async-done(((f32[4,96,128]{2,1,0:T(8,128)}), f32[4,96,128]{2,1,0:T(8,128)S(1)}, u32[]{:S(2)}, u32[]{:S(2)}) %all-to-all-start.4) | async-done | bytes 196640 | tf_op jit(solution)/shard_map/all_to_all | solution.py:304
  88.0 0.3 right.1
  88.3 11.1 %all_to_all.38 = f32[8,48,128]{2,1,0:T(8,128)S(1)} all-to-all(f32[8,48,128]{2,1,0:T(8,128)S(1)} %right.1), channel_id=1, replica_groups=mesh['x'=4,'y'=8,'core'=2,'z'=8] {'z'}, dimensions={0} | all-to-all | bytes 393216 | tf_op jit(solution)/shard_map/all_to_all | solution.py:308
  99.4 0.0 copy-done.2
  99.4 0.1 broadcast_in_dim.7
  99.5 13.4 %all_to_all.39.factor_ref = bf16[32,48,128]{2,1,0:T(8,128)(2,1)S(1)} all-to-all(bf16[32,48,128]{2,1,0:T(8,128)(2,1)S(1)} %broadcast_in_dim.7), channel_id=1, replica_groups=mesh['x'=4,'y'=8,'core'=2,'z'=8] {'x','y'}, dimensions={0} | all-to-all | bytes 786432 | tf_op jit(solution)/shard_map/all_to_all | solution.py:253
  112.8 7.5 %collective-permute-start.1 = (bf16[32,48,128]{2,1,0:T(8,128)(2,1)S(1)}, bf16[32,48,128]{2,1,0:T(8,128)(2,1)}, u32[]{:S(2)}, u32[]{:S(2)}) collective-permute-start(bf16[32,48,128]{2,1,0:T(8,128)(2,1)S(1)} %all_to_all.39.factor_ref), channel_id=1, source_target_pairs={{0,8},{8,0},{1,9},{9,1},{2,10},{10,2},{3,11},{11,3},{4,12},{12,4},... | collective-permute-start | bytes 1179656 | tf_op jit(solution)/shard_map/ppermute | solution.py:310
  120.4 0.0 copy-done.1
  120.4 0.0 copy-done
  120.4 1.3 own.1
  121.7 0.1 collective-permute-done.1.factor_ref
  121.8 2.4 %other.1 = (bf16[128,6144]{1,0:T(8,128)(2,1)}, bf16[64,768]{1,0:T(8,128)(2,1)}) custom-call(s32[1]{0:T(128)} %bitcast.core_ref, s32[1]{0:T(128)} %bitcast.1.z_ref, bf16[128,64]{1,0:T(8,128)(2,1)S(1)} %get-tuple-element.15.round_ref, bf16[32,48,128]{2,1,0:T(8,128)(2,1)} %collective-permute-done.1.factor_ref, bf16[128,6144]{1,0:T(8,128)(2,1)S(1)} %bitcast.16, ...), custom_call_target="tpu_custom_call" | custom-call | tf_op jit(solution)/shard_map/other/pallas_call | solution.py:318
  (3 shorter events, 0.0 us)
Async XLA Ops:
  9.0 25.1 %all-to-all-start = ((bf16[8,64,384]{2,1,0:T(8,128)(2,1)}), bf16[8,64,384]{2,1,0:T(8,128)(2,1)S(1)}, u32[]{:S(2)}, u32[]{:S(2)}) async-start(bf16[8,64,384]{2,1,0:T(8,128)(2,1)} %get-tuple-element.12), calls=%async_computation | async-start | bytes 786432 | tf_op jit(solution)/shard_map/all_to_all | solution.py:286
  19.9 59.6 %reduce-scatter.2.cloned.1.call-start = ((), (), s32[]{:S(2)}) async-start(), calls=%async_computation.8 | async-start | bytes 1769472 | tf_op jit(solution)/shard_map/reduce_scatter | solution.py:284
  19.9 4.8 %collective-permute-start = (bf16[8,128,384]{2,1,0:T(8,128)(2,1)S(1)}, bf16[8,128,384]{2,1,0:T(8,128)(2,1)S(1)}, u32[]{:S(2)}, u32[]{:S(2)}) collective-permute-start(bf16[8,128,384]{2,1,0:T(8,128)(2,1)S(1)} %get-tuple-element.13), channel_id=1, source_target_pairs={{0,8},{8,0},{1,9},{9,1},{2,10},{10,2},{3,11},{11,3},{4,12},{12,4},... | collective-permute-start | bytes 2359304 | tf_op jit(solution)/shard_map/ppermute | solution.py:282
  68.9 51.5 %copy-start.1 = (bf16[1,128,6144]{2,1,0:T(8,128)(2,1)S(1)}, bf16[1,128,6144]{2,1,0:T(8,128)(2,1)}, u32[]{:S(2)}) copy-start(bf16[1,128,6144]{2,1,0:T(8,128)(2,1)} %param.4) | copy-start | bytes 4718596
  69.1 51.3 %copy-start = (bf16[1,128,6144]{2,1,0:T(8,128)(2,1)S(1)}, bf16[1,128,6144]{2,1,0:T(8,128)(2,1)}, u32[]{:S(2)}) copy-start(bf16[1,128,6144]{2,1,0:T(8,128)(2,1)} %param.3) | copy-start | bytes 4718596
  79.5 8.5 %all-to-all-start.4 = ((f32[4,96,128]{2,1,0:T(8,128)}), f32[4,96,128]{2,1,0:T(8,128)S(1)}, u32[]{:S(2)}, u32[]{:S(2)}) async-start(f32[4,96,128]{2,1,0:T(8,128)} %bitcast.24), calls=%async_computation.5 | async-start | bytes 393216 | tf_op jit(solution)/shard_map/all_to_all | solution.py:304
  86.4 13.0 %copy-start.2 = (bf16[128,64]{1,0:T(8,128)(2,1)}, bf16[128,64]{1,0:T(8,128)(2,1)S(1)}, u32[]{:S(2)}) copy-start(bf16[128,64]{1,0:T(8,128)(2,1)S(1)} %get-tuple-element.14.round_ref) | copy-start | bytes 49156
  112.8 9.0 %collective-permute-start.1 = (bf16[32,48,128]{2,1,0:T(8,128)(2,1)S(1)}, bf16[32,48,128]{2,1,0:T(8,128)(2,1)}, u32[]{:S(2)}, u32[]{:S(2)}) collective-permute-start(bf16[32,48,128]{2,1,0:T(8,128)(2,1)S(1)} %all_to_all.39.factor_ref), channel_id=1, source_target_pairs={{0,8},{8,0},{1,9},{9,1},{2,10},{10,2},{3,11},{11,3},{4,12},{12,4},... | collective-permute-start | bytes 1179656 | tf_op jit(solution)/shard_map/ppermute | solution.py:310
Sparse Core Ops, SparseCore 0:
  26.5 40.3 reduce-scatter.1
